TPU v7x, 32 devices: a whole 2x2x4 slice. The times are simulated.
32 devices in a mesh: dp: 8 (over z, core), ctx: 4 (over y, x).
Axes of the slice: x: 2, y: 2, z: 4, core: 2. Of those that a mesh axis runs over, the one named last changes fastest.
Arguments:
- residual_in: bfloat16 [8, 512, 1536], P('dp', 'ctx'), may hold values from -64 to 64
- query_rows: bfloat16 [8, 512, 1536], P('dp', 'ctx'), may hold values from -6 to 6
- key_rows: bfloat16 [8, 512, 1536], P('dp', 'ctx'), may hold values from -6 to 6
- value_rows: bfloat16 [8, 512, 1536], P('dp', 'ctx'), may hold values from -6 to 6
- lengths: int32 [8], P('dp'), may hold values from 128 to 512, as said below
- out_weight: bfloat16 [1536, 1536], replicated, may hold values from -0.15625 to 0.15625
- norm_gain: float32 [1536], replicated, may hold values from 0.25 to 1.75
- conv_kernel: float32 [31, 1536], replicated, may hold values from -1 to 1
- conv_bias: float32 [1536], replicated, may hold values from -3 to 3
- conv_gain: float32 [1536], replicated, may hold values from 0.25 to 1.75
- point_weight: bfloat16 [1536, 1536], replicated, may hold values from -0.15625 to 0.15625
- grad_out: bfloat16 [8, 512, 1536], P('dp', 'ctx'), may hold values from -6 to 6
Outputs:
- block_out: bfloat16 [8, 512, 1536], P('dp', 'ctx')
- grad_residual: bfloat16 [8, 512, 1536], P('dp', 'ctx')
- grad_query: bfloat16 [8, 512, 1536], P('dp', 'ctx')
- grad_key: bfloat16 [8, 512, 1536], P('dp', 'ctx')
- grad_value: bfloat16 [8, 512, 1536], P('dp', 'ctx')
- grad_out_weight: float32 [1536, 1536], P(None, ('dp', 'ctx'))
- grad_point_weight: float32 [1536, 1536], P(None, ('dp', 'ctx'))
- grad_kernel: float32 [31, 1536], P(None, ('dp', 'ctx'))
- grad_vectors: float32 [3, 1536], P(None, ('dp', 'ctx'))
Inputs may be any that keep to these rules, and one draw needn't show every extreme that they name: `lengths`: in every draw some utterance has all 512 frames.
All inputs are finite; a program needn't handle non-finite values.
Results may differ from a plain program's by a relative error of at most 0.028.
Values may be sent and summed in bfloat16 or wider, within the bound.
No kernel may reach another device: no remote copies, remote signals or barrier semaphores. Data moves between devices by JAX's collectives and lax.ppermute only.
A program may use at most 192 MiB of HBM per device.

v0:
```python
import functools

import jax
import jax.numpy as jnp
from jax import lax
from jax.experimental import pallas as pl
from jax.experimental.pallas import tpu as pltpu
from jax.sharding import PartitionSpec as P

HEADS = 24
HEAD_DIM = 64
SCALE = HEAD_DIM ** (-0.5)

NEG_FILL = -1e30
EPSILON = 1e-05

LANES = 128
EDGE = 16
NEAR = 3
BAND = 16
EXTRA = 48

NN = (((1,), (0,)), ((), ()))
NT = (((1,), (1,)), ((), ()))
TN = (((0,), (0,)), ((), ()))


def dot(left, right, dims=NN):
    return lax.dot_general(left, right, dims, preferred_element_type=jnp.float32)


def call(
    kernel, name, outs, scratch=(), semaphores=0, far=(), megabytes=28, flops=0, moved=0, exps=0
):
    vmem = pl.BlockSpec(memory_space=pltpu.VMEM)
    smem = pl.BlockSpec(memory_space=pltpu.SMEM)
    anywhere = pl.BlockSpec(memory_space=pl.ANY)

    def run(*arrays):
        scratches = [pltpu.VMEM(shape, kind) for shape, kind in scratch]
        if semaphores:
            scratches.append(pltpu.SemaphoreType.DMA((semaphores,)))
        return pl.pallas_call(
            kernel,
            name=name,
            in_specs=[smem if a.ndim == 1 else anywhere if "in" in far else vmem for a in arrays],
            out_specs=[anywhere if "out" in far else vmem] * len(outs),
            out_shape=[jax.ShapeDtypeStruct(shape, kind) for shape, kind in outs],
            scratch_shapes=scratches,
            compiler_params=pltpu.CompilerParams(vmem_limit_bytes=megabytes << 20),
            cost_estimate=pl.CostEstimate(flops=flops, bytes_accessed=moved, transcendentals=exps),
        )(*arrays)

    return run


def valid_of(first, rows, length):
    return first + lax.broadcasted_iota(jnp.int32, (rows, 1), 0) < length


def moments(rows):
    centre = jnp.mean(rows, axis=-1, keepdims=True)
    centred = rows - centre
    inv_scale = lax.rsqrt(jnp.mean(centred * centred, axis=-1, keepdims=True) + EPSILON)
    return centred * inv_scale, inv_scale


def norm_back(grad_normed, normed, inv_scale):
    first_mean = jnp.mean(grad_normed, axis=-1, keepdims=True)
    second_mean = jnp.mean(grad_normed * normed, axis=-1, keepdims=True)
    return inv_scale * (grad_normed - first_mean - normed * second_mean)


def fold(rows):
    total = rows[:8]
    for at in range(8, rows.shape[0], 8):
        total = total + rows[at : at + 8]
    return total


def at_group(info, by, ways, share, visit):
    if share % LANES == 0:
        visit(pl.ds(pl.multiple_of((info[0] ^ by) * share, LANES), share))
        return
    for at in range(ways):

        @pl.when((info[0] ^ by) == at)
        def _():
            visit(slice(at * share, (at + 1) * share))


def neighbours(ways):
    return [by for by in (1, 3, 7, 15) if by < ways]


def edge_rows(frames, at):
    return slice(3 * frames + at * 3 * EDGE, 3 * frames + (at + 1) * 3 * EDGE)


def pack_kernel(ways, query, key, value, residual, grad_out, *refs):
    blocks, whole, ends, arrived = refs[:ways], refs[ways], refs[ways + 1], refs[ways + 2]
    info = [lax.axis_index("ctx")]
    frames, width = query.shape
    share, reach = width // ways, 2 * EDGE
    pairs = [(rows, whole.at[slot]) for slot, rows in enumerate((query, key, value))]
    for side, tail in enumerate((False, True)):
        for rows, start, count in ((residual, 0, reach), (grad_out, reach, EDGE)):
            first = frames - count if tail else 0
            pairs.append((rows.at[pl.ds(first, count)], ends.at[side, pl.ds(start, count)]))
    copies = [
        pltpu.make_async_copy(source, target, arrived.at[at])
        for at, (source, target) in enumerate(pairs)
    ]
    for copy in copies:
        copy.start()
    for slot, copy in enumerate(copies[:3]):
        copy.wait()
        for by in range(ways):

            def visit(lanes):
                blocks[by][slot * frames : (slot + 1) * frames, :] = whole[slot, :, lanes]

            at_group(info, by, ways, share, visit)
    for copy in copies[3:]:
        copy.wait()
    for by in neighbours(ways):
        side = jnp.where((info[0] ^ by) > info[0], 1, 0)
        for at in range(ways):
            blocks[by][edge_rows(frames, at), :] = ends[side, :, at * share : (at + 1) * share]


def unpack_kernel(ways, info, *refs):
    blocks, outs, arrived = refs[:ways], refs[ways:-1], refs[-1]
    share = blocks[0].shape[2]
    copies = []
    for by in range(ways):
        for slot, rows in enumerate(outs):
            lanes = pl.ds(pl.multiple_of((info[0] ^ by) * share, LANES), share)
            copy = pltpu.make_async_copy(
                blocks[by].at[slot], rows.at[:, lanes], arrived.at[len(copies)]
            )
            copy.start()
            copies.append(copy)
    for copy in copies:
        copy.wait()


def unpack_parts_kernel(ways, info, *refs):
    blocks, outs = refs[:ways], refs[ways:]
    share = blocks[0].shape[2]
    for by in range(ways):
        for slot, rows in enumerate(outs):

            def visit(lanes):
                rows[:, lanes] = blocks[by][slot]

            at_group(info, by, ways, share, visit)


def mask_kernel(lower, info, grad_out, masked, *halves):
    frames, width = grad_out.shape
    valid = valid_of(info[0] * frames, frames, info[1])
    masked[...] = jnp.where(valid, grad_out[...].astype(jnp.float32), 0.0).astype(jnp.bfloat16)
    quarter = width // 4
    for by, half in enumerate(halves):
        for at in range(2):
            start = (2 * at + ((info[2] // lower) ^ by) % 2) * quarter
            lanes = pl.ds(pl.multiple_of(start, LANES), quarter)
            half[:, at * quarter : (at + 1) * quarter] = masked[:, lanes]


def grad_act_kernel(info, masked, point_weight, block, grad_act, own_block):
    own_block[...] = block[...]
    width = masked.shape[1]
    step = width // 3
    for at in range(0, width, step):
        grad_act[:, at : at + step] = dot(masked[...], point_weight[at : at + step, :], NT)


def mask_edges_kernel(frames, info, before, after, point_weight, grad_act):
    width = grad_act.shape[1]
    first = info[0] * frames
    sides = []
    for side, start in ((before, first - EDGE), (after, first + frames)):
        valid = valid_of(start, EDGE, info[1])
        rows = side[2 * EDGE :, :].astype(jnp.float32)
        sides.append(jnp.where(valid, rows, 0.0).astype(jnp.bfloat16))
    masked = jnp.concatenate(sides, axis=0)
    step = width // 3
    for at in range(0, width, step):
        grad_act[:, at : at + step] = dot(masked, point_weight[at : at + step, :], NT)


def gather_heads(info, blocks, query, key, value, bias):
    frames = query.shape[0] // len(blocks)
    for by, block in enumerate(blocks):
        rows = slice(by * frames, (by + 1) * frames)
        query[rows] = block[:frames, :] * jnp.bfloat16(SCALE)
        key[rows] = block[frames : 2 * frames, :]
        value[rows] = block[2 * frames : 3 * frames, :]
        valid = valid_of((info[0] ^ by) * frames, frames, info[1])
        bias[rows] = jnp.broadcast_to(jnp.where(valid, 0.0, NEG_FILL), (frames, LANES))


def attend_kernel(ways, info, *refs):
    blocks, outs = refs[:ways], refs[ways : 2 * ways]
    attended, log_total, before, after, query, key, value, bias, turned = refs[2 * ways :]
    gather_heads(info, blocks, query, key, value, bias)
    total_frames, share = query.shape
    frames = total_frames // ways
    for side, other in ((before, info[0] - 1), (after, info[0] + 1)):
        side[...] = jnp.zeros_like(side)
        for by in neighbours(ways):

            @pl.when((info[0] ^ other) == by)
            def _():
                for at in range(ways):
                    lanes = slice(at * share, (at + 1) * share)
                    side[:, lanes] = blocks[by][edge_rows(frames, at), :]

    for head in range(share // HEAD_DIM):
        part = slice(head * HEAD_DIM, (head + 1) * HEAD_DIM)
        spread = jnp.concatenate([bias[...]] * (total_frames // LANES), axis=1)
        scores = dot(key[:, part], query[:, part], NT) + spread
        row_max = jnp.max(scores, axis=0, keepdims=True)
        weights = jnp.exp(scores - row_max)
        total = jnp.sum(weights, axis=0, keepdims=True)
        turned[part, :] = dot(value[:, part], weights.astype(jnp.bfloat16), TN) / total
        log_total[head : head + 1, :] = row_max + jnp.log(total)
    attended[...] = turned[...].T.astype(jnp.bfloat16)
    reach = 2 * EDGE
    for by in range(ways):
        other = info[0] ^ by
        before = (info[0] ^ jnp.maximum(other - 1, 0)) * frames + frames - reach
        after = (info[0] ^ jnp.minimum(other + 1, ways - 1)) * frames
        outs[by][:reach] = attended[pl.ds(pl.multiple_of(before, reach), reach), :]
        outs[by][reach : reach + frames] = attended[by * frames : (by + 1) * frames, :]
        outs[by][reach + frames :] = attended[pl.ds(pl.multiple_of(after, reach), reach), :]


def attend_back_kernel(ways, info, *refs):
    blocks, messages = refs[:ways], refs[ways : 2 * ways]
    attended, log_total = refs[2 * ways : 2 * ways + 2]
    outs = refs[2 * ways + 2 : 3 * ways + 2]
    query, key, value, bias, grad, turned = refs[3 * ways + 2 :]
    gather_heads(info, blocks, query, key, value, bias)
    total_frames, share = query.shape
    frames = total_frames // ways
    for by in range(ways):
        grad[by * frames : (by + 1) * frames] = messages[by][:frames, :]
    turned[...] = (grad[...].astype(jnp.float32) * attended[...].astype(jnp.float32)).T
    for head in range(share // HEAD_DIM):
        part = slice(head * HEAD_DIM, (head + 1) * HEAD_DIM)
        delta = jnp.sum(turned[part, :], axis=0, keepdims=True)
        spread = jnp.concatenate([bias[...]] * (total_frames // LANES), axis=1)
        scores = dot(key[:, part], query[:, part], NT) + spread
        probs = jnp.exp(scores - log_total[head : head + 1, :])
        value_grad = dot(probs.astype(jnp.bfloat16), grad[:, part])
        prob_grad = dot(value[:, part], grad[:, part], NT)
        score_grad = (probs * (prob_grad - delta)).astype(jnp.bfloat16)
        key_grad = dot(score_grad, query[:, part])
        turned[part, :] = dot(key[:, part], score_grad, TN) * SCALE
        for by in range(ways):
            rows = slice(by * frames, (by + 1) * frames)
            outs[by][1, :, part] = key_grad[rows].astype(jnp.bfloat16)
            outs[by][2, :, part] = value_grad[rows].astype(jnp.bfloat16)
    query_grad = turned[...].T.astype(jnp.bfloat16)
    for by in range(ways):
        outs[by][0] = query_grad[by * frames : (by + 1) * frames]


def gather_kernel(ways, info, *refs):
    blocks, messages = refs[:ways], refs[ways:]
    frames, share, reach = messages[0].shape[0], blocks[0].shape[1], 2 * EDGE
    for by, message in enumerate(messages):
        lacking = [slot for slot in range(ways) if slot != by]
        for at, slot in enumerate(lacking):
            message[:, at * share : (at + 1) * share] = blocks[slot][reach : reach + frames, :]


def project_kernel(ways, info, *refs):
    blocks = refs[:ways]
    residual, before, after, out_weight, params = refs[ways : ways + 5]
    mixed, conv_in, attended = refs[ways + 5 :]
    frames, width = residual.shape
    share = width // ways
    reach = 2 * EDGE
    rows = frames + 2 * reach
    for by in range(ways):
        for at in range(ways):

            @pl.when((info[0] ^ by) == at)
            def _():
                attended[:, at * share : (at + 1) * share] = blocks[by][...]

    step = width // 3
    for at in range(0, width, step):
        part = slice(at, at + step)
        mixed[:reach, part] = before[:reach, part].astype(jnp.float32)
        mixed[reach : reach + frames, part] = residual[:, part].astype(jnp.float32)
        mixed[reach + frames :, part] = after[:reach, part].astype(jnp.float32)
        mixed[:, part] += dot(attended[...], out_weight[:, part])

    gain = params[31:32, :]
    first = info[0] * frames - reach

    def band(index, carry):
        at = pl.ds(pl.multiple_of(index * BAND, BAND), BAND)
        normed, _ = moments(mixed[at, :])
        position = first + index * BAND + lax.broadcasted_iota(jnp.int32, (BAND, 1), 0)
        valid = (position >= 0) & (position < info[1])
        conv_in[at, :] = jnp.where(valid, normed * gain, 0.0).astype(jnp.bfloat16)
        return carry

    lax.fori_loop(0, rows // BAND, band, 0)


def stride_of(rows):
    return rows // 8 + 1


def in_columns(ref, rows):
    for at in range(ref.shape[0]):
        ref[at, : rows.shape[0]] = rows[:, at * LANES : (at + 1) * LANES].astype(jnp.float32)


def from_columns(ref, rows):
    return jnp.concatenate([ref[at, rows, :] for at in range(ref.shape[0])], axis=1)


def strided(ref, index, start, stride):
    return ref[index, pl.ds(start, 8, stride=stride), :]


def depthwise(padded, taps, tap_of, out, rows):
    stride = stride_of(rows)

    def column(index, carry):
        part = pl.ds(pl.multiple_of(index * LANES, LANES), LANES)
        cells = [strided(padded, index, at + 1, stride) for at in range(stride + 2 * EDGE - 2)]
        total = [None] * stride
        for offset in range(1, 2 * EDGE):
            tap = tap_of(offset)
            scale = jnp.broadcast_to(taps[tap : tap + 1, part], (8, LANES))
            for at in range(stride):
                term = cells[at + offset - 1] * scale
                total[at] = term if total[at] is None else total[at] + term
        for at in range(stride):
            out[index, pl.ds(at, 8, stride=stride), :] = total[at]
        return carry

    lax.fori_loop(0, out.shape[0], column, 0)


def tap_grads(padded, grad, start, rows, taps):
    stride = rows // 8

    def column(index, carry):
        part = pl.ds(pl.multiple_of(index * LANES, LANES), LANES)
        cells = [
            strided(padded, index, start + at + 1, stride) for at in range(stride + 2 * EDGE - 2)
        ]
        grads = [strided(grad, index, start + at, stride) for at in range(stride)]
        for tap in range(2 * EDGE - 1):
            total = cells[tap] * grads[0]
            for at in range(1, stride):
                total = total + cells[at + tap] * grads[at]
            taps[tap : tap + 1, part] = jnp.sum(total, axis=0, keepdims=True)
        return carry

    lax.fori_loop(0, grad.shape[0], column, 0)


def conv_kernel_body(lower, info, conv_in, params, grad_own, grad_edges, *refs):
    conv_act, grad_conv, sums = refs[:3]
    halves = refs[3:-5]
    padded, conv, grad_act, bias_sum, gain_sum = refs[-5:]
    frames, width = grad_own.shape
    rows, wide = frames + 2 * EDGE, frames + 4 * EDGE
    in_columns(padded, conv_in[...])
    padded[:, wide:, :] = jnp.zeros((width // LANES, padded.shape[1] - wide, LANES), jnp.float32)
    grad_act[:EDGE] = grad_edges[:EDGE]
    grad_act[EDGE : EDGE + frames] = grad_own[...]
    grad_act[EDGE + frames :] = grad_edges[EDGE:]
    depthwise(padded, params, lambda offset: offset - 1, conv, rows)
    bias, gain = params[32:33, :], params[33:34, :]
    bias_sum[...] = jnp.zeros_like(bias_sum)
    gain_sum[...] = jnp.zeros_like(gain_sum)

    def band(index, carry):
        at = pl.ds(pl.multiple_of(index * BAND, BAND), BAND)
        normed, inv_scale = moments(from_columns(conv, at) + bias)
        scaled = normed * gain
        gate = 0.5 + 0.5 * jnp.tanh(0.5 * scaled)
        conv_act[at, :] = (scaled * gate).astype(jnp.bfloat16)
        grad_scaled = grad_act[at, :] * gate * (1.0 + scaled * (1.0 - gate))
        grad_rows = norm_back(grad_scaled * gain, normed, inv_scale)
        for column in range(width // LANES):
            grad_conv[column, at, :] = grad_rows[:, column * LANES : (column + 1) * LANES]

        @pl.when((index >= EDGE // BAND) & (index < (EDGE + frames) // BAND))
        def _():
            bias_sum[...] += fold(grad_rows)
            gain_sum[...] += fold(grad_scaled * normed)

        return carry

    lax.fori_loop(0, rows // BAND, band, 0)
    sums[0:1, :] = jnp.sum(bias_sum[...], axis=0, keepdims=True)
    sums[1:2, :] = jnp.sum(gain_sum[...], axis=0, keepdims=True)
    half = width // 2
    for by, block in enumerate(halves):
        start = ((info[2] // (2 * lower)) ^ by) * half
        block[...] = conv_act[EDGE : EDGE + frames, pl.ds(pl.multiple_of(start, LANES), half)]


def block_out_kernel(info, conv_act, mixed, point_weight, block_out):
    frames, width = block_out.shape
    step = width // 3
    for at in range(0, width, step):
        part = slice(at, at + step)
        block_out[:, part] = (
            mixed[2 * EDGE : 2 * EDGE + frames, part]
            + dot(conv_act[EDGE : EDGE + frames, :], point_weight[:, part])
        ).astype(jnp.bfloat16)


def conv_back_kernel(ways, slim, info, grad_conv, conv_in, params, masked, mixed, out_weight, *refs):
    conv_sums, grad_residual, messages = refs[0], refs[1], refs[2 : 2 + ways]
    padded, padded_in, conv, gain_sum, taps, packed, chosen = refs[2 + ways :]
    frames, width = grad_residual.shape
    share = width // ways
    reached = frames + 2 * EDGE
    padded[:, :reached, :] = grad_conv[...].astype(jnp.bfloat16).astype(jnp.float32)
    padded[:, reached:, :] = jnp.zeros(
        (width // LANES, padded.shape[1] - reached, LANES), jnp.float32
    )
    depthwise(padded, params, lambda offset: 31 - offset, conv, frames)
    gain = params[31:32, :]
    gain_sum[...] = jnp.zeros_like(gain_sum)

    def band(index, carry):
        at = pl.ds(pl.multiple_of(index * BAND, BAND), BAND)
        own_mixed = pl.ds(pl.multiple_of(index * BAND + 2 * EDGE, BAND), BAND)
        valid = valid_of(info[0] * frames + index * BAND, BAND, info[1])
        grad_in = jnp.where(valid, from_columns(conv, at), 0.0)
        normed, inv_scale = moments(mixed[own_mixed, :])
        grad_mixed = norm_back(grad_in * gain, normed, inv_scale)
        gain_sum[...] += fold(grad_in * normed)
        grad_residual[at, :] = (masked[at, :].astype(jnp.float32) + grad_mixed).astype(
            jnp.bfloat16
        )
        return carry

    lax.fori_loop(0, frames // BAND, band, 0)
    for by in range(ways):
        at = pl.ds(pl.multiple_of((info[0] ^ by) * share, share), share)
        messages[by][:frames] = dot(grad_residual[...], out_weight[at, :], NT).astype(jnp.bfloat16)

    in_columns(padded_in, conv_in[...])
    tap_grads(padded_in, grad_conv, EDGE, frames, taps)
    taps[31:32, :] = conv_sums[0:1, :]
    taps[32:33, :] = jnp.sum(gain_sum[...], axis=0, keepdims=True)
    taps[33:34, :] = conv_sums[1:2, :]
    taps[34:, :] = jnp.zeros((EXTRA - 34, width), jnp.float32)
    packed[:frames] = grad_residual[...]
    packed[frames:] = taps[...].astype(jnp.bfloat16)
    for at in range(ways):
        pieces = []
        for start in range(at * slim, width, ways * slim):
            pieces.append(packed[:, start : start + slim])
        chosen[at] = jnp.concatenate(pieces, axis=1)
    for by in range(ways):
        messages[by][frames:] = chosen[info[0] ^ by]


def split_rows(info, parts, terms, sent, kept):
    rows = terms.shape[0] // parts
    for bit in range(2):

        @pl.when(info[2] % 2 == bit)
        def _():
            for at in range(parts // 2):
                own, other = (2 * at + bit) * rows, (2 * at + 1 - bit) * rows
                kept[at] = terms[own : own + rows, :]
                sent[at] = terms[other : other + rows, :].astype(jnp.bfloat16)


def point_kernel(shift, info, *refs):
    grads, acts, (sent, kept, terms) = refs[:4], refs[4:8], refs[8:]
    left = jnp.concatenate([grad[...] for grad in grads], axis=0)
    right = jnp.concatenate([act[...] for act in acts], axis=0)
    step = terms.shape[1] // 2
    for at in range(0, 2 * step, step):
        part = slice(at, at + step)
        terms[:, part] = dot(left, right[:, part], TN)
    pieces, slim = kept.shape[0], kept.shape[1] // 2
    for bit in range(2):

        @pl.when(((info[2] >> shift) & 1) == bit)
        def _():
            for at in range(pieces):
                for side in range(2):
                    base = side * 2 * pieces * slim
                    own = base + (bit * pieces + at) * slim
                    other = base + ((1 - bit) * pieces + at) * slim
                    rows = slice(side * slim, (side + 1) * slim)
                    kept[at, rows, :] = terms[own : own + slim, :]
                    sent[at, rows, :] = terms[other : other + slim, :].astype(jnp.bfloat16)


def spread_kernel(info, kept, received, own, *blocks):
    own[...] = kept[info[0]] + received[info[0]].astype(jnp.float32)
    for by, block in enumerate(blocks, 1):
        at = info[0] ^ by
        block[...] = (kept[at] + received[at].astype(jnp.float32)).astype(jnp.bfloat16)


def point_sum_kernel(shift, info, *refs):
    blocks, (own, other) = refs[:-2], refs[-2:]
    rows = own.shape[0]
    total = blocks[0][...]
    for block in blocks[1:]:
        total = total + block[...].astype(jnp.float32)
    for at in range(2):

        @pl.when(((info[2] >> shift) & 1) == at)
        def _():
            own[...] = total[at * rows : (at + 1) * rows, :]
            other[...] = total[(1 - at) * rows : (2 - at) * rows, :].astype(jnp.bfloat16)


def weight_kernel(ways, parts, info, *refs):
    grads, rows = refs[:ways], refs[ways : 2 * ways]
    attended, sent, kept, terms = refs[2 * ways :]
    total_frames, share = attended.shape
    frames = total_frames // ways
    width = ways * share
    slim = share // parts
    left = jnp.concatenate([grad[frames : 2 * frames, :] for grad in grads], axis=0)
    for slot in range(ways):
        if slot == 0:
            right = attended[...]
        else:
            pieces = []
            for by in range(ways):
                at = (by ^ slot) - (1 if (by ^ slot) > by else 0)
                pieces.append(rows[by][:, at * share : (at + 1) * share])
            right = jnp.concatenate(pieces, axis=0)
        terms[:, slot * share : (slot + 1) * share] = dot(left, right, TN)
    small = jnp.zeros((EXTRA, share), jnp.float32)
    for grad in grads:
        small = small + grad[2 * frames :, :].astype(jnp.float32)
    filler = jnp.zeros((LANES - EXTRA, share), jnp.float32)
    terms[:, width:] = jnp.concatenate([small, filler], axis=0).T
    split_rows(info, parts, terms, sent, kept)


def halve_kernel(axis, shift, alternate, info, kept, received, sent, still_kept):
    bit = (info[axis] >> shift) & 1
    count = sent.shape[0]
    for at in range(count):
        if alternate:
            own, other = 2 * at + bit, 2 * at + 1 - bit
        else:
            own, other = bit * count + at, (1 - bit) * count + at
        still_kept[at] = kept[own] + received[own].astype(jnp.float32)
        sent[at] = (kept[other] + received[other].astype(jnp.float32)).astype(jnp.bfloat16)


def finish_kernel(ways, shift, info, kept, received, own, other, weight, taps, vectors, point):
    width = weight.shape[1]
    share, half = width // ways, width // 2
    for at in range(2):

        @pl.when(((info[2] >> shift) & 1) == at)
        def _():
            point[:, at * half : (at + 1) * half] = own[...]
            point[:, (1 - at) * half : (2 - at) * half] = other[...].astype(jnp.float32)

    total = kept[0] + received[0].astype(jnp.float32)
    for by in range(ways):
        for at in range(ways):

            @pl.when((info[0] ^ by) == at)
            def _():
                weight[:, at * share : (at + 1) * share] = total[:, by * share : (by + 1) * share]

    small = total[:, width:].T
    taps[...] = small[:31]
    vectors[...] = small[31:34]


def swap(block, axis, by):
    return lax.ppermute(block, axis, [(i, i ^ by) for i in range(lax.axis_size(axis))])


def swap_all(blocks, axis, step=1):
    return [blocks[0]] + [swap(block, axis, step * by) for by, block in enumerate(blocks[1:], 1)]


def local(
    residual_in,
    query_rows,
    key_rows,
    value_rows,
    lengths,
    out_weight,
    norm_gain,
    conv_kernel,
    conv_bias,
    conv_gain,
    point_weight,
    grad_out,
):
    ways = lax.axis_size("ctx")
    parts = lax.axis_size("dp")
    own = lax.axis_index("ctx")
    place = lax.axis_index("dp")
    frames, width = residual_in.shape[1:]
    share = width // ways
    slim = share // parts
    heads = HEADS // ways
    every = ways * frames
    lower = parts // 4
    half = width // 2
    tiles = width // LANES
    bf16, f32 = jnp.bfloat16, jnp.float32
    square = 2 * frames * width * width
    rows_bytes = 2 * frames * width
    reached, wide = frames + 2 * EDGE, frames + 4 * EDGE

    info = jnp.stack([own, lengths[0], place]).astype(jnp.int32)
    params = jnp.concatenate(
        [conv_kernel, norm_gain[None], conv_bias[None], conv_gain[None]], axis=0
    )

    by_tiles = share % LANES == 0
    packed_rows = [3 * frames + 3 * EDGE * ways * (by in neighbours(ways)) for by in range(ways)]
    packed = call(
        functools.partial(pack_kernel, ways),
        "pack",
        [((rows, share), bf16) for rows in packed_rows],
        scratch=[((3, frames, width), bf16), ((2, 3 * EDGE, width), bf16)],
        semaphores=7,
        far=("in",),
        megabytes=58,
        moved=6 * rows_bytes,
    )(query_rows[0], key_rows[0], value_rows[0], residual_in[0], grad_out[0])
    packed = swap_all(packed, "ctx")

    masked, *masked_halves = call(
        functools.partial(mask_kernel, lower),
        "mask",
        [((frames, width), bf16)] + [((frames, half), bf16)] * 2,
        moved=4 * rows_bytes,
    )(info, grad_out[0])
    masked_halves = swap_all([masked_halves[by % 2] for by in range(4)], "dp", lower)
    grad_own, packed[0] = call(
        grad_act_kernel,
        "grad_act",
        [((frames, width), f32), ((3 * frames, share), bf16)],
        flops=square,
        moved=6 * rows_bytes + 2 * width * width,
    )(info, masked, point_weight, packed[0])

    packed, grad_own = lax.optimization_barrier((packed, grad_own))
    head_scratch = [((every, share), bf16)] * 3 + [((every, LANES), f32)]
    pair_flops = 2 * heads * every * every * HEAD_DIM
    *returned, attended, log_total, before, after = call(
        functools.partial(attend_kernel, ways),
        "attend",
        [((wide, share), bf16)] * ways + [((every, share), bf16), ((heads, every), f32)]
        + [((3 * EDGE, width), bf16)] * 2,
        scratch=head_scratch + [((share, every), f32)],
        flops=8 * pair_flops,
        moved=4 * rows_bytes,
        exps=heads * every * every,
    )(info, *packed)
    returned, masked_halves[1:3] = lax.optimization_barrier((returned, masked_halves[1:3]))
    returned = swap_all(returned, "ctx")
    grad_edges = call(
        functools.partial(mask_edges_kernel, frames),
        "mask_edges",
        [((2 * EDGE, width), f32)],
        flops=square,
        moved=2 * width * width,
    )(info, before, after, point_weight)[0]
    returned, grad_edges, masked_halves = lax.optimization_barrier(
        (returned, grad_edges, masked_halves)
    )
    messages = call(
        functools.partial(gather_kernel, ways),
        "gather",
        [((frames, width - share), bf16)] * ways,
        moved=8 * rows_bytes,
    )(info, *returned)
    arrived = swap_all(messages, "ctx")

    returned, messages = lax.optimization_barrier((returned, messages))
    mixed, conv_in = call(
        functools.partial(project_kernel, ways),
        "project",
        [((wide, width), f32), ((wide, width), bf16)],
        scratch=[((wide, width), bf16)],
        flops=square,
        moved=6 * rows_bytes + 2 * width * width,
    )(info, *returned, residual_in[0], before, after, out_weight, params)
    spread = 8 * stride_of(reached)
    conv_act, grad_conv, conv_sums, *act_halves = call(
        functools.partial(conv_kernel_body, lower),
        "conv",
        [
            ((reached, width), bf16),
            ((tiles, reached, LANES), f32),
            ((2, width), f32),
        ]
        + [((frames, half), bf16)] * 2,
        scratch=[
            ((tiles, spread + 2 * EDGE, LANES), f32),
            ((tiles, spread, LANES), f32),
            ((reached, width), f32),
            ((8, width), f32),
            ((8, width), f32),
        ],
        flops=frames * width * 4000,
        moved=6 * rows_bytes,
        exps=frames * width,
    )(info, conv_in, params, grad_own, grad_edges)
    near, act_halves = lax.optimization_barrier((arrived[:NEAR], act_halves))
    act_halves = swap_all([act_halves[by // 2] for by in range(4)], "dp", lower)
    far, grad_conv = lax.optimization_barrier((arrived[NEAR:], grad_conv))

    spread = 8 * stride_of(frames)
    grad_residual, *grad_messages = call(
        functools.partial(conv_back_kernel, ways, slim),
        "conv_back",
        [((frames, width), bf16)] + [((2 * frames + EXTRA, share), bf16)] * ways,
        scratch=[
            ((tiles, spread + 2 * EDGE, LANES), f32),
            ((tiles, wide, LANES), f32),
            ((tiles, spread, LANES), f32),
            ((8, width), f32),
            ((EXTRA, width), f32),
            ((frames + EXTRA, width), bf16),
            ((ways, frames + EXTRA, share), bf16),
        ],
        flops=frames * width * 8000,
        moved=8 * rows_bytes + 2 * width * width,
    )(
        info,
        grad_conv,
        conv_in,
        params,
        masked,
        mixed,
        out_weight,
        conv_sums,
    )
    act_halves[1], grad_messages[NEAR:] = lax.optimization_barrier(
        (act_halves[1], grad_messages[NEAR:])
    )
    act_halves, conv_act = lax.optimization_barrier((act_halves, conv_act))
    messages = near + far
    grad_messages = swap_all(grad_messages, "ctx")

    block_out = call(
        block_out_kernel,
        "block_out",
        [((frames, width), bf16)],
        flops=square,
        moved=4 * rows_bytes + 2 * width * width,
    )(info, conv_act, mixed, point_weight)[0]

    def halve(kept, received, axis, shift, alternate):
        extent = (kept.shape[0] // 2,) + kept.shape[1:]
        return call(
            functools.partial(halve_kernel, 0 if axis == "ctx" else 2, shift, alternate),
            "halve",
            [(extent, bf16), (extent, f32)],
            moved=16 * extent[0] * extent[1] * extent[2],
        )(info, kept, received)

    grad_messages[1], act_halves = lax.optimization_barrier((grad_messages[1], act_halves))
    bits = list(reversed(range(lower.bit_length() - 1)))
    point_half = (lower * ways // 2, 2 * slim, half)
    point_sent, point_kept = call(
        functools.partial(point_kernel, bits[0]),
        "point_terms",
        [(point_half, bf16), (point_half, f32)],
        scratch=[((half, half), f32)],
        flops=square,
        moved=8 * rows_bytes,
    )(info, *masked_halves, *act_halves)
    grad_messages, point_sent, block_out = lax.optimization_barrier(
        (grad_messages, point_sent, block_out)
    )
    extent = width + LANES
    core_half = (parts // 2, slim, extent)
    sent, kept = call(
        functools.partial(weight_kernel, ways, parts),
        "out_terms",
        [(core_half, bf16), (core_half, f32)],
        scratch=[((share, extent), f32)],
        flops=square,
        moved=10 * rows_bytes,
    )(info, *grad_messages, *messages, attended)
    received = swap(sent, "dp", 1)
    for shift in range(1, parts.bit_length() - 1):
        sent, kept = halve(kept, received, "dp", shift, True)
        received = swap(sent, "dp", 2**shift)

    point_received = swap(point_sent, "dp", 2 ** bits[0])
    for shift in bits[1:]:
        point_sent, point_kept = halve(point_kept, point_received, "dp", shift, False)
        point_received = swap(point_sent, "dp", 2**shift)
    pieces = call(
        spread_kernel,
        "spread",
        [((2 * slim, half), f32)] + [((2 * slim, half), bf16)] * (ways - 1),
        moved=slim * width * 6 * ways,
    )(info, point_kept, point_received)
    pieces = swap_all(pieces, "ctx")
    grad_packed = call(
        functools.partial(attend_back_kernel, ways),
        "attend_back",
        [((3, frames, share), bf16)] * ways,
        scratch=head_scratch + [((every, share), bf16), ((share, every), f32)],
        flops=20 * pair_flops,
        moved=8 * rows_bytes,
        exps=heads * every * every,
    )(info, *packed, *grad_messages, attended, log_total)
    pieces, grad_packed = lax.optimization_barrier((pieces, grad_packed))
    grad_packed = swap_all(grad_packed, "ctx")
    layer_bit = (parts // 2).bit_length() - 1
    point_own, point_other = call(
        functools.partial(point_sum_kernel, layer_bit),
        "point_sum",
        [((slim, half), f32), ((slim, half), bf16)],
        moved=slim * width * (parts + 8),
    )(info, *pieces)
    point_other = swap(point_other, "dp", parts // 2)

    out_total, taps, vectors, point_total = call(
        functools.partial(finish_kernel, ways, layer_bit),
        "finish",
        [((slim, width), f32), ((31, slim), f32), ((3, slim), f32), ((slim, width), f32)],
        moved=slim * extent * (parts + 8),
    )(info, kept, received, point_own, point_other)

    grad_query, grad_key, grad_value = call(
        functools.partial(unpack_kernel if by_tiles else unpack_parts_kernel, ways),
        "unpack",
        [((frames, width), bf16)] * 3,
        semaphores=3 * ways if by_tiles else 0,
        far=("out",) if by_tiles else (),
        moved=6 * rows_bytes,
    )(info, *grad_packed)

    return (
        block_out[None],
        grad_residual[None],
        grad_query[None],
        grad_key[None],
        grad_value[None],
        out_total.T,
        point_total.T,
        taps,
        vectors,
    )


def solution(mesh):
    rows = P("dp", "ctx", None)
    columns = P(None, ("dp", "ctx"))
    in_specs = (rows, rows, rows, rows, P("dp"), P(), P(), P(), P(), P(), P(), rows)
    out_specs = (rows,) * 5 + (columns,) * 4
    return jax.shard_map(local, mesh=mesh, in_specs=in_specs, out_specs=out_specs, check_vma=False)
```

profile of v0, /device:TPU:0, one launch (start us, length us, event | category | flops | bytes accessed | tf_op | source)
XLA Modules:
  0.0 115.9 jit_solution(16343702784364323819)
XLA Ops:
  0.7 0.0 slice-start
  0.7 2.6 %pack.1 = (bf16[384,384]{1,0:T(8,128)(2,1)}, bf16[576,384]{1,0:T(8,128)(2,1)}, bf16[384,384]{1,0:T(8,128)(2,1)}, bf16[576,384]{1,0:T(8,128)(2,1)}) custom-call(bf16[128,1536]{1,0:T(8,128)(2,1)} %bitcast.22, bf16[128,1536]{1,0:T(8,128)(2,1)} %bitcast.23, bf16[128,1536]{1,0:T(8,128)(2,1)} %bitcast.24, bf16[128,1536]{1,0:T(8,128)(2,1)} %bitcast.18, ...), custom_call_target="tpu_custom_call" | custom-call | bytes 2359296 | tf_op jit(solution)/shard_map/pack/pallas_call | solution.py:43
  3.3 3.0 %collective-permute-start = (bf16[576,384]{1,0:T(8,128)(2,1)}, bf16[576,384]{1,0:T(8,128)(2,1)S(1)}, u32[]{:S(2)}, u32[]{:S(2)}) collective-permute-start(bf16[576,384]{1,0:T(8,128)(2,1)} %get-tuple-element.127), channel_id=1, source_target_pairs={{0,1},{1,0},{2,3},{3,2},{4,5},{5,4},{6,7},{7,6},{8,9},{9,8},{10,11... | collective-permute-start | bytes 1327112 | tf_op jit(solution)/shard_map/ppermute | solution.py:595
  6.3 1.5 %collective-permute-start.2 = (bf16[576,384]{1,0:T(8,128)(2,1)}, bf16[576,384]{1,0:T(8,128)(2,1)S(1)}, u32[]{:S(2)}, u32[]{:S(2)}) collective-permute-start(bf16[576,384]{1,0:T(8,128)(2,1)} %get-tuple-element.129), channel_id=1, source_target_pairs={{0,3},{1,2},{2,1},{3,0},{4,7},{5,6},{6,5},{7,4},{8,11},{9,10},{10,... | collective-permute-start | bytes 1327112 | tf_op jit(solution)/shard_map/ppermute | solution.py:595
  7.7 0.0 collective-permute-start.1
  8.4 0.1 pad_add_fusion.info
  8.5 0.7 mask.1
  9.3 2.1 %collective-permute-start.3 = (bf16[128,768]{1,0:T(8,128)(2,1)S(1)}, bf16[128,768]{1,0:T(8,128)(2,1)S(1)}, u32[]{:S(2)}, u32[]{:S(2)}) collective-permute-start(bf16[128,768]{1,0:T(8,128)(2,1)S(1)} %get-tuple-element.139), channel_id=1, source_target_pairs={{0,8},{4,12},{8,0},{12,4},{16,24},{20,28},{24,16},{28,20},{1,9},{5... | collective-permute-start | bytes 589832 | tf_op jit(solution)/shard_map/ppermute | solution.py:595
  11.4 2.6 %collective-permute-start.4 = (bf16[128,768]{1,0:T(8,128)(2,1)S(1)}, bf16[128,768]{1,0:T(8,128)(2,1)S(1)}, u32[]{:S(2)}, u32[]{:S(2)}) collective-permute-start(bf16[128,768]{1,0:T(8,128)(2,1)S(1)} %get-tuple-element.184.refs_0_), channel_id=1, source_target_pairs={{0,16},{4,20},{8,24},{12,28},{16,0},{20,4},{24,8},{28,12},{1,17},{... | collective-permute-start | bytes 589832 | tf_op jit(solution)/shard_map/ppermute | solution.py:595
  13.9 2.3 %copy-done = bf16[1536,1536]{1,0:T(8,128)(2,1)S(1)} copy-done((bf16[1536,1536]{1,0:T(8,128)(2,1)S(1)}, bf16[1536,1536]{1,0:T(8,128)(2,1)}, u32[]{:S(2)}) %copy-start) | copy-done | bytes 4718616
  16.3 1.0 copy-done.3
  17.2 2.2 %grad_act.1 = (f32[128,1536]{1,0:T(8,128)S(1)}, bf16[384,384]{1,0:T(8,128)(2,1)S(1)}) custom-call(s32[3]{0:T(128)S(1)} %pad_add_fusion.info, bf16[128,1536]{1,0:T(8,128)(2,1)S(1)} %get-tuple-element.124.masked, bf16[1536,1536]{1,0:T(8,128)(2,1)S(1)} %copy-done, bf16[384,384]{1,0:T(8,128)(2,1)S(1)} %copy-done.3), custom_call_target="tpu_custom_call" | custom-call | flops 603979776 | bytes 7077888 | tf_op jit(solution)/shard_map/grad_act/pallas_call | solution.py:43
  19.5 0.3 collective-permute-start.8
  19.8 0.0 collective-permute-done.refs_1_
  19.8 7.6 %collective-permute-done.2.refs_3_ = bf16[576,384]{1,0:T(8,128)(2,1)S(1)} collective-permute-done((bf16[576,384]{1,0:T(8,128)(2,1)}, bf16[576,384]{1,0:T(8,128)(2,1)S(1)}, u32[]{:S(2)}, u32[]{:S(2)}) %collective-permute-start.2) | collective-permute-done | bytes 442400 | tf_op jit(solution)/shard_map/ppermute | solution.py:595
  27.3 4.1 %attend.1 = (bf16[192,384]{1,0:T(8,128)(2,1)S(1)}, bf16[192,384]{1,0:T(8,128)(2,1)S(1)}, bf16[192,384]{1,0:T(8,128)(2,1)S(1)}, bf16[192,384]{1,0:T(8,128)(2,1)S(...) custom-call(s32[3]{0:T(128)S(1)} %pad_add_fusion.info, ...), custom_call_target="tpu_custom_call" | custom-call | flops 1610612736 | bytes 1572864 | tf_op jit(solution)/shard_map/attend/pallas_call | solution.py:43
  31.5 0.0 collective-permute-done.3.refs_1_
  31.5 1.6 %collective-permute-start.5 = (bf16[192,384]{1,0:T(8,128)(2,1)S(1)}, bf16[192,384]{1,0:T(8,128)(2,1)S(1)}, u32[]{:S(2)}, u32[]{:S(2)}) collective-permute-start(bf16[192,384]{1,0:T(8,128)(2,1)S(1)} %get-tuple-element.142), channel_id=1, source_target_pairs={{0,1},{1,0},{2,3},{3,2},{4,5},{5,4},{6,7},{7,6},{8,9},{9,8},{10,11... | collective-permute-start | bytes 442376 | tf_op jit(solution)/shard_map/ppermute | solution.py:595
  33.0 0.5 collective-permute-start.6
  33.5 1.5 %collective-permute-start.7 = (bf16[192,384]{1,0:T(8,128)(2,1)S(1)}, bf16[192,384]{1,0:T(8,128)(2,1)S(1)}, u32[]{:S(2)}, u32[]{:S(2)}) collective-permute-start(bf16[192,384]{1,0:T(8,128)(2,1)S(1)} %get-tuple-element.144), channel_id=1, source_target_pairs={{0,3},{1,2},{2,1},{3,0},{4,7},{5,6},{6,5},{7,4},{8,11},{9,10},{10,... | collective-permute-start | bytes 442376 | tf_op jit(solution)/shard_map/ppermute | solution.py:595
  35.1 0.0 copy-start.4
  35.1 2.0 %mask_edges.1.grad_edges = f32[32,1536]{1,0:T(8,128)S(1)} custom-call(s32[3]{0:T(128)S(1)} %pad_add_fusion.info, bf16[48,1536]{1,0:T(8,128)(2,1)S(1)} %get-tuple-element.145.before.refs_5_, bf16[48,1536]{1,0:T(8,128)(2,1)S(1)} %get-tuple-element.146.after.refs_6_, bf16[1536,1536]{1,0:T(8,128)(2,1)S(1)} %bitcast.15), custom_call_target="tpu_custom_call" | custom-call | flops 603979776 | bytes 4718592 | tf_op jit(solution)/shard_map/mask_edges/pallas_call | solution.py:43
  37.1 0.0 collective-permute-done.8.refs_3_
  37.2 0.8 collective-permute-done.5.refs_1_
  38.0 2.8 %collective-permute-done.6.refs_2_ = bf16[192,384]{1,0:T(8,128)(2,1)S(1)} collective-permute-done((bf16[192,384]{1,0:T(8,128)(2,1)S(1)}, bf16[192,384]{1,0:T(8,128)(2,1)S(1)}, u32[]{:S(2)}, u32[]{:S(2)}) %collective-permute-start.6) | collective-permute-done | bytes 147488 | tf_op jit(solution)/shard_map/ppermute | solution.py:595
  40.7 0.6 gather.1
  41.4 1.1 collective-permute-start.9
  42.5 1.4 %collective-permute-start.11 = (bf16[128,1152]{1,0:T(8,128)(2,1)S(1)}, bf16[128,1152]{1,0:T(8,128)(2,1)S(1)}, u32[]{:S(2)}, u32[]{:S(2)}) collective-permute-start(bf16[128,1152]{1,0:T(8,128)(2,1)S(1)} %get-tuple-element.155), channel_id=1, source_target_pairs={{0,1},{1,0},{2,3},{3,2},{4,5},{5,4},{6,7},{7,6},{8,9},{9,8},{10,11... | collective-permute-start | bytes 884744 | tf_op jit(solution)/shard_map/ppermute | solution.py:595
  43.9 1.0 collective-permute-start.12
  45.0 4.2 %project.1 = (f32[192,1536]{1,0:T(8,128)S(1)}, bf16[192,1536]{1,0:T(8,128)(2,1)S(1)}) custom-call(s32[3]{0:T(128)S(1)} %pad_add_fusion.info, bf16[192,384]{1,0:T(8,128)(2,1)S(1)} %get-tuple-element.157.refs_0_, bf16[192,384]{1,0:T(8,128)(2,1)S(1)} %collective-permute-done.5.refs_1_, bf16[192,384]{1,0:T(8,128)(2,1)S(1)} %collective-permute-done.6.refs_2_, ...), custom_call_target="tpu_custom_call" | custom-call | flops 603979776 | bytes 7077888 | tf_op jit(solution)/shard_map/project/pallas_call | solution.py:43
  49.2 6.6 %conv.1 = (bf16[160,1536]{1,0:T(8,128)(2,1)S(1)}, f32[12,160,128]{2,1,0:T(8,128)S(1)}, f32[2,1536]{1,0:T(2,128)S(1)}, bf16[128,768]{1,0:T(8,128)(2,1)S(1)}, bf16[128,768]{1,0:T(8,128)(2,1)S(1)}) custom-call(s32[3]{0:T(128)S(1)} %pad_add_fusion.info, bf16[192,1536]{1,0:T(8,128)(2,1)S(1)} %get-tuple-element.161.conv_in, ...), custom_call_target="tpu_custom_call" | custom-call | flops 786432000 | bytes 2359296 | tf_op jit(solution)/shard_map/conv/pallas_call | solution.py:43
  55.8 3.7 %collective-permute-start.15 = (bf16[128,768]{1,0:T(8,128)(2,1)S(1)}, bf16[128,768]{1,0:T(8,128)(2,1)S(1)}, u32[]{:S(2)}, u32[]{:S(2)}) collective-permute-start(bf16[128,768]{1,0:T(8,128)(2,1)S(1)} %get-tuple-element.175), channel_id=1, source_target_pairs={{0,24},{4,28},{8,16},{12,20},{16,8},{20,12},{24,0},{28,4},{1,25},{... | collective-permute-start | bytes 589832 | tf_op jit(solution)/shard_map/ppermute | solution.py:595
  59.5 0.8 collective-permute-start.13
  60.3 9.7 %conv_back.1 = (bf16[128,1536]{1,0:T(8,128)(2,1)}, bf16[304,384]{1,0:T(8,128)(2,1)S(1)}, bf16[304,384]{1,0:T(8,128)(2,1)S(1)}, bf16[304,384]{1,0:T(8,128)(2,1)S(1)}, bf16[304,384]{1,0:T(8,128)(2,1)S(1)}) custom-call(s32[3]{0:T(128)S(1)} %pad_add_fusion.info, f32[12,160,128]{2,1,0:T(8,128)S(1)} %get-tuple-element.165.grad_conv, ...), custom_call_target="tpu_custom_call" | custom-call | flops 1572864000 | bytes 7864320 | tf_op jit(solution)/shard_map/conv_back/pallas_call | solution.py:43
  69.9 0.4 collective-permute-start.10
  70.4 1.2 %collective-permute-start.16 = (bf16[304,384]{1,0:T(8,128)(2,1)S(1)}, bf16[304,384]{1,0:T(8,128)(2,1)S(1)}, u32[]{:S(2)}, u32[]{:S(2)}) collective-permute-start(bf16[304,384]{1,0:T(8,128)(2,1)S(1)} %get-tuple-element.182), channel_id=1, source_target_pairs={{0,2},{1,3},{2,0},{3,1},{4,6},{5,7},{6,4},{7,5},{8,10},{9,11},{10,... | collective-permute-start | bytes 700424 | tf_op jit(solution)/shard_map/ppermute | solution.py:595
  71.6 1.8 %collective-permute-start.17 = (bf16[304,384]{1,0:T(8,128)(2,1)S(1)}, bf16[304,384]{1,0:T(8,128)(2,1)S(1)}, u32[]{:S(2)}, u32[]{:S(2)}) collective-permute-start(bf16[304,384]{1,0:T(8,128)(2,1)S(1)} %get-tuple-element.183), channel_id=1, source_target_pairs={{0,3},{1,2},{2,1},{3,0},{4,7},{5,6},{6,5},{7,4},{8,11},{9,10},{10,... | collective-permute-start | bytes 700424 | tf_op jit(solution)/shard_map/ppermute | solution.py:595
  73.4 1.5 %collective-permute-done.14.refs_6_ = bf16[128,768]{1,0:T(8,128)(2,1)S(1)} collective-permute-done((bf16[128,768]{1,0:T(8,128)(2,1)S(1)}, bf16[128,768]{1,0:T(8,128)(2,1)S(1)}, u32[]{:S(2)}, u32[]{:S(2)}) %collective-permute-start.14) | collective-permute-done | bytes 196640 | tf_op jit(solution)/shard_map/ppermute | solution.py:595
  75.0 2.1 %block_out.1 = bf16[128,1536]{1,0:T(8,128)(2,1)} custom-call(s32[3]{0:T(128)S(1)} %pad_add_fusion.info, bf16[160,1536]{1,0:T(8,128)(2,1)S(1)} %get-tuple-element.193.conv_act, f32[192,1536]{1,0:T(8,128)S(1)} %get-tuple-element.166.mixed, bf16[1536,1536]{1,0:T(8,128)(2,1)S(1)} %bitcast.15), custom_call_target="tpu_custom_call" | custom-call | flops 603979776 | bytes 6291456 | tf_op jit(solution)/shard_map/block_out/pallas_call | solution.py:43
  77.1 1.3 %collective-permute-done.10.refs_5_.refs_1_ = bf16[304,384]{1,0:T(8,128)(2,1)S(1)} collective-permute-done((bf16[304,384]{1,0:T(8,128)(2,1)S(1)}, bf16[304,384]{1,0:T(8,128)(2,1)S(1)}, u32[]{:S(2)}, u32[]{:S(2)}) %collective-permute-start.10) | collective-permute-done | bytes 233504 | tf_op jit(solution)/shard_map/ppermute | solution.py:595
  78.3 1.8 %point_terms.1 = (bf16[4,96,768]{2,1,0:T(8,128)(2,1)S(1)}, f32[4,96,768]{2,1,0:T(8,128)S(1)}) custom-call(s32[3]{0:T(128)S(1)} %pad_add_fusion.info, bf16[128,768]{1,0:T(8,128)(2,1)S(1)} %get-tuple-element.184.refs_0_, bf16[128,768]{1,0:T(8,128)(2,1)S(1)} %collective-permute-done.3.refs_1_, bf16[128,768]{1,0:T(8,128)(2,1)S(1)} %collective-permute-done.4.refs_2_, ...), custom_call_target="tpu_custom_call" | custom-call | flops 603979776 | bytes 3145728 | tf_op jit(solution)/shard_map/point_terms/pallas_call | solution.py:43
  80.2 1.6 %collective-permute-done.17.refs_7_.refs_3_ = bf16[304,384]{1,0:T(8,128)(2,1)S(1)} collective-permute-done((bf16[304,384]{1,0:T(8,128)(2,1)S(1)}, bf16[304,384]{1,0:T(8,128)(2,1)S(1)}, u32[]{:S(2)}, u32[]{:S(2)}) %collective-permute-start.17) | collective-permute-done | bytes 233504 | tf_op jit(solution)/shard_map/ppermute | solution.py:595
  81.8 1.7 %out_terms.1 = (bf16[4,48,1664]{2,1,0:T(8,128)(2,1)S(1)}, f32[4,48,1664]{2,1,0:T(8,128)S(1)}) custom-call(s32[3]{0:T(128)S(1)} %pad_add_fusion.info, bf16[304,384]{1,0:T(8,128)(2,1)S(1)} %get-tuple-element.202.refs_4_.refs_0_, bf16[304,384]{1,0:T(8,128)(2,1)S(1)} %collective-permute-done.10.refs_5_.refs_1_, ...), custom_call_target="tpu_custom_call" | custom-call | flops 603979776 | bytes 3932160 | tf_op jit(solution)/shard_map/out_terms/pallas_call | solution.py:43
  83.5 0.1 collective-permute-start.25
  83.6 0.5 collective-permute-start.18
  84.1 2.4 %collective-permute-done.18.received = bf16[4,96,768]{2,1,0:T(8,128)(2,1)S(1)} collective-permute-done((bf16[4,96,768]{2,1,0:T(8,128)(2,1)S(1)}, bf16[4,96,768]{2,1,0:T(8,128)(2,1)S(1)}, u32[]{:S(2)}, u32[]{:S(2)}) %collective-permute-start.18) | collective-permute-done | bytes 589856 | tf_op jit(solution)/shard_map/ppermute | solution.py:595
  86.5 0.6 spread.1
  87.1 0.9 collective-permute-start.19
  88.0 1.5 %collective-permute-start.20 = (bf16[96,768]{1,0:T(8,128)(2,1)S(1)}, bf16[96,768]{1,0:T(8,128)(2,1)S(1)}, u32[]{:S(2)}, u32[]{:S(2)}) collective-permute-start(bf16[96,768]{1,0:T(8,128)(2,1)S(1)} %get-tuple-element.200), channel_id=1, source_target_pairs={{0,2},{1,3},{2,0},{3,1},{4,6},{5,7},{6,4},{7,5},{8,10},{9,11},{10,... | collective-permute-start | bytes 442376 | tf_op jit(solution)/shard_map/ppermute | solution.py:595
  89.5 1.2 %collective-permute-start.21 = (bf16[96,768]{1,0:T(8,128)(2,1)S(1)}, bf16[96,768]{1,0:T(8,128)(2,1)S(1)}, u32[]{:S(2)}, u32[]{:S(2)}) collective-permute-start(bf16[96,768]{1,0:T(8,128)(2,1)S(1)} %get-tuple-element.201), channel_id=1, source_target_pairs={{0,3},{1,2},{2,1},{3,0},{4,7},{5,6},{6,5},{7,4},{8,11},{9,10},{10,... | collective-permute-start | bytes 442376 | tf_op jit(solution)/shard_map/ppermute | solution.py:595
  90.7 0.7 halve.2
  91.4 1.5 %collective-permute-start.26 = (bf16[2,48,1664]{2,1,0:T(8,128)(2,1)S(1)}, bf16[2,48,1664]{2,1,0:T(8,128)(2,1)S(1)}, u32[]{:S(2)}, u32[]{:S(2)}) collective-permute-start(bf16[2,48,1664]{2,1,0:T(8,128)(2,1)S(1)} %get-tuple-element.226), channel_id=1, source_target_pairs={{0,8},{4,12},{8,0},{12,4},{16,24},{20,28},{24,16},{28,20},{1,9},{5... | collective-permute-start | bytes 958472 | tf_op jit(solution)/shard_map/ppermute | solution.py:595
  92.9 4.8 %attend_back.1 = (bf16[3,128,384]{2,1,0:T(8,128)(2,1)S(1)}, bf16[3,128,384]{2,1,0:T(8,128)(2,1)S(1)}, bf16[3,128,384]{2,1,0:T(8,128)(2,1)S(1)}, bf16[3,128,384]{2,1,0:T(8,128)(2,1)S(1)}) custom-call(s32[3]{0:T(128)S(1)} %pad_add_fusion.info, bf16[384,384]{1,0:T(8,128)(2,1)S(1)} %get-tuple-element.131.refs_0_, ...), custom_call_target="tpu_custom_call" | custom-call | flops 4026531840 | bytes 3145728 | tf_op jit(solution)/shard_map/attend_back/pallas_call | solution.py:43
  97.8 0.9 collective-permute-start.22
  98.7 1.5 %collective-permute-start.23 = (bf16[3,128,384]{2,1,0:T(8,128)(2,1)S(1)}, bf16[3,128,384]{2,1,0:T(8,128)(2,1)S(1)}, u32[]{:S(2)}, u32[]{:S(2)}) collective-permute-start(bf16[3,128,384]{2,1,0:T(8,128)(2,1)S(1)} %get-tuple-element.214), channel_id=1, source_target_pairs={{0,2},{1,3},{2,0},{3,1},{4,6},{5,7},{6,4},{7,5},{8,10},{9,11},{10,... | collective-permute-start | bytes 884744 | tf_op jit(solution)/shard_map/ppermute | solution.py:595
  100.2 1.1 collective-permute-start.24
  101.3 0.6 halve.3
  101.9 2.7 %collective-permute-start.27 = (bf16[1,48,1664]{2,1,0:T(8,128)(2,1)S(1)}, bf16[1,48,1664]{2,1,0:T(8,128)(2,1)S(1)}, u32[]{:S(2)}, u32[]{:S(2)}) collective-permute-start(bf16[1,48,1664]{2,1,0:T(8,128)(2,1)S(1)} %get-tuple-element.228), channel_id=1, source_target_pairs={{0,16},{4,20},{8,24},{12,28},{16,0},{20,4},{24,8},{28,12},{1,17},{... | collective-permute-start | bytes 479240 | tf_op jit(solution)/shard_map/ppermute | solution.py:595
  104.6 0.6 point_sum.1
  105.3 0.4 collective-permute-start.28
  105.6 2.1 %collective-permute-done.22.refs_1_ = bf16[3,128,384]{2,1,0:T(8,128)(2,1)S(1)} collective-permute-done((bf16[3,128,384]{2,1,0:T(8,128)(2,1)S(1)}, bf16[3,128,384]{2,1,0:T(8,128)(2,1)S(1)}, u32[]{:S(2)}, u32[]{:S(2)}) %collective-permute-start.22) | collective-permute-done | bytes 294944 | tf_op jit(solution)/shard_map/ppermute | solution.py:595
  107.8 4.9 %collective-permute-done.23.refs_2_ = bf16[3,128,384]{2,1,0:T(8,128)(2,1)S(1)} collective-permute-done((bf16[3,128,384]{2,1,0:T(8,128)(2,1)S(1)}, bf16[3,128,384]{2,1,0:T(8,128)(2,1)S(1)}, u32[]{:S(2)}, u32[]{:S(2)}) %collective-permute-start.23) | collective-permute-done | bytes 294944 | tf_op jit(solution)/shard_map/ppermute | solution.py:595
  112.7 1.6 %unpack.1 = (bf16[128,1536]{1,0:T(8,128)(2,1)}, bf16[128,1536]{1,0:T(8,128)(2,1)}, bf16[128,1536]{1,0:T(8,128)(2,1)}) custom-call(s32[3]{0:T(128)S(1)} %pad_add_fusion.info, bf16[3,128,384]{2,1,0:T(8,128)(2,1)S(1)} %get-tuple-element.212.refs_0_, bf16[3,128,384]{2,1,0:T(8,128)(2,1)S(1)} %collective-permute-done.22.refs_1_, ...), custom_call_target="tpu_custom_call" | custom-call | bytes 2359296 | tf_op jit(solution)/shard_map/unpack/pallas_call | solution.py:43
  114.3 1.6 %finish.1 = (f32[48,1536]{1,0:T(8,128)}, f32[31,48]{1,0:T(8,128)}, f32[3,48]{1,0:T(4,128)}, f32[48,1536]{1,0:T(8,128)}) custom-call(s32[3]{0:T(128)S(1)} %pad_add_fusion.info, f32[1,48,1664]{2,1,0:T(8,128)S(1)} %get-tuple-element.227.kept, bf16[1,48,1664]{2,1,0:T(8,128)(2,1)S(1)} %collective-permute-done.27.received, f32[48,768]{1,0:T(8,128)S(1)} %get-tuple-element.233.own, ...), custom_call_target="tpu_custom_call" | custom-call | bytes 1277952 | tf_op jit(solution)/shard_map/finish/pallas_call | solution.py:43
  (44 shorter events, 0.1 us)
Async XLA Ops:
  0.6 7.9 %copy-start.2 = (bf16[1,128,1536]{2,1,0:T(8,128)(2,1)S(1)}, bf16[1,128,1536]{2,1,0:T(8,128)(2,1)}, u32[]{:S(2)}) copy-start(bf16[1,128,1536]{2,1,0:T(8,128)(2,1)} %param.23) | copy-start | bytes 1179652
  0.7 34.4 %slice-start = ((s8[4718592]{0:T(1024)(128)(4,1)}), s8[524288]{0:T(1024)(128)(4,1)S(1)}, s32[]{:S(2)}) async-start(s8[4718592]{0:T(1024)(128)(4,1)} %bitcast.14), calls=%async_computation | async-start | bytes 1048576
  3.3 16.5 %collective-permute-start = (bf16[576,384]{1,0:T(8,128)(2,1)}, bf16[576,384]{1,0:T(8,128)(2,1)S(1)}, u32[]{:S(2)}, u32[]{:S(2)}) collective-permute-start(bf16[576,384]{1,0:T(8,128)(2,1)} %get-tuple-element.127), channel_id=1, source_target_pairs={{0,1},{1,0},{2,3},{3,2},{4,5},{5,4},{6,7},{7,6},{8,9},{9,8},{10,11... | collective-permute-start | bytes 1327112 | tf_op jit(solution)/shard_map/ppermute | solution.py:595
  6.3 21.1 %collective-permute-start.2 = (bf16[576,384]{1,0:T(8,128)(2,1)}, bf16[576,384]{1,0:T(8,128)(2,1)S(1)}, u32[]{:S(2)}, u32[]{:S(2)}) collective-permute-start(bf16[576,384]{1,0:T(8,128)(2,1)} %get-tuple-element.129), channel_id=1, source_target_pairs={{0,3},{1,2},{2,1},{3,0},{4,7},{5,6},{6,5},{7,4},{8,11},{9,10},{10,... | collective-permute-start | bytes 1327112 | tf_op jit(solution)/shard_map/ppermute | solution.py:595
  7.7 11.7 %collective-permute-start.1 = (bf16[384,384]{1,0:T(8,128)(2,1)}, bf16[384,384]{1,0:T(8,128)(2,1)S(1)}, u32[]{:S(2)}, u32[]{:S(2)}) collective-permute-start(bf16[384,384]{1,0:T(8,128)(2,1)} %get-tuple-element.128), channel_id=1, source_target_pairs={{0,2},{1,3},{2,0},{3,1},{4,6},{5,7},{6,4},{7,5},{8,10},{9,11},{10,... | collective-permute-start | bytes 884744 | tf_op jit(solution)/shard_map/ppermute | solution.py:595
  9.3 22.2 %collective-permute-start.3 = (bf16[128,768]{1,0:T(8,128)(2,1)S(1)}, bf16[128,768]{1,0:T(8,128)(2,1)S(1)}, u32[]{:S(2)}, u32[]{:S(2)}) collective-permute-start(bf16[128,768]{1,0:T(8,128)(2,1)S(1)} %get-tuple-element.139), channel_id=1, source_target_pairs={{0,8},{4,12},{8,0},{12,4},{16,24},{20,28},{24,16},{28,20},{1,9},{5... | collective-permute-start | bytes 589832 | tf_op jit(solution)/shard_map/ppermute | solution.py:595
  11.4 20.1 %collective-permute-start.4 = (bf16[128,768]{1,0:T(8,128)(2,1)S(1)}, bf16[128,768]{1,0:T(8,128)(2,1)S(1)}, u32[]{:S(2)}, u32[]{:S(2)}) collective-permute-start(bf16[128,768]{1,0:T(8,128)(2,1)S(1)} %get-tuple-element.184.refs_0_), channel_id=1, source_target_pairs={{0,16},{4,20},{8,24},{12,28},{16,0},{20,4},{24,8},{28,12},{1,17},{... | collective-permute-start | bytes 589832 | tf_op jit(solution)/shard_map/ppermute | solution.py:595
  13.9 2.3 %copy-start = (bf16[1536,1536]{1,0:T(8,128)(2,1)S(1)}, bf16[1536,1536]{1,0:T(8,128)(2,1)}, u32[]{:S(2)}) copy-start(bf16[1536,1536]{1,0:T(8,128)(2,1)} %point_weight.5) | copy-start | bytes 14155780
  16.3 1.0 copy-start.3
  17.2 17.9 %slice-start.1 = ((s8[4718592]{0:T(1024)(128)(4,1)}), s8[4194304]{0:T(1024)(128)(4,1)S(1)}, s32[]{:S(2)}) async-start(s8[4718592]{0:T(1024)(128)(4,1)} %bitcast.14), calls=%async_computation.1 | async-start | bytes 8388608
  17.2 27.7 %slice-start.2 = ((s8[4718592]{0:T(1024)(128)(4,1)}), s8[4194304]{0:T(1024)(128)(4,1)S(1)}, s32[]{:S(2)}) async-start(s8[4718592]{0:T(1024)(128)(4,1)} %bitcast.16), calls=%async_computation.2 | async-start | bytes 8388608
  19.5 17.7 %collective-permute-start.8 = (bf16[128,768]{1,0:T(8,128)(2,1)S(1)}, bf16[128,768]{1,0:T(8,128)(2,1)S(1)}, u32[]{:S(2)}, u32[]{:S(2)}) collective-permute-start(bf16[128,768]{1,0:T(8,128)(2,1)S(1)} %get-tuple-element.139), channel_id=1, source_target_pairs={{0,24},{4,28},{8,16},{12,20},{16,8},{20,12},{24,0},{28,4},{1,25},{... | collective-permute-start | bytes 589832 | tf_op jit(solution)/shard_map/ppermute | solution.py:595
  27.3 7.7 %copy-start.5 = (f32[1536]{0:T(1024)S(1)}, f32[1536]{0:T(1024)}, u32[]{:S(2)}) copy-start(f32[1536]{0:T(1024)} %param.18) | copy-start | bytes 18436
  27.3 7.7 %copy-start.6 = (f32[1536]{0:T(1024)S(1)}, f32[1536]{0:T(1024)}, u32[]{:S(2)}) copy-start(f32[1536]{0:T(1024)} %param.20) | copy-start | bytes 18436
  27.3 7.7 %copy-start.7 = (f32[1536]{0:T(1024)S(1)}, f32[1536]{0:T(1024)}, u32[]{:S(2)}) copy-start(f32[1536]{0:T(1024)} %param.21) | copy-start | bytes 18436
  27.3 17.7 %slice-start.3 = ((s8[4718592]{0:T(1024)(128)(4,1)}), s8[524288]{0:T(1024)(128)(4,1)S(1)}, s32[]{:S(2)}) async-start(s8[4718592]{0:T(1024)(128)(4,1)} %bitcast.16), calls=%async_computation.3 | async-start | bytes 1048576
  31.5 6.5 %collective-permute-start.5 = (bf16[192,384]{1,0:T(8,128)(2,1)S(1)}, bf16[192,384]{1,0:T(8,128)(2,1)S(1)}, u32[]{:S(2)}, u32[]{:S(2)}) collective-permute-start(bf16[192,384]{1,0:T(8,128)(2,1)S(1)} %get-tuple-element.142), channel_id=1, source_target_pairs={{0,1},{1,0},{2,3},{3,2},{4,5},{5,4},{6,7},{7,6},{8,9},{9,8},{10,11... | collective-permute-start | bytes 442376 | tf_op jit(solution)/shard_map/ppermute | solution.py:595
  33.0 7.7 %collective-permute-start.6 = (bf16[192,384]{1,0:T(8,128)(2,1)S(1)}, bf16[192,384]{1,0:T(8,128)(2,1)S(1)}, u32[]{:S(2)}, u32[]{:S(2)}) collective-permute-start(bf16[192,384]{1,0:T(8,128)(2,1)S(1)} %get-tuple-element.143), channel_id=1, source_target_pairs={{0,2},{1,3},{2,0},{3,1},{4,6},{5,7},{6,4},{7,5},{8,10},{9,11},{10,... | collective-permute-start | bytes 442376 | tf_op jit(solution)/shard_map/ppermute | solution.py:595
  33.5 7.2 %collective-permute-start.7 = (bf16[192,384]{1,0:T(8,128)(2,1)S(1)}, bf16[192,384]{1,0:T(8,128)(2,1)S(1)}, u32[]{:S(2)}, u32[]{:S(2)}) collective-permute-start(bf16[192,384]{1,0:T(8,128)(2,1)S(1)} %get-tuple-element.144), channel_id=1, source_target_pairs={{0,3},{1,2},{2,1},{3,0},{4,7},{5,6},{6,5},{7,4},{8,11},{9,10},{10,... | collective-permute-start | bytes 442376 | tf_op jit(solution)/shard_map/ppermute | solution.py:595
  35.1 9.8 %copy-start.4 = (f32[31,1536]{1,0:T(8,128)S(1)}, f32[31,1536]{1,0:T(8,128)}, u32[]{:S(2)}) copy-start(f32[31,1536]{1,0:T(8,128)} %param.19) | copy-start | bytes 571396
  37.1 7.9 %copy-start.1 = (bf16[1,128,1536]{2,1,0:T(8,128)(2,1)S(1)}, bf16[1,128,1536]{2,1,0:T(8,128)(2,1)}, u32[]{:S(2)}) copy-start(bf16[1,128,1536]{2,1,0:T(8,128)(2,1)} %param.12) | copy-start | bytes 1179652
  41.4 18.1 %collective-permute-start.9 = (bf16[128,1152]{1,0:T(8,128)(2,1)S(1)}, bf16[128,1152]{1,0:T(8,128)(2,1)S(1)}, u32[]{:S(2)}, u32[]{:S(2)}) collective-permute-start(bf16[128,1152]{1,0:T(8,128)(2,1)S(1)} %get-tuple-element.153), channel_id=1, source_target_pairs={{0,3},{1,2},{2,1},{3,0},{4,7},{5,6},{6,5},{7,4},{8,11},{9,10},{10,... | collective-permute-start | bytes 884744 | tf_op jit(solution)/shard_map/ppermute | solution.py:595
  42.5 13.3 %collective-permute-start.11 = (bf16[128,1152]{1,0:T(8,128)(2,1)S(1)}, bf16[128,1152]{1,0:T(8,128)(2,1)S(1)}, u32[]{:S(2)}, u32[]{:S(2)}) collective-permute-start(bf16[128,1152]{1,0:T(8,128)(2,1)S(1)} %get-tuple-element.155), channel_id=1, source_target_pairs={{0,1},{1,0},{2,3},{3,2},{4,5},{5,4},{6,7},{7,6},{8,9},{9,8},{10,11... | collective-permute-start | bytes 884744 | tf_op jit(solution)/shard_map/ppermute | solution.py:595
  43.9 11.9 %collective-permute-start.12 = (bf16[128,1152]{1,0:T(8,128)(2,1)S(1)}, bf16[128,1152]{1,0:T(8,128)(2,1)S(1)}, u32[]{:S(2)}, u32[]{:S(2)}) collective-permute-start(bf16[128,1152]{1,0:T(8,128)(2,1)S(1)} %get-tuple-element.156), channel_id=1, source_target_pairs={{0,2},{1,3},{2,0},{3,1},{4,6},{5,7},{6,4},{7,5},{8,10},{9,11},{10,... | collective-permute-start | bytes 884744 | tf_op jit(solution)/shard_map/ppermute | solution.py:595
  55.8 17.6 %collective-permute-start.15 = (bf16[128,768]{1,0:T(8,128)(2,1)S(1)}, bf16[128,768]{1,0:T(8,128)(2,1)S(1)}, u32[]{:S(2)}, u32[]{:S(2)}) collective-permute-start(bf16[128,768]{1,0:T(8,128)(2,1)S(1)} %get-tuple-element.175), channel_id=1, source_target_pairs={{0,24},{4,28},{8,16},{12,20},{16,8},{20,12},{24,0},{28,4},{1,25},{... | collective-permute-start | bytes 589832 | tf_op jit(solution)/shard_map/ppermute | solution.py:595
  59.5 15.5 %collective-permute-start.14 = (bf16[128,768]{1,0:T(8,128)(2,1)S(1)}, bf16[128,768]{1,0:T(8,128)(2,1)S(1)}, u32[]{:S(2)}, u32[]{:S(2)}) collective-permute-start(bf16[128,768]{1,0:T(8,128)(2,1)S(1)} %get-tuple-element.175), channel_id=1, source_target_pairs={{0,16},{4,20},{8,24},{12,28},{16,0},{20,4},{24,8},{28,12},{1,17},{... | collective-permute-start | bytes 589832 | tf_op jit(solution)/shard_map/ppermute | solution.py:595
  59.5 12.1 %collective-permute-start.13 = (bf16[128,768]{1,0:T(8,128)(2,1)S(1)}, bf16[128,768]{1,0:T(8,128)(2,1)S(1)}, u32[]{:S(2)}, u32[]{:S(2)}) collective-permute-start(bf16[128,768]{1,0:T(8,128)(2,1)S(1)} %get-tuple-element.188.refs_4_), channel_id=1, source_target_pairs={{0,8},{4,12},{8,0},{12,4},{16,24},{20,28},{24,16},{28,20},{1,9},{5... | collective-permute-start | bytes 589832 | tf_op jit(solution)/shard_map/ppermute | solution.py:595
  69.9 8.4 %collective-permute-start.10 = (bf16[304,384]{1,0:T(8,128)(2,1)S(1)}, bf16[304,384]{1,0:T(8,128)(2,1)S(1)}, u32[]{:S(2)}, u32[]{:S(2)}) collective-permute-start(bf16[304,384]{1,0:T(8,128)(2,1)S(1)} %get-tuple-element.169), channel_id=1, source_target_pairs={{0,1},{1,0},{2,3},{3,2},{4,5},{5,4},{6,7},{7,6},{8,9},{9,8},{10,11... | collective-permute-start | bytes 700424 | tf_op jit(solution)/shard_map/ppermute | solution.py:595
  70.4 9.8 %collective-permute-start.16 = (bf16[304,384]{1,0:T(8,128)(2,1)S(1)}, bf16[304,384]{1,0:T(8,128)(2,1)S(1)}, u32[]{:S(2)}, u32[]{:S(2)}) collective-permute-start(bf16[304,384]{1,0:T(8,128)(2,1)S(1)} %get-tuple-element.182), channel_id=1, source_target_pairs={{0,2},{1,3},{2,0},{3,1},{4,6},{5,7},{6,4},{7,5},{8,10},{9,11},{10,... | collective-permute-start | bytes 700424 | tf_op jit(solution)/shard_map/ppermute | solution.py:595
  71.6 10.2 %collective-permute-start.17 = (bf16[304,384]{1,0:T(8,128)(2,1)S(1)}, bf16[304,384]{1,0:T(8,128)(2,1)S(1)}, u32[]{:S(2)}, u32[]{:S(2)}) collective-permute-start(bf16[304,384]{1,0:T(8,128)(2,1)S(1)} %get-tuple-element.183), channel_id=1, source_target_pairs={{0,3},{1,2},{2,1},{3,0},{4,7},{5,6},{6,5},{7,4},{8,11},{9,10},{10,... | collective-permute-start | bytes 700424 | tf_op jit(solution)/shard_map/ppermute | solution.py:595
  83.5 7.2 %collective-permute-start.25 = (bf16[4,48,1664]{2,1,0:T(8,128)(2,1)S(1)}, bf16[4,48,1664]{2,1,0:T(8,128)(2,1)S(1)}, u32[]{:S(2)}, u32[]{:S(2)}) collective-permute-start(bf16[4,48,1664]{2,1,0:T(8,128)(2,1)S(1)} %get-tuple-element.224), channel_id=1, source_target_pairs={{0,4},{4,0},{8,12},{12,8},{16,20},{20,16},{24,28},{28,24},{1,5},{5... | collective-permute-start | bytes 1916936 | tf_op jit(solution)/shard_map/ppermute | solution.py:595
  83.6 2.9 %collective-permute-start.18 = (bf16[4,96,768]{2,1,0:T(8,128)(2,1)S(1)}, bf16[4,96,768]{2,1,0:T(8,128)(2,1)S(1)}, u32[]{:S(2)}, u32[]{:S(2)}) collective-permute-start(bf16[4,96,768]{2,1,0:T(8,128)(2,1)S(1)} %get-tuple-element.197), channel_id=1, source_target_pairs={{0,4},{4,0},{8,12},{12,8},{16,20},{20,16},{24,28},{28,24},{1,5},{5... | collective-permute-start | bytes 1769480 | tf_op jit(solution)/shard_map/ppermute | solution.py:595
  87.1 10.6 %collective-permute-start.19 = (bf16[96,768]{1,0:T(8,128)(2,1)S(1)}, bf16[96,768]{1,0:T(8,128)(2,1)S(1)}, u32[]{:S(2)}, u32[]{:S(2)}) collective-permute-start(bf16[96,768]{1,0:T(8,128)(2,1)S(1)} %get-tuple-element.199), channel_id=1, source_target_pairs={{0,1},{1,0},{2,3},{3,2},{4,5},{5,4},{6,7},{7,6},{8,9},{9,8},{10,11... | collective-permute-start | bytes 442376 | tf_op jit(solution)/shard_map/ppermute | solution.py:595
  88.0 9.7 %collective-permute-start.20 = (bf16[96,768]{1,0:T(8,128)(2,1)S(1)}, bf16[96,768]{1,0:T(8,128)(2,1)S(1)}, u32[]{:S(2)}, u32[]{:S(2)}) collective-permute-start(bf16[96,768]{1,0:T(8,128)(2,1)S(1)} %get-tuple-element.200), channel_id=1, source_target_pairs={{0,2},{1,3},{2,0},{3,1},{4,6},{5,7},{6,4},{7,5},{8,10},{9,11},{10,... | collective-permute-start | bytes 442376 | tf_op jit(solution)/shard_map/ppermute | solution.py:595
  89.5 8.2 %collective-permute-start.21 = (bf16[96,768]{1,0:T(8,128)(2,1)S(1)}, bf16[96,768]{1,0:T(8,128)(2,1)S(1)}, u32[]{:S(2)}, u32[]{:S(2)}) collective-permute-start(bf16[96,768]{1,0:T(8,128)(2,1)S(1)} %get-tuple-element.201), channel_id=1, source_target_pairs={{0,3},{1,2},{2,1},{3,0},{4,7},{5,6},{6,5},{7,4},{8,11},{9,10},{10,... | collective-permute-start | bytes 442376 | tf_op jit(solution)/shard_map/ppermute | solution.py:595
  91.4 10.0 %collective-permute-start.26 = (bf16[2,48,1664]{2,1,0:T(8,128)(2,1)S(1)}, bf16[2,48,1664]{2,1,0:T(8,128)(2,1)S(1)}, u32[]{:S(2)}, u32[]{:S(2)}) collective-permute-start(bf16[2,48,1664]{2,1,0:T(8,128)(2,1)S(1)} %get-tuple-element.226), channel_id=1, source_target_pairs={{0,8},{4,12},{8,0},{12,4},{16,24},{20,28},{24,16},{28,20},{1,9},{5... | collective-permute-start | bytes 958472 | tf_op jit(solution)/shard_map/ppermute | solution.py:595
  97.8 10.0 %collective-permute-start.22 = (bf16[3,128,384]{2,1,0:T(8,128)(2,1)S(1)}, bf16[3,128,384]{2,1,0:T(8,128)(2,1)S(1)}, u32[]{:S(2)}, u32[]{:S(2)}) collective-permute-start(bf16[3,128,384]{2,1,0:T(8,128)(2,1)S(1)} %get-tuple-element.213), channel_id=1, source_target_pairs={{0,1},{1,0},{2,3},{3,2},{4,5},{5,4},{6,7},{7,6},{8,9},{9,8},{10,11... | collective-permute-start | bytes 884744 | tf_op jit(solution)/shard_map/ppermute | solution.py:595
  98.7 14.0 %collective-permute-start.23 = (bf16[3,128,384]{2,1,0:T(8,128)(2,1)S(1)}, bf16[3,128,384]{2,1,0:T(8,128)(2,1)S(1)}, u32[]{:S(2)}, u32[]{:S(2)}) collective-permute-start(bf16[3,128,384]{2,1,0:T(8,128)(2,1)S(1)} %get-tuple-element.214), channel_id=1, source_target_pairs={{0,2},{1,3},{2,0},{3,1},{4,6},{5,7},{6,4},{7,5},{8,10},{9,11},{10,... | collective-permute-start | bytes 884744 | tf_op jit(solution)/shard_map/ppermute | solution.py:595
  100.2 12.5 %collective-permute-start.24 = (bf16[3,128,384]{2,1,0:T(8,128)(2,1)S(1)}, bf16[3,128,384]{2,1,0:T(8,128)(2,1)S(1)}, u32[]{:S(2)}, u32[]{:S(2)}) collective-permute-start(bf16[3,128,384]{2,1,0:T(8,128)(2,1)S(1)} %get-tuple-element.215), channel_id=1, source_target_pairs={{0,3},{1,2},{2,1},{3,0},{4,7},{5,6},{6,5},{7,4},{8,11},{9,10},{10,... | collective-permute-start | bytes 884744 | tf_op jit(solution)/shard_map/ppermute | solution.py:595
  101.9 12.4 %collective-permute-start.27 = (bf16[1,48,1664]{2,1,0:T(8,128)(2,1)S(1)}, bf16[1,48,1664]{2,1,0:T(8,128)(2,1)S(1)}, u32[]{:S(2)}, u32[]{:S(2)}) collective-permute-start(bf16[1,48,1664]{2,1,0:T(8,128)(2,1)S(1)} %get-tuple-element.228), channel_id=1, source_target_pairs={{0,16},{4,20},{8,24},{12,28},{16,0},{20,4},{24,8},{28,12},{1,17},{... | collective-permute-start | bytes 479240 | tf_op jit(solution)/shard_map/ppermute | solution.py:595
  105.3 9.0 %collective-permute-start.28 = (bf16[48,768]{1,0:T(8,128)(2,1)S(1)}, bf16[48,768]{1,0:T(8,128)(2,1)S(1)}, u32[]{:S(2)}, u32[]{:S(2)}) collective-permute-start(bf16[48,768]{1,0:T(8,128)(2,1)S(1)} %get-tuple-element.234), channel_id=1, source_target_pairs={{0,16},{4,20},{8,24},{12,28},{16,0},{20,4},{24,8},{28,12},{1,17},{... | collective-permute-start | bytes 221192 | tf_op jit(solution)/shard_map/ppermute | solution.py:595
where the time goes:
time: 116 us
  Pallas kernels  48.9 us (42%)
  starting transfers between devices  36.8 us (32%)
  waiting for transfers between devices  25 us (22%)
  local copies, waits for them, and re-layouts  3.36 us (3%)
  between operations  1.65 us (1%)
    pallas_call x19, Pallas kernels, run(): pl.pallas_call(kernel, name=name, in_specs=[smem if a.ndim == 1 else anyw...  48.9 us
    ppermute x29, starting transfers between devices, swap(): lax.ppermute(block, axis, [(i, i ^ by) for i in range(lax.axis_size(axis))])  36.8 us
    ppermute x29, waiting for transfers between devices, swap(): lax.ppermute(block, axis, [(i, i ^ by) for i in range(lax.axis_size(axis))])  25 us
    unnamed x24, local copies, waits for them, and re-layouts  3.34 us
  transfers between devices with their start and end apart: 29, of which 9 were waited for; matrix products, arithmetic and copies ran while one was open for 0% of the time, Pallas kernels for 37%

commit v1 on v0

--- a/solution.py
+++ b/solution.py
@@ -312,7 +312,7 @@
         conv_in[at, :] = jnp.where(valid, normed * gain, 0.0).astype(jnp.bfloat16)
         return carry
 
-    lax.fori_loop(0, rows // BAND, band, 0)
+    lax.fori_loop(0, rows // BAND, band, 0, unroll=2)
 
 
 def stride_of(rows):
@@ -405,7 +405,7 @@
 
         return carry
 
-    lax.fori_loop(0, rows // BAND, band, 0)
+    lax.fori_loop(0, rows // BAND, band, 0, unroll=2)
     sums[0:1, :] = jnp.sum(bias_sum[...], axis=0, keepdims=True)
     sums[1:2, :] = jnp.sum(gain_sum[...], axis=0, keepdims=True)
     half = width // 2
@@ -452,7 +452,7 @@
         )
         return carry
 
-    lax.fori_loop(0, frames // BAND, band, 0)
+    lax.fori_loop(0, frames // BAND, band, 0, unroll=2)
     for by in range(ways):
         at = pl.ds(pl.multiple_of((info[0] ^ by) * share, share), share)
         messages[by][:frames] = dot(grad_residual[...], out_weight[at, :], NT).astype(jnp.bfloat16)
@@ -848,6 +848,9 @@
         moved=slim * extent * (parts + 8),
     )(info, kept, received, point_own, point_other)
 
+    grad_packed, out_total, point_total = lax.optimization_barrier(
+        (grad_packed, out_total, point_total)
+    )
     grad_query, grad_key, grad_value = call(
         functools.partial(unpack_kernel if by_tiles else unpack_parts_kernel, ways),
         "unpack",

time: 116 us -> 116 us (level)
  waiting for transfers between devices: 25 us -> 27.9 us
  Pallas kernels: 48.9 us -> 46.8 us
    ppermute x29, waiting for transfers between devices: 25 us -> 27.9 us  [swap(): lax.ppermute(block, axis, [(i, i ^ by) for i in range(lax.axis_size(axis))])]
    pallas_call x19, Pallas kernels: 48.9 us -> 46.8 us  [run(): pl.pallas_call(kernel, name=name, in_specs=[smem if a.ndim == 1 else anyw...]
  transfers between devices with their start and end apart: 29 -> 29, of which waited for: 9 -> 9; matrix products, arithmetic and copies ran while one was open for 0% -> 0% of each run, Pallas kernels for 37% -> 35%
where the time goes in v1:
time: 116 us
  Pallas kernels  46.8 us (40%)
  starting transfers between devices  36.1 us (31%)
  waiting for transfers between devices  27.9 us (24%)
  local copies, waits for them, and re-layouts  3.36 us (3%)
  between operations  1.78 us (2%)
    pallas_call x19, Pallas kernels, run(): pl.pallas_call(kernel, name=name, in_specs=[smem if a.ndim == 1 else anyw...  46.8 us
    ppermute x29, starting transfers between devices, swap(): lax.ppermute(block, axis, [(i, i ^ by) for i in range(lax.axis_size(axis))])  36.1 us
    ppermute x29, waiting for transfers between devices, swap(): lax.ppermute(block, axis, [(i, i ^ by) for i in range(lax.axis_size(axis))])  27.9 us
    unnamed x24, local copies, waits for them, and re-layouts  3.34 us
  transfers between devices with their start and end apart: 29, of which 9 were waited for; matrix products, arithmetic and copies ran while one was open for 0% of the time, Pallas kernels for 35%

profile of v1, /device:TPU:0, one launch (start us, length us, event | category | flops | bytes accessed | tf_op | source)
XLA Modules:
  0.0 116.0 jit_solution(11677266152196078885)
XLA Ops:
  0.7 0.0 slice-start
  0.7 2.6 %pack.1 = (bf16[384,384]{1,0:T(8,128)(2,1)}, bf16[576,384]{1,0:T(8,128)(2,1)}, bf16[384,384]{1,0:T(8,128)(2,1)}, bf16[576,384]{1,0:T(8,128)(2,1)}) custom-call(bf16[128,1536]{1,0:T(8,128)(2,1)} %bitcast.22, bf16[128,1536]{1,0:T(8,128)(2,1)} %bitcast.23, bf16[128,1536]{1,0:T(8,128)(2,1)} %bitcast.24, bf16[128,1536]{1,0:T(8,128)(2,1)} %bitcast.18, ...), custom_call_target="tpu_custom_call" | custom-call | bytes 2359296 | tf_op jit(solution)/shard_map/pack/pallas_call | solution.py:43
  3.3 3.0 %collective-permute-start = (bf16[576,384]{1,0:T(8,128)(2,1)}, bf16[576,384]{1,0:T(8,128)(2,1)S(1)}, u32[]{:S(2)}, u32[]{:S(2)}) collective-permute-start(bf16[576,384]{1,0:T(8,128)(2,1)} %get-tuple-element.133), channel_id=1, source_target_pairs={{0,1},{1,0},{2,3},{3,2},{4,5},{5,4},{6,7},{7,6},{8,9},{9,8},{10,11... | collective-permute-start | bytes 1327112 | tf_op jit(solution)/shard_map/ppermute | solution.py:595
  6.3 1.5 %collective-permute-start.2 = (bf16[576,384]{1,0:T(8,128)(2,1)}, bf16[576,384]{1,0:T(8,128)(2,1)S(1)}, u32[]{:S(2)}, u32[]{:S(2)}) collective-permute-start(bf16[576,384]{1,0:T(8,128)(2,1)} %get-tuple-element.135), channel_id=1, source_target_pairs={{0,3},{1,2},{2,1},{3,0},{4,7},{5,6},{6,5},{7,4},{8,11},{9,10},{10,... | collective-permute-start | bytes 1327112 | tf_op jit(solution)/shard_map/ppermute | solution.py:595
  7.7 0.0 collective-permute-start.1
  8.4 0.1 pad_add_fusion.info
  8.5 0.7 mask.1
  9.3 2.1 %collective-permute-start.3 = (bf16[128,768]{1,0:T(8,128)(2,1)S(1)}, bf16[128,768]{1,0:T(8,128)(2,1)S(1)}, u32[]{:S(2)}, u32[]{:S(2)}) collective-permute-start(bf16[128,768]{1,0:T(8,128)(2,1)S(1)} %get-tuple-element.145), channel_id=1, source_target_pairs={{0,8},{4,12},{8,0},{12,4},{16,24},{20,28},{24,16},{28,20},{1,9},{5... | collective-permute-start | bytes 589832 | tf_op jit(solution)/shard_map/ppermute | solution.py:595
  11.4 2.6 %collective-permute-start.4 = (bf16[128,768]{1,0:T(8,128)(2,1)S(1)}, bf16[128,768]{1,0:T(8,128)(2,1)S(1)}, u32[]{:S(2)}, u32[]{:S(2)}) collective-permute-start(bf16[128,768]{1,0:T(8,128)(2,1)S(1)} %get-tuple-element.190.refs_0_), channel_id=1, source_target_pairs={{0,16},{4,20},{8,24},{12,28},{16,0},{20,4},{24,8},{28,12},{1,17},{... | collective-permute-start | bytes 589832 | tf_op jit(solution)/shard_map/ppermute | solution.py:595
  13.9 2.3 %copy-done = bf16[1536,1536]{1,0:T(8,128)(2,1)S(1)} copy-done((bf16[1536,1536]{1,0:T(8,128)(2,1)S(1)}, bf16[1536,1536]{1,0:T(8,128)(2,1)}, u32[]{:S(2)}) %copy-start) | copy-done | bytes 4718616
  16.3 1.0 copy-done.3
  17.2 2.2 %grad_act.1 = (f32[128,1536]{1,0:T(8,128)S(1)}, bf16[384,384]{1,0:T(8,128)(2,1)S(1)}) custom-call(s32[3]{0:T(128)S(1)} %pad_add_fusion.info, bf16[128,1536]{1,0:T(8,128)(2,1)S(1)} %get-tuple-element.130.masked, bf16[1536,1536]{1,0:T(8,128)(2,1)S(1)} %copy-done, bf16[384,384]{1,0:T(8,128)(2,1)S(1)} %copy-done.3), custom_call_target="tpu_custom_call" | custom-call | flops 603979776 | bytes 7077888 | tf_op jit(solution)/shard_map/grad_act/pallas_call | solution.py:43
  19.5 0.0 collective-permute-done.1.refs_2_
  19.5 0.3 collective-permute-start.8
  19.8 7.6 %collective-permute-done.2.refs_3_ = bf16[576,384]{1,0:T(8,128)(2,1)S(1)} collective-permute-done((bf16[576,384]{1,0:T(8,128)(2,1)}, bf16[576,384]{1,0:T(8,128)(2,1)S(1)}, u32[]{:S(2)}, u32[]{:S(2)}) %collective-permute-start.2) | collective-permute-done | bytes 442400 | tf_op jit(solution)/shard_map/ppermute | solution.py:595
  27.3 4.1 %attend.1 = (bf16[192,384]{1,0:T(8,128)(2,1)S(1)}, bf16[192,384]{1,0:T(8,128)(2,1)S(1)}, bf16[192,384]{1,0:T(8,128)(2,1)S(1)}, bf16[192,384]{1,0:T(8,128)(2,1)S(...) custom-call(s32[3]{0:T(128)S(1)} %pad_add_fusion.info, ...), custom_call_target="tpu_custom_call" | custom-call | flops 1610612736 | bytes 1572864 | tf_op jit(solution)/shard_map/attend/pallas_call | solution.py:43
  31.5 0.0 collective-permute-done.3.refs_1_
  31.5 1.6 %collective-permute-start.5 = (bf16[192,384]{1,0:T(8,128)(2,1)S(1)}, bf16[192,384]{1,0:T(8,128)(2,1)S(1)}, u32[]{:S(2)}, u32[]{:S(2)}) collective-permute-start(bf16[192,384]{1,0:T(8,128)(2,1)S(1)} %get-tuple-element.148), channel_id=1, source_target_pairs={{0,1},{1,0},{2,3},{3,2},{4,5},{5,4},{6,7},{7,6},{8,9},{9,8},{10,11... | collective-permute-start | bytes 442376 | tf_op jit(solution)/shard_map/ppermute | solution.py:595
  33.0 0.5 collective-permute-start.6
  33.5 1.5 %collective-permute-start.7 = (bf16[192,384]{1,0:T(8,128)(2,1)S(1)}, bf16[192,384]{1,0:T(8,128)(2,1)S(1)}, u32[]{:S(2)}, u32[]{:S(2)}) collective-permute-start(bf16[192,384]{1,0:T(8,128)(2,1)S(1)} %get-tuple-element.150), channel_id=1, source_target_pairs={{0,3},{1,2},{2,1},{3,0},{4,7},{5,6},{6,5},{7,4},{8,11},{9,10},{10,... | collective-permute-start | bytes 442376 | tf_op jit(solution)/shard_map/ppermute | solution.py:595
  35.1 0.0 copy-start.4
  35.1 2.0 %mask_edges.1.grad_edges = f32[32,1536]{1,0:T(8,128)S(1)} custom-call(s32[3]{0:T(128)S(1)} %pad_add_fusion.info, bf16[48,1536]{1,0:T(8,128)(2,1)S(1)} %get-tuple-element.151.before.refs_5_, bf16[48,1536]{1,0:T(8,128)(2,1)S(1)} %get-tuple-element.152.after.refs_6_, bf16[1536,1536]{1,0:T(8,128)(2,1)S(1)} %bitcast.15), custom_call_target="tpu_custom_call" | custom-call | flops 603979776 | bytes 4718592 | tf_op jit(solution)/shard_map/mask_edges/pallas_call | solution.py:43
  37.1 0.0 collective-permute-done.8.refs_3_
  37.2 0.8 collective-permute-done.5.refs_1_
  38.0 2.8 %collective-permute-done.6.refs_2_ = bf16[192,384]{1,0:T(8,128)(2,1)S(1)} collective-permute-done((bf16[192,384]{1,0:T(8,128)(2,1)S(1)}, bf16[192,384]{1,0:T(8,128)(2,1)S(1)}, u32[]{:S(2)}, u32[]{:S(2)}) %collective-permute-start.6) | collective-permute-done | bytes 147488 | tf_op jit(solution)/shard_map/ppermute | solution.py:595
  40.7 0.6 gather.1
  41.4 1.1 collective-permute-start.9
  42.5 1.4 %collective-permute-start.11 = (bf16[128,1152]{1,0:T(8,128)(2,1)S(1)}, bf16[128,1152]{1,0:T(8,128)(2,1)S(1)}, u32[]{:S(2)}, u32[]{:S(2)}) collective-permute-start(bf16[128,1152]{1,0:T(8,128)(2,1)S(1)} %get-tuple-element.161), channel_id=1, source_target_pairs={{0,1},{1,0},{2,3},{3,2},{4,5},{5,4},{6,7},{7,6},{8,9},{9,8},{10,11... | collective-permute-start | bytes 884744 | tf_op jit(solution)/shard_map/ppermute | solution.py:595
  43.9 1.0 collective-permute-start.12
  45.0 3.1 %project.1 = (f32[192,1536]{1,0:T(8,128)S(1)}, bf16[192,1536]{1,0:T(8,128)(2,1)S(1)}) custom-call(s32[3]{0:T(128)S(1)} %pad_add_fusion.info, bf16[192,384]{1,0:T(8,128)(2,1)S(1)} %get-tuple-element.163.refs_0_, bf16[192,384]{1,0:T(8,128)(2,1)S(1)} %collective-permute-done.5.refs_1_, bf16[192,384]{1,0:T(8,128)(2,1)S(1)} %collective-permute-done.6.refs_2_, ...), custom_call_target="tpu_custom_call" | custom-call | flops 603979776 | bytes 7077888 | tf_op jit(solution)/shard_map/project/pallas_call | solution.py:43
  48.1 6.6 %conv.1 = (bf16[160,1536]{1,0:T(8,128)(2,1)S(1)}, f32[12,160,128]{2,1,0:T(8,128)S(1)}, f32[2,1536]{1,0:T(2,128)S(1)}, bf16[128,768]{1,0:T(8,128)(2,1)S(1)}, bf16[128,768]{1,0:T(8,128)(2,1)S(1)}) custom-call(s32[3]{0:T(128)S(1)} %pad_add_fusion.info, bf16[192,1536]{1,0:T(8,128)(2,1)S(1)} %get-tuple-element.167.conv_in, ...), custom_call_target="tpu_custom_call" | custom-call | flops 786432000 | bytes 2359296 | tf_op jit(solution)/shard_map/conv/pallas_call | solution.py:43
  54.7 0.7 collective-permute-done.11.refs_5_
  55.4 3.6 %collective-permute-start.15 = (bf16[128,768]{1,0:T(8,128)(2,1)S(1)}, bf16[128,768]{1,0:T(8,128)(2,1)S(1)}, u32[]{:S(2)}, u32[]{:S(2)}) collective-permute-start(bf16[128,768]{1,0:T(8,128)(2,1)S(1)} %get-tuple-element.181), channel_id=1, source_target_pairs={{0,24},{4,28},{8,16},{12,20},{16,8},{20,12},{24,0},{28,4},{1,25},{... | collective-permute-start | bytes 589832 | tf_op jit(solution)/shard_map/ppermute | solution.py:595
  59.0 0.8 collective-permute-start.13
  59.8 8.6 %conv_back.1 = (bf16[128,1536]{1,0:T(8,128)(2,1)}, bf16[304,384]{1,0:T(8,128)(2,1)S(1)}, bf16[304,384]{1,0:T(8,128)(2,1)S(1)}, bf16[304,384]{1,0:T(8,128)(2,1)S(1)}, bf16[304,384]{1,0:T(8,128)(2,1)S(1)}) custom-call(s32[3]{0:T(128)S(1)} %pad_add_fusion.info, f32[12,160,128]{2,1,0:T(8,128)S(1)} %get-tuple-element.171.grad_conv, ...), custom_call_target="tpu_custom_call" | custom-call | flops 1572864000 | bytes 7864320 | tf_op jit(solution)/shard_map/conv_back/pallas_call | solution.py:43
  68.4 0.2 collective-permute-start.10
  68.7 1.3 %collective-permute-start.16 = (bf16[304,384]{1,0:T(8,128)(2,1)S(1)}, bf16[304,384]{1,0:T(8,128)(2,1)S(1)}, u32[]{:S(2)}, u32[]{:S(2)}) collective-permute-start(bf16[304,384]{1,0:T(8,128)(2,1)S(1)} %get-tuple-element.188), channel_id=1, source_target_pairs={{0,2},{1,3},{2,0},{3,1},{4,6},{5,7},{6,4},{7,5},{8,10},{9,11},{10,... | collective-permute-start | bytes 700424 | tf_op jit(solution)/shard_map/ppermute | solution.py:595
  70.0 1.0 collective-permute-done.13.refs_5_
  71.0 1.2 %collective-permute-start.17 = (bf16[304,384]{1,0:T(8,128)(2,1)S(1)}, bf16[304,384]{1,0:T(8,128)(2,1)S(1)}, u32[]{:S(2)}, u32[]{:S(2)}) collective-permute-start(bf16[304,384]{1,0:T(8,128)(2,1)S(1)} %get-tuple-element.189), channel_id=1, source_target_pairs={{0,3},{1,2},{2,1},{3,0},{4,7},{5,6},{6,5},{7,4},{8,11},{9,10},{10,... | collective-permute-start | bytes 700424 | tf_op jit(solution)/shard_map/ppermute | solution.py:595
  72.2 2.8 %collective-permute-done.14.refs_6_ = bf16[128,768]{1,0:T(8,128)(2,1)S(1)} collective-permute-done((bf16[128,768]{1,0:T(8,128)(2,1)S(1)}, bf16[128,768]{1,0:T(8,128)(2,1)S(1)}, u32[]{:S(2)}, u32[]{:S(2)}) %collective-permute-start.14) | collective-permute-done | bytes 196640 | tf_op jit(solution)/shard_map/ppermute | solution.py:595
  75.0 2.1 %block_out.1 = bf16[128,1536]{1,0:T(8,128)(2,1)} custom-call(s32[3]{0:T(128)S(1)} %pad_add_fusion.info, bf16[160,1536]{1,0:T(8,128)(2,1)S(1)} %get-tuple-element.199.conv_act, f32[192,1536]{1,0:T(8,128)S(1)} %get-tuple-element.172.mixed, bf16[1536,1536]{1,0:T(8,128)(2,1)S(1)} %bitcast.15), custom_call_target="tpu_custom_call" | custom-call | flops 603979776 | bytes 6291456 | tf_op jit(solution)/shard_map/block_out/pallas_call | solution.py:43
  77.1 1.8 %point_terms.1 = (bf16[4,96,768]{2,1,0:T(8,128)(2,1)S(1)}, f32[4,96,768]{2,1,0:T(8,128)S(1)}) custom-call(s32[3]{0:T(128)S(1)} %pad_add_fusion.info, bf16[128,768]{1,0:T(8,128)(2,1)S(1)} %get-tuple-element.190.refs_0_, bf16[128,768]{1,0:T(8,128)(2,1)S(1)} %collective-permute-done.3.refs_1_, bf16[128,768]{1,0:T(8,128)(2,1)S(1)} %collective-permute-done.4.refs_2_, ...), custom_call_target="tpu_custom_call" | custom-call | flops 603979776 | bytes 3145728 | tf_op jit(solution)/shard_map/point_terms/pallas_call | solution.py:43
  78.9 1.8 %collective-permute-done.17.refs_7_.refs_3_ = bf16[304,384]{1,0:T(8,128)(2,1)S(1)} collective-permute-done((bf16[304,384]{1,0:T(8,128)(2,1)S(1)}, bf16[304,384]{1,0:T(8,128)(2,1)S(1)}, u32[]{:S(2)}, u32[]{:S(2)}) %collective-permute-start.17) | collective-permute-done | bytes 233504 | tf_op jit(solution)/shard_map/ppermute | solution.py:595
  80.7 1.7 %out_terms.1 = (bf16[4,48,1664]{2,1,0:T(8,128)(2,1)S(1)}, f32[4,48,1664]{2,1,0:T(8,128)S(1)}) custom-call(s32[3]{0:T(128)S(1)} %pad_add_fusion.info, bf16[304,384]{1,0:T(8,128)(2,1)S(1)} %get-tuple-element.208.refs_4_.refs_0_, bf16[304,384]{1,0:T(8,128)(2,1)S(1)} %collective-permute-done.10.refs_5_.refs_1_, ...), custom_call_target="tpu_custom_call" | custom-call | flops 603979776 | bytes 3932160 | tf_op jit(solution)/shard_map/out_terms/pallas_call | solution.py:43
  82.4 0.1 collective-permute-start.25
  82.5 0.5 collective-permute-start.18
  83.0 2.4 %collective-permute-done.18.received = bf16[4,96,768]{2,1,0:T(8,128)(2,1)S(1)} collective-permute-done((bf16[4,96,768]{2,1,0:T(8,128)(2,1)S(1)}, bf16[4,96,768]{2,1,0:T(8,128)(2,1)S(1)}, u32[]{:S(2)}, u32[]{:S(2)}) %collective-permute-start.18) | collective-permute-done | bytes 589856 | tf_op jit(solution)/shard_map/ppermute | solution.py:595
  85.4 0.6 spread.1
  86.1 0.8 collective-permute-start.19
  86.9 1.6 %collective-permute-start.20 = (bf16[96,768]{1,0:T(8,128)(2,1)S(1)}, bf16[96,768]{1,0:T(8,128)(2,1)S(1)}, u32[]{:S(2)}, u32[]{:S(2)}) collective-permute-start(bf16[96,768]{1,0:T(8,128)(2,1)S(1)} %get-tuple-element.206), channel_id=1, source_target_pairs={{0,2},{1,3},{2,0},{3,1},{4,6},{5,7},{6,4},{7,5},{8,10},{9,11},{10,... | collective-permute-start | bytes 442376 | tf_op jit(solution)/shard_map/ppermute | solution.py:595
  88.5 1.2 %collective-permute-start.21 = (bf16[96,768]{1,0:T(8,128)(2,1)S(1)}, bf16[96,768]{1,0:T(8,128)(2,1)S(1)}, u32[]{:S(2)}, u32[]{:S(2)}) collective-permute-start(bf16[96,768]{1,0:T(8,128)(2,1)S(1)} %get-tuple-element.207), channel_id=1, source_target_pairs={{0,3},{1,2},{2,1},{3,0},{4,7},{5,6},{6,5},{7,4},{8,11},{9,10},{10,... | collective-permute-start | bytes 442376 | tf_op jit(solution)/shard_map/ppermute | solution.py:595
  89.6 0.7 halve.2
  90.3 1.5 %collective-permute-start.26 = (bf16[2,48,1664]{2,1,0:T(8,128)(2,1)S(1)}, bf16[2,48,1664]{2,1,0:T(8,128)(2,1)S(1)}, u32[]{:S(2)}, u32[]{:S(2)}) collective-permute-start(bf16[2,48,1664]{2,1,0:T(8,128)(2,1)S(1)} %get-tuple-element.229), channel_id=1, source_target_pairs={{0,8},{4,12},{8,0},{12,4},{16,24},{20,28},{24,16},{28,20},{1,9},{5... | collective-permute-start | bytes 958472 | tf_op jit(solution)/shard_map/ppermute | solution.py:595
  91.8 4.8 %attend_back.1 = (bf16[3,128,384]{2,1,0:T(8,128)(2,1)S(1)}, bf16[3,128,384]{2,1,0:T(8,128)(2,1)S(1)}, bf16[3,128,384]{2,1,0:T(8,128)(2,1)S(1)}, bf16[3,128,384]{2,1,0:T(8,128)(2,1)S(1)}) custom-call(s32[3]{0:T(128)S(1)} %pad_add_fusion.info, bf16[384,384]{1,0:T(8,128)(2,1)S(1)} %get-tuple-element.137.refs_0_, ...), custom_call_target="tpu_custom_call" | custom-call | flops 4026531840 | bytes 3145728 | tf_op jit(solution)/shard_map/attend_back/pallas_call | solution.py:43
  96.7 0.6 collective-permute-start.22
  97.3 1.8 %collective-permute-start.23 = (bf16[3,128,384]{2,1,0:T(8,128)(2,1)S(1)}, bf16[3,128,384]{2,1,0:T(8,128)(2,1)S(1)}, u32[]{:S(2)}, u32[]{:S(2)}) collective-permute-start(bf16[3,128,384]{2,1,0:T(8,128)(2,1)S(1)} %get-tuple-element.220), channel_id=1, source_target_pairs={{0,2},{1,3},{2,0},{3,1},{4,6},{5,7},{6,4},{7,5},{8,10},{9,11},{10,... | collective-permute-start | bytes 884744 | tf_op jit(solution)/shard_map/ppermute | solution.py:595
  99.1 1.1 collective-permute-start.24
  100.3 0.6 halve.3
  100.9 2.7 %collective-permute-start.27 = (bf16[1,48,1664]{2,1,0:T(8,128)(2,1)S(1)}, bf16[1,48,1664]{2,1,0:T(8,128)(2,1)S(1)}, u32[]{:S(2)}, u32[]{:S(2)}) collective-permute-start(bf16[1,48,1664]{2,1,0:T(8,128)(2,1)S(1)} %get-tuple-element.231), channel_id=1, source_target_pairs={{0,16},{4,20},{8,24},{12,28},{16,0},{20,4},{24,8},{28,12},{1,17},{... | collective-permute-start | bytes 479240 | tf_op jit(solution)/shard_map/ppermute | solution.py:595
  103.6 0.6 point_sum.1
  104.2 0.4 collective-permute-start.28
  104.6 8.0 %collective-permute-done.28.other = bf16[48,768]{1,0:T(8,128)(2,1)S(1)} collective-permute-done((bf16[48,768]{1,0:T(8,128)(2,1)S(1)}, bf16[48,768]{1,0:T(8,128)(2,1)S(1)}, u32[]{:S(2)}, u32[]{:S(2)}) %collective-permute-start.28) | collective-permute-done | bytes 73760 | tf_op jit(solution)/shard_map/ppermute | solution.py:595
  112.6 1.5 %finish.1 = (f32[48,1536]{1,0:T(8,128)}, f32[31,48]{1,0:T(8,128)}, f32[3,48]{1,0:T(4,128)}, f32[48,1536]{1,0:T(8,128)}) custom-call(s32[3]{0:T(128)S(1)} %pad_add_fusion.info, f32[1,48,1664]{2,1,0:T(8,128)S(1)} %get-tuple-element.230.kept, bf16[1,48,1664]{2,1,0:T(8,128)(2,1)S(1)} %collective-permute-done.27.received, f32[48,768]{1,0:T(8,128)S(1)} %get-tuple-element.236.own, ...), custom_call_target="tpu_custom_call" | custom-call | bytes 1277952 | tf_op jit(solution)/shard_map/finish/pallas_call | solution.py:43
  114.2 1.6 %unpack.1 = (bf16[128,1536]{1,0:T(8,128)(2,1)}, bf16[128,1536]{1,0:T(8,128)(2,1)}, bf16[128,1536]{1,0:T(8,128)(2,1)}) custom-call(s32[3]{0:T(128)S(1)} %pad_add_fusion.info, bf16[3,128,384]{2,1,0:T(8,128)(2,1)S(1)} %get-tuple-element.240.refs_0_, bf16[3,128,384]{2,1,0:T(8,128)(2,1)S(1)} %collective-permute-done.22.refs_1_, ...), custom_call_target="tpu_custom_call" | custom-call | bytes 2359296 | tf_op jit(solution)/shard_map/unpack/pallas_call | solution.py:43
  (44 shorter events, 0.1 us)
Async XLA Ops:
  0.6 7.9 %copy-start.2 = (bf16[1,128,1536]{2,1,0:T(8,128)(2,1)S(1)}, bf16[1,128,1536]{2,1,0:T(8,128)(2,1)}, u32[]{:S(2)}) copy-start(bf16[1,128,1536]{2,1,0:T(8,128)(2,1)} %param.23) | copy-start | bytes 1179652
  0.7 34.4 %slice-start = ((s8[4718592]{0:T(1024)(128)(4,1)}), s8[524288]{0:T(1024)(128)(4,1)S(1)}, s32[]{:S(2)}) async-start(s8[4718592]{0:T(1024)(128)(4,1)} %bitcast.14), calls=%async_computation | async-start | bytes 1048576
  3.3 16.5 %collective-permute-start = (bf16[576,384]{1,0:T(8,128)(2,1)}, bf16[576,384]{1,0:T(8,128)(2,1)S(1)}, u32[]{:S(2)}, u32[]{:S(2)}) collective-permute-start(bf16[576,384]{1,0:T(8,128)(2,1)} %get-tuple-element.133), channel_id=1, source_target_pairs={{0,1},{1,0},{2,3},{3,2},{4,5},{5,4},{6,7},{7,6},{8,9},{9,8},{10,11... | collective-permute-start | bytes 1327112 | tf_op jit(solution)/shard_map/ppermute | solution.py:595
  6.3 21.1 %collective-permute-start.2 = (bf16[576,384]{1,0:T(8,128)(2,1)}, bf16[576,384]{1,0:T(8,128)(2,1)S(1)}, u32[]{:S(2)}, u32[]{:S(2)}) collective-permute-start(bf16[576,384]{1,0:T(8,128)(2,1)} %get-tuple-element.135), channel_id=1, source_target_pairs={{0,3},{1,2},{2,1},{3,0},{4,7},{5,6},{6,5},{7,4},{8,11},{9,10},{10,... | collective-permute-start | bytes 1327112 | tf_op jit(solution)/shard_map/ppermute | solution.py:595
  7.7 11.7 %collective-permute-start.1 = (bf16[384,384]{1,0:T(8,128)(2,1)}, bf16[384,384]{1,0:T(8,128)(2,1)S(1)}, u32[]{:S(2)}, u32[]{:S(2)}) collective-permute-start(bf16[384,384]{1,0:T(8,128)(2,1)} %get-tuple-element.134), channel_id=1, source_target_pairs={{0,2},{1,3},{2,0},{3,1},{4,6},{5,7},{6,4},{7,5},{8,10},{9,11},{10,... | collective-permute-start | bytes 884744 | tf_op jit(solution)/shard_map/ppermute | solution.py:595
  9.3 22.2 %collective-permute-start.3 = (bf16[128,768]{1,0:T(8,128)(2,1)S(1)}, bf16[128,768]{1,0:T(8,128)(2,1)S(1)}, u32[]{:S(2)}, u32[]{:S(2)}) collective-permute-start(bf16[128,768]{1,0:T(8,128)(2,1)S(1)} %get-tuple-element.145), channel_id=1, source_target_pairs={{0,8},{4,12},{8,0},{12,4},{16,24},{20,28},{24,16},{28,20},{1,9},{5... | collective-permute-start | bytes 589832 | tf_op jit(solution)/shard_map/ppermute | solution.py:595
  11.4 20.1 %collective-permute-start.4 = (bf16[128,768]{1,0:T(8,128)(2,1)S(1)}, bf16[128,768]{1,0:T(8,128)(2,1)S(1)}, u32[]{:S(2)}, u32[]{:S(2)}) collective-permute-start(bf16[128,768]{1,0:T(8,128)(2,1)S(1)} %get-tuple-element.190.refs_0_), channel_id=1, source_target_pairs={{0,16},{4,20},{8,24},{12,28},{16,0},{20,4},{24,8},{28,12},{1,17},{... | collective-permute-start | bytes 589832 | tf_op jit(solution)/shard_map/ppermute | solution.py:595
  13.9 2.3 %copy-start = (bf16[1536,1536]{1,0:T(8,128)(2,1)S(1)}, bf16[1536,1536]{1,0:T(8,128)(2,1)}, u32[]{:S(2)}) copy-start(bf16[1536,1536]{1,0:T(8,128)(2,1)} %point_weight.5) | copy-start | bytes 14155780
  16.3 1.0 copy-start.3
  17.2 17.9 %slice-start.1 = ((s8[4718592]{0:T(1024)(128)(4,1)}), s8[4194304]{0:T(1024)(128)(4,1)S(1)}, s32[]{:S(2)}) async-start(s8[4718592]{0:T(1024)(128)(4,1)} %bitcast.14), calls=%async_computation.1 | async-start | bytes 8388608
  17.2 27.7 %slice-start.2 = ((s8[4718592]{0:T(1024)(128)(4,1)}), s8[4194304]{0:T(1024)(128)(4,1)S(1)}, s32[]{:S(2)}) async-start(s8[4718592]{0:T(1024)(128)(4,1)} %bitcast.16), calls=%async_computation.2 | async-start | bytes 8388608
  19.5 17.7 %collective-permute-start.8 = (bf16[128,768]{1,0:T(8,128)(2,1)S(1)}, bf16[128,768]{1,0:T(8,128)(2,1)S(1)}, u32[]{:S(2)}, u32[]{:S(2)}) collective-permute-start(bf16[128,768]{1,0:T(8,128)(2,1)S(1)} %get-tuple-element.145), channel_id=1, source_target_pairs={{0,24},{4,28},{8,16},{12,20},{16,8},{20,12},{24,0},{28,4},{1,25},{... | collective-permute-start | bytes 589832 | tf_op jit(solution)/shard_map/ppermute | solution.py:595
  27.3 7.7 %copy-start.5 = (f32[1536]{0:T(1024)S(1)}, f32[1536]{0:T(1024)}, u32[]{:S(2)}) copy-start(f32[1536]{0:T(1024)} %param.18) | copy-start | bytes 18436
  27.3 7.7 %copy-start.6 = (f32[1536]{0:T(1024)S(1)}, f32[1536]{0:T(1024)}, u32[]{:S(2)}) copy-start(f32[1536]{0:T(1024)} %param.20) | copy-start | bytes 18436
  27.3 7.7 %copy-start.7 = (f32[1536]{0:T(1024)S(1)}, f32[1536]{0:T(1024)}, u32[]{:S(2)}) copy-start(f32[1536]{0:T(1024)} %param.21) | copy-start | bytes 18436
  27.3 17.7 %slice-start.3 = ((s8[4718592]{0:T(1024)(128)(4,1)}), s8[524288]{0:T(1024)(128)(4,1)S(1)}, s32[]{:S(2)}) async-start(s8[4718592]{0:T(1024)(128)(4,1)} %bitcast.16), calls=%async_computation.3 | async-start | bytes 1048576
  31.5 6.5 %collective-permute-start.5 = (bf16[192,384]{1,0:T(8,128)(2,1)S(1)}, bf16[192,384]{1,0:T(8,128)(2,1)S(1)}, u32[]{:S(2)}, u32[]{:S(2)}) collective-permute-start(bf16[192,384]{1,0:T(8,128)(2,1)S(1)} %get-tuple-element.148), channel_id=1, source_target_pairs={{0,1},{1,0},{2,3},{3,2},{4,5},{5,4},{6,7},{7,6},{8,9},{9,8},{10,11... | collective-permute-start | bytes 442376 | tf_op jit(solution)/shard_map/ppermute | solution.py:595
  33.0 7.7 %collective-permute-start.6 = (bf16[192,384]{1,0:T(8,128)(2,1)S(1)}, bf16[192,384]{1,0:T(8,128)(2,1)S(1)}, u32[]{:S(2)}, u32[]{:S(2)}) collective-permute-start(bf16[192,384]{1,0:T(8,128)(2,1)S(1)} %get-tuple-element.149), channel_id=1, source_target_pairs={{0,2},{1,3},{2,0},{3,1},{4,6},{5,7},{6,4},{7,5},{8,10},{9,11},{10,... | collective-permute-start | bytes 442376 | tf_op jit(solution)/shard_map/ppermute | solution.py:595
  33.5 7.2 %collective-permute-start.7 = (bf16[192,384]{1,0:T(8,128)(2,1)S(1)}, bf16[192,384]{1,0:T(8,128)(2,1)S(1)}, u32[]{:S(2)}, u32[]{:S(2)}) collective-permute-start(bf16[192,384]{1,0:T(8,128)(2,1)S(1)} %get-tuple-element.150), channel_id=1, source_target_pairs={{0,3},{1,2},{2,1},{3,0},{4,7},{5,6},{6,5},{7,4},{8,11},{9,10},{10,... | collective-permute-start | bytes 442376 | tf_op jit(solution)/shard_map/ppermute | solution.py:595
  35.1 9.8 %copy-start.4 = (f32[31,1536]{1,0:T(8,128)S(1)}, f32[31,1536]{1,0:T(8,128)}, u32[]{:S(2)}) copy-start(f32[31,1536]{1,0:T(8,128)} %param.19) | copy-start | bytes 571396
  37.1 7.9 %copy-start.1 = (bf16[1,128,1536]{2,1,0:T(8,128)(2,1)S(1)}, bf16[1,128,1536]{2,1,0:T(8,128)(2,1)}, u32[]{:S(2)}) copy-start(bf16[1,128,1536]{2,1,0:T(8,128)(2,1)} %param.12) | copy-start | bytes 1179652
  41.4 17.6 %collective-permute-start.9 = (bf16[128,1152]{1,0:T(8,128)(2,1)S(1)}, bf16[128,1152]{1,0:T(8,128)(2,1)S(1)}, u32[]{:S(2)}, u32[]{:S(2)}) collective-permute-start(bf16[128,1152]{1,0:T(8,128)(2,1)S(1)} %get-tuple-element.159), channel_id=1, source_target_pairs={{0,3},{1,2},{2,1},{3,0},{4,7},{5,6},{6,5},{7,4},{8,11},{9,10},{10,... | collective-permute-start | bytes 884744 | tf_op jit(solution)/shard_map/ppermute | solution.py:595
  42.5 12.9 %collective-permute-start.11 = (bf16[128,1152]{1,0:T(8,128)(2,1)S(1)}, bf16[128,1152]{1,0:T(8,128)(2,1)S(1)}, u32[]{:S(2)}, u32[]{:S(2)}) collective-permute-start(bf16[128,1152]{1,0:T(8,128)(2,1)S(1)} %get-tuple-element.161), channel_id=1, source_target_pairs={{0,1},{1,0},{2,3},{3,2},{4,5},{5,4},{6,7},{7,6},{8,9},{9,8},{10,11... | collective-permute-start | bytes 884744 | tf_op jit(solution)/shard_map/ppermute | solution.py:595
  43.9 11.5 %collective-permute-start.12 = (bf16[128,1152]{1,0:T(8,128)(2,1)S(1)}, bf16[128,1152]{1,0:T(8,128)(2,1)S(1)}, u32[]{:S(2)}, u32[]{:S(2)}) collective-permute-start(bf16[128,1152]{1,0:T(8,128)(2,1)S(1)} %get-tuple-element.162), channel_id=1, source_target_pairs={{0,2},{1,3},{2,0},{3,1},{4,6},{5,7},{6,4},{7,5},{8,10},{9,11},{10,... | collective-permute-start | bytes 884744 | tf_op jit(solution)/shard_map/ppermute | solution.py:595
  55.4 16.8 %collective-permute-start.15 = (bf16[128,768]{1,0:T(8,128)(2,1)S(1)}, bf16[128,768]{1,0:T(8,128)(2,1)S(1)}, u32[]{:S(2)}, u32[]{:S(2)}) collective-permute-start(bf16[128,768]{1,0:T(8,128)(2,1)S(1)} %get-tuple-element.181), channel_id=1, source_target_pairs={{0,24},{4,28},{8,16},{12,20},{16,8},{20,12},{24,0},{28,4},{1,25},{... | collective-permute-start | bytes 589832 | tf_op jit(solution)/shard_map/ppermute | solution.py:595
  59.0 15.9 %collective-permute-start.14 = (bf16[128,768]{1,0:T(8,128)(2,1)S(1)}, bf16[128,768]{1,0:T(8,128)(2,1)S(1)}, u32[]{:S(2)}, u32[]{:S(2)}) collective-permute-start(bf16[128,768]{1,0:T(8,128)(2,1)S(1)} %get-tuple-element.181), channel_id=1, source_target_pairs={{0,16},{4,20},{8,24},{12,28},{16,0},{20,4},{24,8},{28,12},{1,17},{... | collective-permute-start | bytes 589832 | tf_op jit(solution)/shard_map/ppermute | solution.py:595
  59.0 11.9 %collective-permute-start.13 = (bf16[128,768]{1,0:T(8,128)(2,1)S(1)}, bf16[128,768]{1,0:T(8,128)(2,1)S(1)}, u32[]{:S(2)}, u32[]{:S(2)}) collective-permute-start(bf16[128,768]{1,0:T(8,128)(2,1)S(1)} %get-tuple-element.194.refs_4_), channel_id=1, source_target_pairs={{0,8},{4,12},{8,0},{12,4},{16,24},{20,28},{24,16},{28,20},{1,9},{5... | collective-permute-start | bytes 589832 | tf_op jit(solution)/shard_map/ppermute | solution.py:595
  68.4 8.6 %collective-permute-start.10 = (bf16[304,384]{1,0:T(8,128)(2,1)S(1)}, bf16[304,384]{1,0:T(8,128)(2,1)S(1)}, u32[]{:S(2)}, u32[]{:S(2)}) collective-permute-start(bf16[304,384]{1,0:T(8,128)(2,1)S(1)} %get-tuple-element.175), channel_id=1, source_target_pairs={{0,1},{1,0},{2,3},{3,2},{4,5},{5,4},{6,7},{7,6},{8,9},{9,8},{10,11... | collective-permute-start | bytes 700424 | tf_op jit(solution)/shard_map/ppermute | solution.py:595
  68.7 10.3 %collective-permute-start.16 = (bf16[304,384]{1,0:T(8,128)(2,1)S(1)}, bf16[304,384]{1,0:T(8,128)(2,1)S(1)}, u32[]{:S(2)}, u32[]{:S(2)}) collective-permute-start(bf16[304,384]{1,0:T(8,128)(2,1)S(1)} %get-tuple-element.188), channel_id=1, source_target_pairs={{0,2},{1,3},{2,0},{3,1},{4,6},{5,7},{6,4},{7,5},{8,10},{9,11},{10,... | collective-permute-start | bytes 700424 | tf_op jit(solution)/shard_map/ppermute | solution.py:595
  71.0 9.8 %collective-permute-start.17 = (bf16[304,384]{1,0:T(8,128)(2,1)S(1)}, bf16[304,384]{1,0:T(8,128)(2,1)S(1)}, u32[]{:S(2)}, u32[]{:S(2)}) collective-permute-start(bf16[304,384]{1,0:T(8,128)(2,1)S(1)} %get-tuple-element.189), channel_id=1, source_target_pairs={{0,3},{1,2},{2,1},{3,0},{4,7},{5,6},{6,5},{7,4},{8,11},{9,10},{10,... | collective-permute-start | bytes 700424 | tf_op jit(solution)/shard_map/ppermute | solution.py:595
  82.4 7.2 %collective-permute-start.25 = (bf16[4,48,1664]{2,1,0:T(8,128)(2,1)S(1)}, bf16[4,48,1664]{2,1,0:T(8,128)(2,1)S(1)}, u32[]{:S(2)}, u32[]{:S(2)}) collective-permute-start(bf16[4,48,1664]{2,1,0:T(8,128)(2,1)S(1)} %get-tuple-element.227), channel_id=1, source_target_pairs={{0,4},{4,0},{8,12},{12,8},{16,20},{20,16},{24,28},{28,24},{1,5},{5... | collective-permute-start | bytes 1916936 | tf_op jit(solution)/shard_map/ppermute | solution.py:595
  82.5 2.9 %collective-permute-start.18 = (bf16[4,96,768]{2,1,0:T(8,128)(2,1)S(1)}, bf16[4,96,768]{2,1,0:T(8,128)(2,1)S(1)}, u32[]{:S(2)}, u32[]{:S(2)}) collective-permute-start(bf16[4,96,768]{2,1,0:T(8,128)(2,1)S(1)} %get-tuple-element.203), channel_id=1, source_target_pairs={{0,4},{4,0},{8,12},{12,8},{16,20},{20,16},{24,28},{28,24},{1,5},{5... | collective-permute-start | bytes 1769480 | tf_op jit(solution)/shard_map/ppermute | solution.py:595
  86.1 10.6 %collective-permute-start.19 = (bf16[96,768]{1,0:T(8,128)(2,1)S(1)}, bf16[96,768]{1,0:T(8,128)(2,1)S(1)}, u32[]{:S(2)}, u32[]{:S(2)}) collective-permute-start(bf16[96,768]{1,0:T(8,128)(2,1)S(1)} %get-tuple-element.205), channel_id=1, source_target_pairs={{0,1},{1,0},{2,3},{3,2},{4,5},{5,4},{6,7},{7,6},{8,9},{9,8},{10,11... | collective-permute-start | bytes 442376 | tf_op jit(solution)/shard_map/ppermute | solution.py:595
  86.9 9.8 %collective-permute-start.20 = (bf16[96,768]{1,0:T(8,128)(2,1)S(1)}, bf16[96,768]{1,0:T(8,128)(2,1)S(1)}, u32[]{:S(2)}, u32[]{:S(2)}) collective-permute-start(bf16[96,768]{1,0:T(8,128)(2,1)S(1)} %get-tuple-element.206), channel_id=1, source_target_pairs={{0,2},{1,3},{2,0},{3,1},{4,6},{5,7},{6,4},{7,5},{8,10},{9,11},{10,... | collective-permute-start | bytes 442376 | tf_op jit(solution)/shard_map/ppermute | solution.py:595
  88.5 8.2 %collective-permute-start.21 = (bf16[96,768]{1,0:T(8,128)(2,1)S(1)}, bf16[96,768]{1,0:T(8,128)(2,1)S(1)}, u32[]{:S(2)}, u32[]{:S(2)}) collective-permute-start(bf16[96,768]{1,0:T(8,128)(2,1)S(1)} %get-tuple-element.207), channel_id=1, source_target_pairs={{0,3},{1,2},{2,1},{3,0},{4,7},{5,6},{6,5},{7,4},{8,11},{9,10},{10,... | collective-permute-start | bytes 442376 | tf_op jit(solution)/shard_map/ppermute | solution.py:595
  90.3 10.0 %collective-permute-start.26 = (bf16[2,48,1664]{2,1,0:T(8,128)(2,1)S(1)}, bf16[2,48,1664]{2,1,0:T(8,128)(2,1)S(1)}, u32[]{:S(2)}, u32[]{:S(2)}) collective-permute-start(bf16[2,48,1664]{2,1,0:T(8,128)(2,1)S(1)} %get-tuple-element.229), channel_id=1, source_target_pairs={{0,8},{4,12},{8,0},{12,4},{16,24},{20,28},{24,16},{28,20},{1,9},{5... | collective-permute-start | bytes 958472 | tf_op jit(solution)/shard_map/ppermute | solution.py:595
  96.7 17.5 %collective-permute-start.22 = (bf16[3,128,384]{2,1,0:T(8,128)(2,1)S(1)}, bf16[3,128,384]{2,1,0:T(8,128)(2,1)S(1)}, u32[]{:S(2)}, u32[]{:S(2)}) collective-permute-start(bf16[3,128,384]{2,1,0:T(8,128)(2,1)S(1)} %get-tuple-element.219), channel_id=1, source_target_pairs={{0,1},{1,0},{2,3},{3,2},{4,5},{5,4},{6,7},{7,6},{8,9},{9,8},{10,11... | collective-permute-start | bytes 884744 | tf_op jit(solution)/shard_map/ppermute | solution.py:595
  97.3 16.8 %collective-permute-start.23 = (bf16[3,128,384]{2,1,0:T(8,128)(2,1)S(1)}, bf16[3,128,384]{2,1,0:T(8,128)(2,1)S(1)}, u32[]{:S(2)}, u32[]{:S(2)}) collective-permute-start(bf16[3,128,384]{2,1,0:T(8,128)(2,1)S(1)} %get-tuple-element.220), channel_id=1, source_target_pairs={{0,2},{1,3},{2,0},{3,1},{4,6},{5,7},{6,4},{7,5},{8,10},{9,11},{10,... | collective-permute-start | bytes 884744 | tf_op jit(solution)/shard_map/ppermute | solution.py:595
  99.1 15.1 %collective-permute-start.24 = (bf16[3,128,384]{2,1,0:T(8,128)(2,1)S(1)}, bf16[3,128,384]{2,1,0:T(8,128)(2,1)S(1)}, u32[]{:S(2)}, u32[]{:S(2)}) collective-permute-start(bf16[3,128,384]{2,1,0:T(8,128)(2,1)S(1)} %get-tuple-element.221), channel_id=1, source_target_pairs={{0,3},{1,2},{2,1},{3,0},{4,7},{5,6},{6,5},{7,4},{8,11},{9,10},{10,... | collective-permute-start | bytes 884744 | tf_op jit(solution)/shard_map/ppermute | solution.py:595
  100.9 11.8 %collective-permute-start.27 = (bf16[1,48,1664]{2,1,0:T(8,128)(2,1)S(1)}, bf16[1,48,1664]{2,1,0:T(8,128)(2,1)S(1)}, u32[]{:S(2)}, u32[]{:S(2)}) collective-permute-start(bf16[1,48,1664]{2,1,0:T(8,128)(2,1)S(1)} %get-tuple-element.231), channel_id=1, source_target_pairs={{0,16},{4,20},{8,24},{12,28},{16,0},{20,4},{24,8},{28,12},{1,17},{... | collective-permute-start | bytes 479240 | tf_op jit(solution)/shard_map/ppermute | solution.py:595
  104.2 8.4 %collective-permute-start.28 = (bf16[48,768]{1,0:T(8,128)(2,1)S(1)}, bf16[48,768]{1,0:T(8,128)(2,1)S(1)}, u32[]{:S(2)}, u32[]{:S(2)}) collective-permute-start(bf16[48,768]{1,0:T(8,128)(2,1)S(1)} %get-tuple-element.237), channel_id=1, source_target_pairs={{0,16},{4,20},{8,24},{12,28},{16,0},{20,4},{24,8},{28,12},{1,17},{... | collective-permute-start | bytes 221192 | tf_op jit(solution)/shard_map/ppermute | solution.py:595

commit v2 on v0

--- a/solution.py
+++ b/solution.py
@@ -312,7 +312,7 @@
         conv_in[at, :] = jnp.where(valid, normed * gain, 0.0).astype(jnp.bfloat16)
         return carry
 
-    lax.fori_loop(0, rows // BAND, band, 0)
+    lax.fori_loop(0, rows // BAND, band, 0, unroll=4)
 
 
 def stride_of(rows):
@@ -387,7 +387,7 @@
     bias_sum[...] = jnp.zeros_like(bias_sum)
     gain_sum[...] = jnp.zeros_like(gain_sum)
 
-    def band(index, carry):
+    def band(index, inner):
         at = pl.ds(pl.multiple_of(index * BAND, BAND), BAND)
         normed, inv_scale = moments(from_columns(conv, at) + bias)
         scaled = normed * gain
@@ -398,14 +398,18 @@
         for column in range(width // LANES):
             grad_conv[column, at, :] = grad_rows[:, column * LANES : (column + 1) * LANES]
 
-        @pl.when((index >= EDGE // BAND) & (index < (EDGE + frames) // BAND))
-        def _():
+        if inner:
             bias_sum[...] += fold(grad_rows)
             gain_sum[...] += fold(grad_scaled * normed)
 
+    def inner_band(index, carry):
+        band(index, True)
         return carry
 
-    lax.fori_loop(0, rows // BAND, band, 0)
+    for index in range(EDGE // BAND):
+        band(index, False)
+        band((EDGE + frames) // BAND + index, False)
+    lax.fori_loop(EDGE // BAND, (EDGE + frames) // BAND, inner_band, 0, unroll=2)
     sums[0:1, :] = jnp.sum(bias_sum[...], axis=0, keepdims=True)
     sums[1:2, :] = jnp.sum(gain_sum[...], axis=0, keepdims=True)
     half = width // 2
@@ -452,7 +456,7 @@
         )
         return carry
 
-    lax.fori_loop(0, frames // BAND, band, 0)
+    lax.fori_loop(0, frames // BAND, band, 0, unroll=4)
     for by in range(ways):
         at = pl.ds(pl.multiple_of((info[0] ^ by) * share, share), share)
         messages[by][:frames] = dot(grad_residual[...], out_weight[at, :], NT).astype(jnp.bfloat16)

time: 116 us -> 114 us (0.983)
  Pallas kernels: 48.9 us -> 44.3 us
  waiting for transfers between devices: 25 us -> 28.7 us
    pallas_call x19, Pallas kernels: 48.9 us -> 44.3 us  [run(): pl.pallas_call(kernel, name=name, in_specs=[smem if a.ndim == 1 else anyw...]
    ppermute x29, waiting for transfers between devices: 25 us -> 28.7 us  [swap(): lax.ppermute(block, axis, [(i, i ^ by) for i in range(lax.axis_size(axis))])]
  transfers between devices with their start and end apart: 29 -> 29, of which waited for: 9 -> 11; matrix products, arithmetic and copies ran while one was open for 0% -> 0% of each run, Pallas kernels for 37% -> 33%
where the time goes in v2:
time: 114 us
  Pallas kernels  44.3 us (39%)
  starting transfers between devices  36.1 us (32%)
  waiting for transfers between devices  28.7 us (25%)
  local copies, waits for them, and re-layouts  3.36 us (3%)
  between operations  1.64 us (1%)
    pallas_call x19, Pallas kernels, run(): pl.pallas_call(kernel, name=name, in_specs=[smem if a.ndim == 1 else anyw...  44.3 us
    ppermute x29, starting transfers between devices, swap(): lax.ppermute(block, axis, [(i, i ^ by) for i in range(lax.axis_size(axis))])  36.1 us
    ppermute x29, waiting for transfers between devices, swap(): lax.ppermute(block, axis, [(i, i ^ by) for i in range(lax.axis_size(axis))])  28.7 us
    unnamed x24, local copies, waits for them, and re-layouts  3.34 us
  transfers between devices with their start and end apart: 29, of which 11 were waited for; matrix products, arithmetic and copies ran while one was open for 0% of the time, Pallas kernels for 33%

profile of v2, /device:TPU:0, one launch (start us, length us, event | category | flops | bytes accessed | tf_op | source)
XLA Modules:
  0.0 114.2 jit_solution(14473606624677685428)
XLA Ops:
  0.7 0.0 slice-start
  0.7 2.6 %pack.1 = (bf16[384,384]{1,0:T(8,128)(2,1)}, bf16[576,384]{1,0:T(8,128)(2,1)}, bf16[384,384]{1,0:T(8,128)(2,1)}, bf16[576,384]{1,0:T(8,128)(2,1)}) custom-call(bf16[128,1536]{1,0:T(8,128)(2,1)} %bitcast.22, bf16[128,1536]{1,0:T(8,128)(2,1)} %bitcast.23, bf16[128,1536]{1,0:T(8,128)(2,1)} %bitcast.24, bf16[128,1536]{1,0:T(8,128)(2,1)} %bitcast.18, ...), custom_call_target="tpu_custom_call" | custom-call | bytes 2359296 | tf_op jit(solution)/shard_map/pack/pallas_call | solution.py:43
  3.3 3.0 %collective-permute-start = (bf16[576,384]{1,0:T(8,128)(2,1)}, bf16[576,384]{1,0:T(8,128)(2,1)S(1)}, u32[]{:S(2)}, u32[]{:S(2)}) collective-permute-start(bf16[576,384]{1,0:T(8,128)(2,1)} %get-tuple-element.127), channel_id=1, source_target_pairs={{0,1},{1,0},{2,3},{3,2},{4,5},{5,4},{6,7},{7,6},{8,9},{9,8},{10,11... | collective-permute-start | bytes 1327112 | tf_op jit(solution)/shard_map/ppermute | solution.py:599
  6.3 1.5 %collective-permute-start.2 = (bf16[576,384]{1,0:T(8,128)(2,1)}, bf16[576,384]{1,0:T(8,128)(2,1)S(1)}, u32[]{:S(2)}, u32[]{:S(2)}) collective-permute-start(bf16[576,384]{1,0:T(8,128)(2,1)} %get-tuple-element.129), channel_id=1, source_target_pairs={{0,3},{1,2},{2,1},{3,0},{4,7},{5,6},{6,5},{7,4},{8,11},{9,10},{10,... | collective-permute-start | bytes 1327112 | tf_op jit(solution)/shard_map/ppermute | solution.py:599
  7.7 0.0 collective-permute-start.1
  8.4 0.1 pad_add_fusion.info
  8.5 0.7 mask.1
  9.3 2.1 %collective-permute-start.3 = (bf16[128,768]{1,0:T(8,128)(2,1)S(1)}, bf16[128,768]{1,0:T(8,128)(2,1)S(1)}, u32[]{:S(2)}, u32[]{:S(2)}) collective-permute-start(bf16[128,768]{1,0:T(8,128)(2,1)S(1)} %get-tuple-element.139), channel_id=1, source_target_pairs={{0,8},{4,12},{8,0},{12,4},{16,24},{20,28},{24,16},{28,20},{1,9},{5... | collective-permute-start | bytes 589832 | tf_op jit(solution)/shard_map/ppermute | solution.py:599
  11.4 2.6 %collective-permute-start.4 = (bf16[128,768]{1,0:T(8,128)(2,1)S(1)}, bf16[128,768]{1,0:T(8,128)(2,1)S(1)}, u32[]{:S(2)}, u32[]{:S(2)}) collective-permute-start(bf16[128,768]{1,0:T(8,128)(2,1)S(1)} %get-tuple-element.184.refs_0_), channel_id=1, source_target_pairs={{0,16},{4,20},{8,24},{12,28},{16,0},{20,4},{24,8},{28,12},{1,17},{... | collective-permute-start | bytes 589832 | tf_op jit(solution)/shard_map/ppermute | solution.py:599
  13.9 2.3 %copy-done = bf16[1536,1536]{1,0:T(8,128)(2,1)S(1)} copy-done((bf16[1536,1536]{1,0:T(8,128)(2,1)S(1)}, bf16[1536,1536]{1,0:T(8,128)(2,1)}, u32[]{:S(2)}) %copy-start) | copy-done | bytes 4718616
  16.3 1.0 copy-done.3
  17.2 2.2 %grad_act.1 = (f32[128,1536]{1,0:T(8,128)S(1)}, bf16[384,384]{1,0:T(8,128)(2,1)S(1)}) custom-call(s32[3]{0:T(128)S(1)} %pad_add_fusion.info, bf16[128,1536]{1,0:T(8,128)(2,1)S(1)} %get-tuple-element.124.masked, bf16[1536,1536]{1,0:T(8,128)(2,1)S(1)} %copy-done, bf16[384,384]{1,0:T(8,128)(2,1)S(1)} %copy-done.3), custom_call_target="tpu_custom_call" | custom-call | flops 603979776 | bytes 7077888 | tf_op jit(solution)/shard_map/grad_act/pallas_call | solution.py:43
  19.5 0.3 collective-permute-start.8
  19.8 7.6 %collective-permute-done.2.refs_3_ = bf16[576,384]{1,0:T(8,128)(2,1)S(1)} collective-permute-done((bf16[576,384]{1,0:T(8,128)(2,1)}, bf16[576,384]{1,0:T(8,128)(2,1)S(1)}, u32[]{:S(2)}, u32[]{:S(2)}) %collective-permute-start.2) | collective-permute-done | bytes 442400 | tf_op jit(solution)/shard_map/ppermute | solution.py:599
  27.3 4.1 %attend.1 = (bf16[192,384]{1,0:T(8,128)(2,1)S(1)}, bf16[192,384]{1,0:T(8,128)(2,1)S(1)}, bf16[192,384]{1,0:T(8,128)(2,1)S(1)}, bf16[192,384]{1,0:T(8,128)(2,1)S(...) custom-call(s32[3]{0:T(128)S(1)} %pad_add_fusion.info, ...), custom_call_target="tpu_custom_call" | custom-call | flops 1610612736 | bytes 1572864 | tf_op jit(solution)/shard_map/attend/pallas_call | solution.py:43
  31.5 1.6 %collective-permute-start.5 = (bf16[192,384]{1,0:T(8,128)(2,1)S(1)}, bf16[192,384]{1,0:T(8,128)(2,1)S(1)}, u32[]{:S(2)}, u32[]{:S(2)}) collective-permute-start(bf16[192,384]{1,0:T(8,128)(2,1)S(1)} %get-tuple-element.142), channel_id=1, source_target_pairs={{0,1},{1,0},{2,3},{3,2},{4,5},{5,4},{6,7},{7,6},{8,9},{9,8},{10,11... | collective-permute-start | bytes 442376 | tf_op jit(solution)/shard_map/ppermute | solution.py:599
  33.0 0.5 collective-permute-start.6
  33.5 1.5 %collective-permute-start.7 = (bf16[192,384]{1,0:T(8,128)(2,1)S(1)}, bf16[192,384]{1,0:T(8,128)(2,1)S(1)}, u32[]{:S(2)}, u32[]{:S(2)}) collective-permute-start(bf16[192,384]{1,0:T(8,128)(2,1)S(1)} %get-tuple-element.144), channel_id=1, source_target_pairs={{0,3},{1,2},{2,1},{3,0},{4,7},{5,6},{6,5},{7,4},{8,11},{9,10},{10,... | collective-permute-start | bytes 442376 | tf_op jit(solution)/shard_map/ppermute | solution.py:599
  35.1 0.0 copy-start.4
  35.1 2.0 %mask_edges.1.grad_edges = f32[32,1536]{1,0:T(8,128)S(1)} custom-call(s32[3]{0:T(128)S(1)} %pad_add_fusion.info, bf16[48,1536]{1,0:T(8,128)(2,1)S(1)} %get-tuple-element.145.before.refs_5_, bf16[48,1536]{1,0:T(8,128)(2,1)S(1)} %get-tuple-element.146.after.refs_6_, bf16[1536,1536]{1,0:T(8,128)(2,1)S(1)} %bitcast.15), custom_call_target="tpu_custom_call" | custom-call | flops 603979776 | bytes 4718592 | tf_op jit(solution)/shard_map/mask_edges/pallas_call | solution.py:43
  37.1 0.0 collective-permute-done.8.refs_3_
  37.2 0.8 collective-permute-done.5.refs_1_
  38.0 2.8 %collective-permute-done.6.refs_2_ = bf16[192,384]{1,0:T(8,128)(2,1)S(1)} collective-permute-done((bf16[192,384]{1,0:T(8,128)(2,1)S(1)}, bf16[192,384]{1,0:T(8,128)(2,1)S(1)}, u32[]{:S(2)}, u32[]{:S(2)}) %collective-permute-start.6) | collective-permute-done | bytes 147488 | tf_op jit(solution)/shard_map/ppermute | solution.py:599
  40.7 0.6 gather.1
  41.4 1.1 %collective-permute-start.9 = (bf16[128,1152]{1,0:T(8,128)(2,1)S(1)}, bf16[128,1152]{1,0:T(8,128)(2,1)S(1)}, u32[]{:S(2)}, u32[]{:S(2)}) collective-permute-start(bf16[128,1152]{1,0:T(8,128)(2,1)S(1)} %get-tuple-element.153), channel_id=1, source_target_pairs={{0,3},{1,2},{2,1},{3,0},{4,7},{5,6},{6,5},{7,4},{8,11},{9,10},{10,... | collective-permute-start | bytes 884744 | tf_op jit(solution)/shard_map/ppermute | solution.py:599
  42.5 1.4 %collective-permute-start.11 = (bf16[128,1152]{1,0:T(8,128)(2,1)S(1)}, bf16[128,1152]{1,0:T(8,128)(2,1)S(1)}, u32[]{:S(2)}, u32[]{:S(2)}) collective-permute-start(bf16[128,1152]{1,0:T(8,128)(2,1)S(1)} %get-tuple-element.155), channel_id=1, source_target_pairs={{0,1},{1,0},{2,3},{3,2},{4,5},{5,4},{6,7},{7,6},{8,9},{9,8},{10,11... | collective-permute-start | bytes 884744 | tf_op jit(solution)/shard_map/ppermute | solution.py:599
  43.9 1.0 collective-permute-start.12
  45.0 2.5 %project.1 = (f32[192,1536]{1,0:T(8,128)S(1)}, bf16[192,1536]{1,0:T(8,128)(2,1)S(1)}) custom-call(s32[3]{0:T(128)S(1)} %pad_add_fusion.info, bf16[192,384]{1,0:T(8,128)(2,1)S(1)} %get-tuple-element.157.refs_0_, bf16[192,384]{1,0:T(8,128)(2,1)S(1)} %collective-permute-done.5.refs_1_, bf16[192,384]{1,0:T(8,128)(2,1)S(1)} %collective-permute-done.6.refs_2_, ...), custom_call_target="tpu_custom_call" | custom-call | flops 603979776 | bytes 7077888 | tf_op jit(solution)/shard_map/project/pallas_call | solution.py:43
  47.6 5.2 %conv.1 = (bf16[160,1536]{1,0:T(8,128)(2,1)S(1)}, f32[12,160,128]{2,1,0:T(8,128)S(1)}, f32[2,1536]{1,0:T(2,128)S(1)}, bf16[128,768]{1,0:T(8,128)(2,1)S(1)}, bf16[128,768]{1,0:T(8,128)(2,1)S(1)}) custom-call(s32[3]{0:T(128)S(1)} %pad_add_fusion.info, bf16[192,1536]{1,0:T(8,128)(2,1)S(1)} %get-tuple-element.161.conv_in, ...), custom_call_target="tpu_custom_call" | custom-call | flops 786432000 | bytes 2359296 | tf_op jit(solution)/shard_map/conv/pallas_call | solution.py:43
  52.8 2.6 %collective-permute-done.11.refs_5_ = bf16[128,1152]{1,0:T(8,128)(2,1)S(1)} collective-permute-done((bf16[128,1152]{1,0:T(8,128)(2,1)S(1)}, bf16[128,1152]{1,0:T(8,128)(2,1)S(1)}, u32[]{:S(2)}, u32[]{:S(2)}) %collective-permute-start.11) | collective-permute-done | bytes 294944 | tf_op jit(solution)/shard_map/ppermute | solution.py:599
  55.4 3.6 %collective-permute-start.15 = (bf16[128,768]{1,0:T(8,128)(2,1)S(1)}, bf16[128,768]{1,0:T(8,128)(2,1)S(1)}, u32[]{:S(2)}, u32[]{:S(2)}) collective-permute-start(bf16[128,768]{1,0:T(8,128)(2,1)S(1)} %get-tuple-element.175), channel_id=1, source_target_pairs={{0,24},{4,28},{8,16},{12,20},{16,8},{20,12},{24,0},{28,4},{1,25},{... | collective-permute-start | bytes 589832 | tf_op jit(solution)/shard_map/ppermute | solution.py:599
  59.0 0.8 collective-permute-start.13
  59.8 8.1 %conv_back.1 = (bf16[128,1536]{1,0:T(8,128)(2,1)}, bf16[304,384]{1,0:T(8,128)(2,1)S(1)}, bf16[304,384]{1,0:T(8,128)(2,1)S(1)}, bf16[304,384]{1,0:T(8,128)(2,1)S(1)}, bf16[304,384]{1,0:T(8,128)(2,1)S(1)}) custom-call(s32[3]{0:T(128)S(1)} %pad_add_fusion.info, f32[12,160,128]{2,1,0:T(8,128)S(1)} %get-tuple-element.165.grad_conv, ...), custom_call_target="tpu_custom_call" | custom-call | flops 1572864000 | bytes 7864320 | tf_op jit(solution)/shard_map/conv_back/pallas_call | solution.py:43
  67.9 0.2 collective-permute-start.10
  68.1 1.3 %collective-permute-start.16 = (bf16[304,384]{1,0:T(8,128)(2,1)S(1)}, bf16[304,384]{1,0:T(8,128)(2,1)S(1)}, u32[]{:S(2)}, u32[]{:S(2)}) collective-permute-start(bf16[304,384]{1,0:T(8,128)(2,1)S(1)} %get-tuple-element.182), channel_id=1, source_target_pairs={{0,2},{1,3},{2,0},{3,1},{4,6},{5,7},{6,4},{7,5},{8,10},{9,11},{10,... | collective-permute-start | bytes 700424 | tf_op jit(solution)/shard_map/ppermute | solution.py:599
  69.5 1.5 %collective-permute-done.13.refs_5_ = bf16[128,768]{1,0:T(8,128)(2,1)S(1)} collective-permute-done((bf16[128,768]{1,0:T(8,128)(2,1)S(1)}, bf16[128,768]{1,0:T(8,128)(2,1)S(1)}, u32[]{:S(2)}, u32[]{:S(2)}) %collective-permute-start.13) | collective-permute-done | bytes 196640 | tf_op jit(solution)/shard_map/ppermute | solution.py:599
  71.0 1.2 %collective-permute-start.17 = (bf16[304,384]{1,0:T(8,128)(2,1)S(1)}, bf16[304,384]{1,0:T(8,128)(2,1)S(1)}, u32[]{:S(2)}, u32[]{:S(2)}) collective-permute-start(bf16[304,384]{1,0:T(8,128)(2,1)S(1)} %get-tuple-element.183), channel_id=1, source_target_pairs={{0,3},{1,2},{2,1},{3,0},{4,7},{5,6},{6,5},{7,4},{8,11},{9,10},{10,... | collective-permute-start | bytes 700424 | tf_op jit(solution)/shard_map/ppermute | solution.py:599
  72.2 2.8 %collective-permute-done.14.refs_6_ = bf16[128,768]{1,0:T(8,128)(2,1)S(1)} collective-permute-done((bf16[128,768]{1,0:T(8,128)(2,1)S(1)}, bf16[128,768]{1,0:T(8,128)(2,1)S(1)}, u32[]{:S(2)}, u32[]{:S(2)}) %collective-permute-start.14) | collective-permute-done | bytes 196640 | tf_op jit(solution)/shard_map/ppermute | solution.py:599
  75.0 2.1 %block_out.1 = bf16[128,1536]{1,0:T(8,128)(2,1)} custom-call(s32[3]{0:T(128)S(1)} %pad_add_fusion.info, bf16[160,1536]{1,0:T(8,128)(2,1)S(1)} %get-tuple-element.193.conv_act, f32[192,1536]{1,0:T(8,128)S(1)} %get-tuple-element.166.mixed, bf16[1536,1536]{1,0:T(8,128)(2,1)S(1)} %bitcast.15), custom_call_target="tpu_custom_call" | custom-call | flops 603979776 | bytes 6291456 | tf_op jit(solution)/shard_map/block_out/pallas_call | solution.py:43
  77.1 1.8 %point_terms.1 = (bf16[4,96,768]{2,1,0:T(8,128)(2,1)S(1)}, f32[4,96,768]{2,1,0:T(8,128)S(1)}) custom-call(s32[3]{0:T(128)S(1)} %pad_add_fusion.info, bf16[128,768]{1,0:T(8,128)(2,1)S(1)} %get-tuple-element.184.refs_0_, bf16[128,768]{1,0:T(8,128)(2,1)S(1)} %collective-permute-done.3.refs_1_, bf16[128,768]{1,0:T(8,128)(2,1)S(1)} %collective-permute-done.4.refs_2_, ...), custom_call_target="tpu_custom_call" | custom-call | flops 603979776 | bytes 3145728 | tf_op jit(solution)/shard_map/point_terms/pallas_call | solution.py:43
  78.9 1.3 %collective-permute-done.17.refs_7_.refs_3_ = bf16[304,384]{1,0:T(8,128)(2,1)S(1)} collective-permute-done((bf16[304,384]{1,0:T(8,128)(2,1)S(1)}, bf16[304,384]{1,0:T(8,128)(2,1)S(1)}, u32[]{:S(2)}, u32[]{:S(2)}) %collective-permute-start.17) | collective-permute-done | bytes 233504 | tf_op jit(solution)/shard_map/ppermute | solution.py:599
  80.2 1.7 %out_terms.1 = (bf16[4,48,1664]{2,1,0:T(8,128)(2,1)S(1)}, f32[4,48,1664]{2,1,0:T(8,128)S(1)}) custom-call(s32[3]{0:T(128)S(1)} %pad_add_fusion.info, bf16[304,384]{1,0:T(8,128)(2,1)S(1)} %get-tuple-element.202.refs_4_.refs_0_, bf16[304,384]{1,0:T(8,128)(2,1)S(1)} %collective-permute-done.10.refs_5_.refs_1_, ...), custom_call_target="tpu_custom_call" | custom-call | flops 603979776 | bytes 3932160 | tf_op jit(solution)/shard_map/out_terms/pallas_call | solution.py:43
  81.9 0.1 collective-permute-start.25
  82.0 0.5 collective-permute-start.18
  82.5 2.4 %collective-permute-done.18.received = bf16[4,96,768]{2,1,0:T(8,128)(2,1)S(1)} collective-permute-done((bf16[4,96,768]{2,1,0:T(8,128)(2,1)S(1)}, bf16[4,96,768]{2,1,0:T(8,128)(2,1)S(1)}, u32[]{:S(2)}, u32[]{:S(2)}) %collective-permute-start.18) | collective-permute-done | bytes 589856 | tf_op jit(solution)/shard_map/ppermute | solution.py:599
  84.9 0.6 spread.1
  85.5 0.8 collective-permute-start.19
  86.4 1.6 %collective-permute-start.20 = (bf16[96,768]{1,0:T(8,128)(2,1)S(1)}, bf16[96,768]{1,0:T(8,128)(2,1)S(1)}, u32[]{:S(2)}, u32[]{:S(2)}) collective-permute-start(bf16[96,768]{1,0:T(8,128)(2,1)S(1)} %get-tuple-element.200), channel_id=1, source_target_pairs={{0,2},{1,3},{2,0},{3,1},{4,6},{5,7},{6,4},{7,5},{8,10},{9,11},{10,... | collective-permute-start | bytes 442376 | tf_op jit(solution)/shard_map/ppermute | solution.py:599
  87.9 1.2 %collective-permute-start.21 = (bf16[96,768]{1,0:T(8,128)(2,1)S(1)}, bf16[96,768]{1,0:T(8,128)(2,1)S(1)}, u32[]{:S(2)}, u32[]{:S(2)}) collective-permute-start(bf16[96,768]{1,0:T(8,128)(2,1)S(1)} %get-tuple-element.201), channel_id=1, source_target_pairs={{0,3},{1,2},{2,1},{3,0},{4,7},{5,6},{6,5},{7,4},{8,11},{9,10},{10,... | collective-permute-start | bytes 442376 | tf_op jit(solution)/shard_map/ppermute | solution.py:599
  89.1 0.7 halve.2
  89.8 1.5 %collective-permute-start.26 = (bf16[2,48,1664]{2,1,0:T(8,128)(2,1)S(1)}, bf16[2,48,1664]{2,1,0:T(8,128)(2,1)S(1)}, u32[]{:S(2)}, u32[]{:S(2)}) collective-permute-start(bf16[2,48,1664]{2,1,0:T(8,128)(2,1)S(1)} %get-tuple-element.226), channel_id=1, source_target_pairs={{0,8},{4,12},{8,0},{12,4},{16,24},{20,28},{24,16},{28,20},{1,9},{5... | collective-permute-start | bytes 958472 | tf_op jit(solution)/shard_map/ppermute | solution.py:599
  91.3 4.8 %attend_back.1 = (bf16[3,128,384]{2,1,0:T(8,128)(2,1)S(1)}, bf16[3,128,384]{2,1,0:T(8,128)(2,1)S(1)}, bf16[3,128,384]{2,1,0:T(8,128)(2,1)S(1)}, bf16[3,128,384]{2,1,0:T(8,128)(2,1)S(1)}) custom-call(s32[3]{0:T(128)S(1)} %pad_add_fusion.info, bf16[384,384]{1,0:T(8,128)(2,1)S(1)} %get-tuple-element.131.refs_0_, ...), custom_call_target="tpu_custom_call" | custom-call | flops 4026531840 | bytes 3145728 | tf_op jit(solution)/shard_map/attend_back/pallas_call | solution.py:43
  96.2 0.6 collective-permute-start.22
  96.8 1.8 %collective-permute-start.23 = (bf16[3,128,384]{2,1,0:T(8,128)(2,1)S(1)}, bf16[3,128,384]{2,1,0:T(8,128)(2,1)S(1)}, u32[]{:S(2)}, u32[]{:S(2)}) collective-permute-start(bf16[3,128,384]{2,1,0:T(8,128)(2,1)S(1)} %get-tuple-element.214), channel_id=1, source_target_pairs={{0,2},{1,3},{2,0},{3,1},{4,6},{5,7},{6,4},{7,5},{8,10},{9,11},{10,... | collective-permute-start | bytes 884744 | tf_op jit(solution)/shard_map/ppermute | solution.py:599
  98.6 1.2 %collective-permute-start.24 = (bf16[3,128,384]{2,1,0:T(8,128)(2,1)S(1)}, bf16[3,128,384]{2,1,0:T(8,128)(2,1)S(1)}, u32[]{:S(2)}, u32[]{:S(2)}) collective-permute-start(bf16[3,128,384]{2,1,0:T(8,128)(2,1)S(1)} %get-tuple-element.215), channel_id=1, source_target_pairs={{0,3},{1,2},{2,1},{3,0},{4,7},{5,6},{6,5},{7,4},{8,11},{9,10},{10,... | collective-permute-start | bytes 884744 | tf_op jit(solution)/shard_map/ppermute | solution.py:599
  99.7 0.6 halve.3
  100.3 2.7 %collective-permute-start.27 = (bf16[1,48,1664]{2,1,0:T(8,128)(2,1)S(1)}, bf16[1,48,1664]{2,1,0:T(8,128)(2,1)S(1)}, u32[]{:S(2)}, u32[]{:S(2)}) collective-permute-start(bf16[1,48,1664]{2,1,0:T(8,128)(2,1)S(1)} %get-tuple-element.228), channel_id=1, source_target_pairs={{0,16},{4,20},{8,24},{12,28},{16,0},{20,4},{24,8},{28,12},{1,17},{... | collective-permute-start | bytes 479240 | tf_op jit(solution)/shard_map/ppermute | solution.py:599
  103.1 0.6 point_sum.1
  103.7 0.4 collective-permute-start.28
  104.0 2.1 %collective-permute-done.22.refs_1_ = bf16[3,128,384]{2,1,0:T(8,128)(2,1)S(1)} collective-permute-done((bf16[3,128,384]{2,1,0:T(8,128)(2,1)S(1)}, bf16[3,128,384]{2,1,0:T(8,128)(2,1)S(1)}, u32[]{:S(2)}, u32[]{:S(2)}) %collective-permute-start.22) | collective-permute-done | bytes 294944 | tf_op jit(solution)/shard_map/ppermute | solution.py:599
  106.2 3.9 %collective-permute-done.23.refs_2_ = bf16[3,128,384]{2,1,0:T(8,128)(2,1)S(1)} collective-permute-done((bf16[3,128,384]{2,1,0:T(8,128)(2,1)S(1)}, bf16[3,128,384]{2,1,0:T(8,128)(2,1)S(1)}, u32[]{:S(2)}, u32[]{:S(2)}) %collective-permute-start.23) | collective-permute-done | bytes 294944 | tf_op jit(solution)/shard_map/ppermute | solution.py:599
  110.1 0.9 collective-permute-done.24.refs_3_
  111.0 1.6 %unpack.1 = (bf16[128,1536]{1,0:T(8,128)(2,1)}, bf16[128,1536]{1,0:T(8,128)(2,1)}, bf16[128,1536]{1,0:T(8,128)(2,1)}) custom-call(s32[3]{0:T(128)S(1)} %pad_add_fusion.info, bf16[3,128,384]{2,1,0:T(8,128)(2,1)S(1)} %get-tuple-element.212.refs_0_, bf16[3,128,384]{2,1,0:T(8,128)(2,1)S(1)} %collective-permute-done.22.refs_1_, ...), custom_call_target="tpu_custom_call" | custom-call | bytes 2359296 | tf_op jit(solution)/shard_map/unpack/pallas_call | solution.py:43
  112.6 1.6 %finish.1 = (f32[48,1536]{1,0:T(8,128)}, f32[31,48]{1,0:T(8,128)}, f32[3,48]{1,0:T(4,128)}, f32[48,1536]{1,0:T(8,128)}) custom-call(s32[3]{0:T(128)S(1)} %pad_add_fusion.info, f32[1,48,1664]{2,1,0:T(8,128)S(1)} %get-tuple-element.227.kept, bf16[1,48,1664]{2,1,0:T(8,128)(2,1)S(1)} %collective-permute-done.27.received, f32[48,768]{1,0:T(8,128)S(1)} %get-tuple-element.233.own, ...), custom_call_target="tpu_custom_call" | custom-call | bytes 1277952 | tf_op jit(solution)/shard_map/finish/pallas_call | solution.py:43
  (44 shorter events, 0.1 us)
Async XLA Ops:
  0.6 7.9 %copy-start.2 = (bf16[1,128,1536]{2,1,0:T(8,128)(2,1)S(1)}, bf16[1,128,1536]{2,1,0:T(8,128)(2,1)}, u32[]{:S(2)}) copy-start(bf16[1,128,1536]{2,1,0:T(8,128)(2,1)} %param.23) | copy-start | bytes 1179652
  0.7 34.4 %slice-start = ((s8[4718592]{0:T(1024)(128)(4,1)}), s8[524288]{0:T(1024)(128)(4,1)S(1)}, s32[]{:S(2)}) async-start(s8[4718592]{0:T(1024)(128)(4,1)} %bitcast.14), calls=%async_computation | async-start | bytes 1048576
  3.3 16.5 %collective-permute-start = (bf16[576,384]{1,0:T(8,128)(2,1)}, bf16[576,384]{1,0:T(8,128)(2,1)S(1)}, u32[]{:S(2)}, u32[]{:S(2)}) collective-permute-start(bf16[576,384]{1,0:T(8,128)(2,1)} %get-tuple-element.127), channel_id=1, source_target_pairs={{0,1},{1,0},{2,3},{3,2},{4,5},{5,4},{6,7},{7,6},{8,9},{9,8},{10,11... | collective-permute-start | bytes 1327112 | tf_op jit(solution)/shard_map/ppermute | solution.py:599
  6.3 21.1 %collective-permute-start.2 = (bf16[576,384]{1,0:T(8,128)(2,1)}, bf16[576,384]{1,0:T(8,128)(2,1)S(1)}, u32[]{:S(2)}, u32[]{:S(2)}) collective-permute-start(bf16[576,384]{1,0:T(8,128)(2,1)} %get-tuple-element.129), channel_id=1, source_target_pairs={{0,3},{1,2},{2,1},{3,0},{4,7},{5,6},{6,5},{7,4},{8,11},{9,10},{10,... | collective-permute-start | bytes 1327112 | tf_op jit(solution)/shard_map/ppermute | solution.py:599
  7.7 11.7 %collective-permute-start.1 = (bf16[384,384]{1,0:T(8,128)(2,1)}, bf16[384,384]{1,0:T(8,128)(2,1)S(1)}, u32[]{:S(2)}, u32[]{:S(2)}) collective-permute-start(bf16[384,384]{1,0:T(8,128)(2,1)} %get-tuple-element.128), channel_id=1, source_target_pairs={{0,2},{1,3},{2,0},{3,1},{4,6},{5,7},{6,4},{7,5},{8,10},{9,11},{10,... | collective-permute-start | bytes 884744 | tf_op jit(solution)/shard_map/ppermute | solution.py:599
  9.3 22.2 %collective-permute-start.3 = (bf16[128,768]{1,0:T(8,128)(2,1)S(1)}, bf16[128,768]{1,0:T(8,128)(2,1)S(1)}, u32[]{:S(2)}, u32[]{:S(2)}) collective-permute-start(bf16[128,768]{1,0:T(8,128)(2,1)S(1)} %get-tuple-element.139), channel_id=1, source_target_pairs={{0,8},{4,12},{8,0},{12,4},{16,24},{20,28},{24,16},{28,20},{1,9},{5... | collective-permute-start | bytes 589832 | tf_op jit(solution)/shard_map/ppermute | solution.py:599
  11.4 20.1 %collective-permute-start.4 = (bf16[128,768]{1,0:T(8,128)(2,1)S(1)}, bf16[128,768]{1,0:T(8,128)(2,1)S(1)}, u32[]{:S(2)}, u32[]{:S(2)}) collective-permute-start(bf16[128,768]{1,0:T(8,128)(2,1)S(1)} %get-tuple-element.184.refs_0_), channel_id=1, source_target_pairs={{0,16},{4,20},{8,24},{12,28},{16,0},{20,4},{24,8},{28,12},{1,17},{... | collective-permute-start | bytes 589832 | tf_op jit(solution)/shard_map/ppermute | solution.py:599
  13.9 2.3 %copy-start = (bf16[1536,1536]{1,0:T(8,128)(2,1)S(1)}, bf16[1536,1536]{1,0:T(8,128)(2,1)}, u32[]{:S(2)}) copy-start(bf16[1536,1536]{1,0:T(8,128)(2,1)} %point_weight.5) | copy-start | bytes 14155780
  16.3 1.0 copy-start.3
  17.2 17.9 %slice-start.1 = ((s8[4718592]{0:T(1024)(128)(4,1)}), s8[4194304]{0:T(1024)(128)(4,1)S(1)}, s32[]{:S(2)}) async-start(s8[4718592]{0:T(1024)(128)(4,1)} %bitcast.14), calls=%async_computation.1 | async-start | bytes 8388608
  17.2 27.7 %slice-start.2 = ((s8[4718592]{0:T(1024)(128)(4,1)}), s8[4194304]{0:T(1024)(128)(4,1)S(1)}, s32[]{:S(2)}) async-start(s8[4718592]{0:T(1024)(128)(4,1)} %bitcast.16), calls=%async_computation.2 | async-start | bytes 8388608
  19.5 17.7 %collective-permute-start.8 = (bf16[128,768]{1,0:T(8,128)(2,1)S(1)}, bf16[128,768]{1,0:T(8,128)(2,1)S(1)}, u32[]{:S(2)}, u32[]{:S(2)}) collective-permute-start(bf16[128,768]{1,0:T(8,128)(2,1)S(1)} %get-tuple-element.139), channel_id=1, source_target_pairs={{0,24},{4,28},{8,16},{12,20},{16,8},{20,12},{24,0},{28,4},{1,25},{... | collective-permute-start | bytes 589832 | tf_op jit(solution)/shard_map/ppermute | solution.py:599
  27.3 7.7 %copy-start.5 = (f32[1536]{0:T(1024)S(1)}, f32[1536]{0:T(1024)}, u32[]{:S(2)}) copy-start(f32[1536]{0:T(1024)} %param.18) | copy-start | bytes 18436
  27.3 7.7 %copy-start.6 = (f32[1536]{0:T(1024)S(1)}, f32[1536]{0:T(1024)}, u32[]{:S(2)}) copy-start(f32[1536]{0:T(1024)} %param.20) | copy-start | bytes 18436
  27.3 7.7 %copy-start.7 = (f32[1536]{0:T(1024)S(1)}, f32[1536]{0:T(1024)}, u32[]{:S(2)}) copy-start(f32[1536]{0:T(1024)} %param.21) | copy-start | bytes 18436
  27.3 17.7 %slice-start.3 = ((s8[4718592]{0:T(1024)(128)(4,1)}), s8[524288]{0:T(1024)(128)(4,1)S(1)}, s32[]{:S(2)}) async-start(s8[4718592]{0:T(1024)(128)(4,1)} %bitcast.16), calls=%async_computation.3 | async-start | bytes 1048576
  31.5 6.5 %collective-permute-start.5 = (bf16[192,384]{1,0:T(8,128)(2,1)S(1)}, bf16[192,384]{1,0:T(8,128)(2,1)S(1)}, u32[]{:S(2)}, u32[]{:S(2)}) collective-permute-start(bf16[192,384]{1,0:T(8,128)(2,1)S(1)} %get-tuple-element.142), channel_id=1, source_target_pairs={{0,1},{1,0},{2,3},{3,2},{4,5},{5,4},{6,7},{7,6},{8,9},{9,8},{10,11... | collective-permute-start | bytes 442376 | tf_op jit(solution)/shard_map/ppermute | solution.py:599
  33.0 7.7 %collective-permute-start.6 = (bf16[192,384]{1,0:T(8,128)(2,1)S(1)}, bf16[192,384]{1,0:T(8,128)(2,1)S(1)}, u32[]{:S(2)}, u32[]{:S(2)}) collective-permute-start(bf16[192,384]{1,0:T(8,128)(2,1)S(1)} %get-tuple-element.143), channel_id=1, source_target_pairs={{0,2},{1,3},{2,0},{3,1},{4,6},{5,7},{6,4},{7,5},{8,10},{9,11},{10,... | collective-permute-start | bytes 442376 | tf_op jit(solution)/shard_map/ppermute | solution.py:599
  33.5 7.2 %collective-permute-start.7 = (bf16[192,384]{1,0:T(8,128)(2,1)S(1)}, bf16[192,384]{1,0:T(8,128)(2,1)S(1)}, u32[]{:S(2)}, u32[]{:S(2)}) collective-permute-start(bf16[192,384]{1,0:T(8,128)(2,1)S(1)} %get-tuple-element.144), channel_id=1, source_target_pairs={{0,3},{1,2},{2,1},{3,0},{4,7},{5,6},{6,5},{7,4},{8,11},{9,10},{10,... | collective-permute-start | bytes 442376 | tf_op jit(solution)/shard_map/ppermute | solution.py:599
  35.1 9.8 %copy-start.4 = (f32[31,1536]{1,0:T(8,128)S(1)}, f32[31,1536]{1,0:T(8,128)}, u32[]{:S(2)}) copy-start(f32[31,1536]{1,0:T(8,128)} %param.19) | copy-start | bytes 571396
  37.1 7.9 %copy-start.1 = (bf16[1,128,1536]{2,1,0:T(8,128)(2,1)S(1)}, bf16[1,128,1536]{2,1,0:T(8,128)(2,1)}, u32[]{:S(2)}) copy-start(bf16[1,128,1536]{2,1,0:T(8,128)(2,1)} %param.12) | copy-start | bytes 1179652
  41.4 17.6 %collective-permute-start.9 = (bf16[128,1152]{1,0:T(8,128)(2,1)S(1)}, bf16[128,1152]{1,0:T(8,128)(2,1)S(1)}, u32[]{:S(2)}, u32[]{:S(2)}) collective-permute-start(bf16[128,1152]{1,0:T(8,128)(2,1)S(1)} %get-tuple-element.153), channel_id=1, source_target_pairs={{0,3},{1,2},{2,1},{3,0},{4,7},{5,6},{6,5},{7,4},{8,11},{9,10},{10,... | collective-permute-start | bytes 884744 | tf_op jit(solution)/shard_map/ppermute | solution.py:599
  42.5 12.9 %collective-permute-start.11 = (bf16[128,1152]{1,0:T(8,128)(2,1)S(1)}, bf16[128,1152]{1,0:T(8,128)(2,1)S(1)}, u32[]{:S(2)}, u32[]{:S(2)}) collective-permute-start(bf16[128,1152]{1,0:T(8,128)(2,1)S(1)} %get-tuple-element.155), channel_id=1, source_target_pairs={{0,1},{1,0},{2,3},{3,2},{4,5},{5,4},{6,7},{7,6},{8,9},{9,8},{10,11... | collective-permute-start | bytes 884744 | tf_op jit(solution)/shard_map/ppermute | solution.py:599
  43.9 11.5 %collective-permute-start.12 = (bf16[128,1152]{1,0:T(8,128)(2,1)S(1)}, bf16[128,1152]{1,0:T(8,128)(2,1)S(1)}, u32[]{:S(2)}, u32[]{:S(2)}) collective-permute-start(bf16[128,1152]{1,0:T(8,128)(2,1)S(1)} %get-tuple-element.156), channel_id=1, source_target_pairs={{0,2},{1,3},{2,0},{3,1},{4,6},{5,7},{6,4},{7,5},{8,10},{9,11},{10,... | collective-permute-start | bytes 884744 | tf_op jit(solution)/shard_map/ppermute | solution.py:599
  55.4 16.8 %collective-permute-start.15 = (bf16[128,768]{1,0:T(8,128)(2,1)S(1)}, bf16[128,768]{1,0:T(8,128)(2,1)S(1)}, u32[]{:S(2)}, u32[]{:S(2)}) collective-permute-start(bf16[128,768]{1,0:T(8,128)(2,1)S(1)} %get-tuple-element.175), channel_id=1, source_target_pairs={{0,24},{4,28},{8,16},{12,20},{16,8},{20,12},{24,0},{28,4},{1,25},{... | collective-permute-start | bytes 589832 | tf_op jit(solution)/shard_map/ppermute | solution.py:599
  59.0 15.9 %collective-permute-start.14 = (bf16[128,768]{1,0:T(8,128)(2,1)S(1)}, bf16[128,768]{1,0:T(8,128)(2,1)S(1)}, u32[]{:S(2)}, u32[]{:S(2)}) collective-permute-start(bf16[128,768]{1,0:T(8,128)(2,1)S(1)} %get-tuple-element.175), channel_id=1, source_target_pairs={{0,16},{4,20},{8,24},{12,28},{16,0},{20,4},{24,8},{28,12},{1,17},{... | collective-permute-start | bytes 589832 | tf_op jit(solution)/shard_map/ppermute | solution.py:599
  59.0 11.9 %collective-permute-start.13 = (bf16[128,768]{1,0:T(8,128)(2,1)S(1)}, bf16[128,768]{1,0:T(8,128)(2,1)S(1)}, u32[]{:S(2)}, u32[]{:S(2)}) collective-permute-start(bf16[128,768]{1,0:T(8,128)(2,1)S(1)} %get-tuple-element.188.refs_4_), channel_id=1, source_target_pairs={{0,8},{4,12},{8,0},{12,4},{16,24},{20,28},{24,16},{28,20},{1,9},{5... | collective-permute-start | bytes 589832 | tf_op jit(solution)/shard_map/ppermute | solution.py:599
  67.9 9.2 %collective-permute-start.10 = (bf16[304,384]{1,0:T(8,128)(2,1)S(1)}, bf16[304,384]{1,0:T(8,128)(2,1)S(1)}, u32[]{:S(2)}, u32[]{:S(2)}) collective-permute-start(bf16[304,384]{1,0:T(8,128)(2,1)S(1)} %get-tuple-element.169), channel_id=1, source_target_pairs={{0,1},{1,0},{2,3},{3,2},{4,5},{5,4},{6,7},{7,6},{8,9},{9,8},{10,11... | collective-permute-start | bytes 700424 | tf_op jit(solution)/shard_map/ppermute | solution.py:599
  68.1 10.8 %collective-permute-start.16 = (bf16[304,384]{1,0:T(8,128)(2,1)S(1)}, bf16[304,384]{1,0:T(8,128)(2,1)S(1)}, u32[]{:S(2)}, u32[]{:S(2)}) collective-permute-start(bf16[304,384]{1,0:T(8,128)(2,1)S(1)} %get-tuple-element.182), channel_id=1, source_target_pairs={{0,2},{1,3},{2,0},{3,1},{4,6},{5,7},{6,4},{7,5},{8,10},{9,11},{10,... | collective-permute-start | bytes 700424 | tf_op jit(solution)/shard_map/ppermute | solution.py:599
  71.0 9.3 %collective-permute-start.17 = (bf16[304,384]{1,0:T(8,128)(2,1)S(1)}, bf16[304,384]{1,0:T(8,128)(2,1)S(1)}, u32[]{:S(2)}, u32[]{:S(2)}) collective-permute-start(bf16[304,384]{1,0:T(8,128)(2,1)S(1)} %get-tuple-element.183), channel_id=1, source_target_pairs={{0,3},{1,2},{2,1},{3,0},{4,7},{5,6},{6,5},{7,4},{8,11},{9,10},{10,... | collective-permute-start | bytes 700424 | tf_op jit(solution)/shard_map/ppermute | solution.py:599
  81.9 7.2 %collective-permute-start.25 = (bf16[4,48,1664]{2,1,0:T(8,128)(2,1)S(1)}, bf16[4,48,1664]{2,1,0:T(8,128)(2,1)S(1)}, u32[]{:S(2)}, u32[]{:S(2)}) collective-permute-start(bf16[4,48,1664]{2,1,0:T(8,128)(2,1)S(1)} %get-tuple-element.224), channel_id=1, source_target_pairs={{0,4},{4,0},{8,12},{12,8},{16,20},{20,16},{24,28},{28,24},{1,5},{5... | collective-permute-start | bytes 1916936 | tf_op jit(solution)/shard_map/ppermute | solution.py:599
  82.0 2.9 %collective-permute-start.18 = (bf16[4,96,768]{2,1,0:T(8,128)(2,1)S(1)}, bf16[4,96,768]{2,1,0:T(8,128)(2,1)S(1)}, u32[]{:S(2)}, u32[]{:S(2)}) collective-permute-start(bf16[4,96,768]{2,1,0:T(8,128)(2,1)S(1)} %get-tuple-element.197), channel_id=1, source_target_pairs={{0,4},{4,0},{8,12},{12,8},{16,20},{20,16},{24,28},{28,24},{1,5},{5... | collective-permute-start | bytes 1769480 | tf_op jit(solution)/shard_map/ppermute | solution.py:599
  85.5 10.6 %collective-permute-start.19 = (bf16[96,768]{1,0:T(8,128)(2,1)S(1)}, bf16[96,768]{1,0:T(8,128)(2,1)S(1)}, u32[]{:S(2)}, u32[]{:S(2)}) collective-permute-start(bf16[96,768]{1,0:T(8,128)(2,1)S(1)} %get-tuple-element.199), channel_id=1, source_target_pairs={{0,1},{1,0},{2,3},{3,2},{4,5},{5,4},{6,7},{7,6},{8,9},{9,8},{10,11... | collective-permute-start | bytes 442376 | tf_op jit(solution)/shard_map/ppermute | solution.py:599
  86.4 9.8 %collective-permute-start.20 = (bf16[96,768]{1,0:T(8,128)(2,1)S(1)}, bf16[96,768]{1,0:T(8,128)(2,1)S(1)}, u32[]{:S(2)}, u32[]{:S(2)}) collective-permute-start(bf16[96,768]{1,0:T(8,128)(2,1)S(1)} %get-tuple-element.200), channel_id=1, source_target_pairs={{0,2},{1,3},{2,0},{3,1},{4,6},{5,7},{6,4},{7,5},{8,10},{9,11},{10,... | collective-permute-start | bytes 442376 | tf_op jit(solution)/shard_map/ppermute | solution.py:599
  87.9 8.2 %collective-permute-start.21 = (bf16[96,768]{1,0:T(8,128)(2,1)S(1)}, bf16[96,768]{1,0:T(8,128)(2,1)S(1)}, u32[]{:S(2)}, u32[]{:S(2)}) collective-permute-start(bf16[96,768]{1,0:T(8,128)(2,1)S(1)} %get-tuple-element.201), channel_id=1, source_target_pairs={{0,3},{1,2},{2,1},{3,0},{4,7},{5,6},{6,5},{7,4},{8,11},{9,10},{10,... | collective-permute-start | bytes 442376 | tf_op jit(solution)/shard_map/ppermute | solution.py:599
  89.8 10.0 %collective-permute-start.26 = (bf16[2,48,1664]{2,1,0:T(8,128)(2,1)S(1)}, bf16[2,48,1664]{2,1,0:T(8,128)(2,1)S(1)}, u32[]{:S(2)}, u32[]{:S(2)}) collective-permute-start(bf16[2,48,1664]{2,1,0:T(8,128)(2,1)S(1)} %get-tuple-element.226), channel_id=1, source_target_pairs={{0,8},{4,12},{8,0},{12,4},{16,24},{20,28},{24,16},{28,20},{1,9},{5... | collective-permute-start | bytes 958472 | tf_op jit(solution)/shard_map/ppermute | solution.py:599
  96.2 10.0 %collective-permute-start.22 = (bf16[3,128,384]{2,1,0:T(8,128)(2,1)S(1)}, bf16[3,128,384]{2,1,0:T(8,128)(2,1)S(1)}, u32[]{:S(2)}, u32[]{:S(2)}) collective-permute-start(bf16[3,128,384]{2,1,0:T(8,128)(2,1)S(1)} %get-tuple-element.213), channel_id=1, source_target_pairs={{0,1},{1,0},{2,3},{3,2},{4,5},{5,4},{6,7},{7,6},{8,9},{9,8},{10,11... | collective-permute-start | bytes 884744 | tf_op jit(solution)/shard_map/ppermute | solution.py:599
  96.8 13.3 %collective-permute-start.23 = (bf16[3,128,384]{2,1,0:T(8,128)(2,1)S(1)}, bf16[3,128,384]{2,1,0:T(8,128)(2,1)S(1)}, u32[]{:S(2)}, u32[]{:S(2)}) collective-permute-start(bf16[3,128,384]{2,1,0:T(8,128)(2,1)S(1)} %get-tuple-element.214), channel_id=1, source_target_pairs={{0,2},{1,3},{2,0},{3,1},{4,6},{5,7},{6,4},{7,5},{8,10},{9,11},{10,... | collective-permute-start | bytes 884744 | tf_op jit(solution)/shard_map/ppermute | solution.py:599
  98.6 12.4 %collective-permute-start.24 = (bf16[3,128,384]{2,1,0:T(8,128)(2,1)S(1)}, bf16[3,128,384]{2,1,0:T(8,128)(2,1)S(1)}, u32[]{:S(2)}, u32[]{:S(2)}) collective-permute-start(bf16[3,128,384]{2,1,0:T(8,128)(2,1)S(1)} %get-tuple-element.215), channel_id=1, source_target_pairs={{0,3},{1,2},{2,1},{3,0},{4,7},{5,6},{6,5},{7,4},{8,11},{9,10},{10,... | collective-permute-start | bytes 884744 | tf_op jit(solution)/shard_map/ppermute | solution.py:599
  100.3 12.3 %collective-permute-start.27 = (bf16[1,48,1664]{2,1,0:T(8,128)(2,1)S(1)}, bf16[1,48,1664]{2,1,0:T(8,128)(2,1)S(1)}, u32[]{:S(2)}, u32[]{:S(2)}) collective-permute-start(bf16[1,48,1664]{2,1,0:T(8,128)(2,1)S(1)} %get-tuple-element.228), channel_id=1, source_target_pairs={{0,16},{4,20},{8,24},{12,28},{16,0},{20,4},{24,8},{28,12},{1,17},{... | collective-permute-start | bytes 479240 | tf_op jit(solution)/shard_map/ppermute | solution.py:599
  103.7 8.9 %collective-permute-start.28 = (bf16[48,768]{1,0:T(8,128)(2,1)S(1)}, bf16[48,768]{1,0:T(8,128)(2,1)S(1)}, u32[]{:S(2)}, u32[]{:S(2)}) collective-permute-start(bf16[48,768]{1,0:T(8,128)(2,1)S(1)} %get-tuple-element.234), channel_id=1, source_target_pairs={{0,16},{4,20},{8,24},{12,28},{16,0},{20,4},{24,8},{28,12},{1,17},{... | collective-permute-start | bytes 221192 | tf_op jit(solution)/shard_map/ppermute | solution.py:599

commit v3 on v2

--- a/solution.py
+++ b/solution.py
@@ -225,7 +225,7 @@
         row_max = jnp.max(scores, axis=0, keepdims=True)
         weights = jnp.exp(scores - row_max)
         total = jnp.sum(weights, axis=0, keepdims=True)
-        turned[part, :] = dot(value[:, part], weights.astype(jnp.bfloat16), TN) / total
+        turned[part, :] = dot(value[:, part], weights.astype(jnp.bfloat16), TN) * (1.0 / total)
         log_total[head : head + 1, :] = row_max + jnp.log(total)
     attended[...] = turned[...].T.astype(jnp.bfloat16)
     reach = 2 * EDGE
@@ -409,7 +409,7 @@
     for index in range(EDGE // BAND):
         band(index, False)
         band((EDGE + frames) // BAND + index, False)
-    lax.fori_loop(EDGE // BAND, (EDGE + frames) // BAND, inner_band, 0, unroll=2)
+    lax.fori_loop(EDGE // BAND, (EDGE + frames) // BAND, inner_band, 0, unroll=4)
     sums[0:1, :] = jnp.sum(bias_sum[...], axis=0, keepdims=True)
     sums[1:2, :] = jnp.sum(gain_sum[...], axis=0, keepdims=True)
     half = width // 2

time: 114 us -> 115 us (level)
  no operation moved by 1% of the time
where the time goes in v3:
time: 115 us; the launch traced here: 114 us
  Pallas kernels  44 us (38%)
  starting transfers between devices  36.1 us (31%)
  waiting for transfers between devices  29.3 us (25%)
  local copies, waits for them, and re-layouts  3.36 us (3%)
  between operations  1.64 us (1%)
    pallas_call x19, Pallas kernels, run(): pl.pallas_call(kernel, name=name, in_specs=[smem if a.ndim == 1 else anyw...  44 us
    ppermute x29, starting transfers between devices, swap(): lax.ppermute(block, axis, [(i, i ^ by) for i in range(lax.axis_size(axis))])  36.1 us
    ppermute x29, waiting for transfers between devices, swap(): lax.ppermute(block, axis, [(i, i ^ by) for i in range(lax.axis_size(axis))])  29.3 us
    unnamed x24, local copies, waits for them, and re-layouts  3.34 us
  transfers between devices with their start and end apart: 29, of which 11 were waited for; matrix products, arithmetic and copies ran while one was open for 0% of the time, Pallas kernels for 33%

profile of v3, /device:TPU:0, one launch (start us, length us, event | category | flops | bytes accessed | tf_op | source)
XLA Modules:
  0.0 114.4 jit_solution(12672743390982776169)
XLA Ops:
  0.7 0.0 slice-start
  0.7 2.6 %pack.1 = (bf16[384,384]{1,0:T(8,128)(2,1)}, bf16[576,384]{1,0:T(8,128)(2,1)}, bf16[384,384]{1,0:T(8,128)(2,1)}, bf16[576,384]{1,0:T(8,128)(2,1)}) custom-call(bf16[128,1536]{1,0:T(8,128)(2,1)} %bitcast.22, bf16[128,1536]{1,0:T(8,128)(2,1)} %bitcast.23, bf16[128,1536]{1,0:T(8,128)(2,1)} %bitcast.24, bf16[128,1536]{1,0:T(8,128)(2,1)} %bitcast.18, ...), custom_call_target="tpu_custom_call" | custom-call | bytes 2359296 | tf_op jit(solution)/shard_map/pack/pallas_call | solution.py:43
  3.3 3.0 %collective-permute-start = (bf16[576,384]{1,0:T(8,128)(2,1)}, bf16[576,384]{1,0:T(8,128)(2,1)S(1)}, u32[]{:S(2)}, u32[]{:S(2)}) collective-permute-start(bf16[576,384]{1,0:T(8,128)(2,1)} %get-tuple-element.127), channel_id=1, source_target_pairs={{0,1},{1,0},{2,3},{3,2},{4,5},{5,4},{6,7},{7,6},{8,9},{9,8},{10,11... | collective-permute-start | bytes 1327112 | tf_op jit(solution)/shard_map/ppermute | solution.py:599
  6.3 1.5 %collective-permute-start.2 = (bf16[576,384]{1,0:T(8,128)(2,1)}, bf16[576,384]{1,0:T(8,128)(2,1)S(1)}, u32[]{:S(2)}, u32[]{:S(2)}) collective-permute-start(bf16[576,384]{1,0:T(8,128)(2,1)} %get-tuple-element.129), channel_id=1, source_target_pairs={{0,3},{1,2},{2,1},{3,0},{4,7},{5,6},{6,5},{7,4},{8,11},{9,10},{10,... | collective-permute-start | bytes 1327112 | tf_op jit(solution)/shard_map/ppermute | solution.py:599
  7.7 0.0 collective-permute-start.1
  8.4 0.1 pad_add_fusion.info
  8.5 0.7 mask.1
  9.3 2.1 %collective-permute-start.3 = (bf16[128,768]{1,0:T(8,128)(2,1)S(1)}, bf16[128,768]{1,0:T(8,128)(2,1)S(1)}, u32[]{:S(2)}, u32[]{:S(2)}) collective-permute-start(bf16[128,768]{1,0:T(8,128)(2,1)S(1)} %get-tuple-element.139), channel_id=1, source_target_pairs={{0,8},{4,12},{8,0},{12,4},{16,24},{20,28},{24,16},{28,20},{1,9},{5... | collective-permute-start | bytes 589832 | tf_op jit(solution)/shard_map/ppermute | solution.py:599
  11.4 2.6 %collective-permute-start.4 = (bf16[128,768]{1,0:T(8,128)(2,1)S(1)}, bf16[128,768]{1,0:T(8,128)(2,1)S(1)}, u32[]{:S(2)}, u32[]{:S(2)}) collective-permute-start(bf16[128,768]{1,0:T(8,128)(2,1)S(1)} %get-tuple-element.184.refs_0_), channel_id=1, source_target_pairs={{0,16},{4,20},{8,24},{12,28},{16,0},{20,4},{24,8},{28,12},{1,17},{... | collective-permute-start | bytes 589832 | tf_op jit(solution)/shard_map/ppermute | solution.py:599
  13.9 2.3 %copy-done = bf16[1536,1536]{1,0:T(8,128)(2,1)S(1)} copy-done((bf16[1536,1536]{1,0:T(8,128)(2,1)S(1)}, bf16[1536,1536]{1,0:T(8,128)(2,1)}, u32[]{:S(2)}) %copy-start) | copy-done | bytes 4718616
  16.3 1.0 copy-done.3
  17.2 2.2 %grad_act.1 = (f32[128,1536]{1,0:T(8,128)S(1)}, bf16[384,384]{1,0:T(8,128)(2,1)S(1)}) custom-call(s32[3]{0:T(128)S(1)} %pad_add_fusion.info, bf16[128,1536]{1,0:T(8,128)(2,1)S(1)} %get-tuple-element.124.masked, bf16[1536,1536]{1,0:T(8,128)(2,1)S(1)} %copy-done, bf16[384,384]{1,0:T(8,128)(2,1)S(1)} %copy-done.3), custom_call_target="tpu_custom_call" | custom-call | flops 603979776 | bytes 7077888 | tf_op jit(solution)/shard_map/grad_act/pallas_call | solution.py:43
  19.5 0.3 collective-permute-start.8
  19.8 7.6 %collective-permute-done.2.refs_3_ = bf16[576,384]{1,0:T(8,128)(2,1)S(1)} collective-permute-done((bf16[576,384]{1,0:T(8,128)(2,1)}, bf16[576,384]{1,0:T(8,128)(2,1)S(1)}, u32[]{:S(2)}, u32[]{:S(2)}) %collective-permute-start.2) | collective-permute-done | bytes 442400 | tf_op jit(solution)/shard_map/ppermute | solution.py:599
  27.3 4.1 %attend.1 = (bf16[192,384]{1,0:T(8,128)(2,1)S(1)}, bf16[192,384]{1,0:T(8,128)(2,1)S(1)}, bf16[192,384]{1,0:T(8,128)(2,1)S(1)}, bf16[192,384]{1,0:T(8,128)(2,1)S(...) custom-call(s32[3]{0:T(128)S(1)} %pad_add_fusion.info, ...), custom_call_target="tpu_custom_call" | custom-call | flops 1610612736 | bytes 1572864 | tf_op jit(solution)/shard_map/attend/pallas_call | solution.py:43
  31.5 1.6 %collective-permute-start.5 = (bf16[192,384]{1,0:T(8,128)(2,1)S(1)}, bf16[192,384]{1,0:T(8,128)(2,1)S(1)}, u32[]{:S(2)}, u32[]{:S(2)}) collective-permute-start(bf16[192,384]{1,0:T(8,128)(2,1)S(1)} %get-tuple-element.142), channel_id=1, source_target_pairs={{0,1},{1,0},{2,3},{3,2},{4,5},{5,4},{6,7},{7,6},{8,9},{9,8},{10,11... | collective-permute-start | bytes 442376 | tf_op jit(solution)/shard_map/ppermute | solution.py:599
  33.0 0.5 collective-permute-start.6
  33.5 1.5 %collective-permute-start.7 = (bf16[192,384]{1,0:T(8,128)(2,1)S(1)}, bf16[192,384]{1,0:T(8,128)(2,1)S(1)}, u32[]{:S(2)}, u32[]{:S(2)}) collective-permute-start(bf16[192,384]{1,0:T(8,128)(2,1)S(1)} %get-tuple-element.144), channel_id=1, source_target_pairs={{0,3},{1,2},{2,1},{3,0},{4,7},{5,6},{6,5},{7,4},{8,11},{9,10},{10,... | collective-permute-start | bytes 442376 | tf_op jit(solution)/shard_map/ppermute | solution.py:599
  35.1 0.0 copy-start.4
  35.1 2.0 %mask_edges.1.grad_edges = f32[32,1536]{1,0:T(8,128)S(1)} custom-call(s32[3]{0:T(128)S(1)} %pad_add_fusion.info, bf16[48,1536]{1,0:T(8,128)(2,1)S(1)} %get-tuple-element.145.before.refs_5_, bf16[48,1536]{1,0:T(8,128)(2,1)S(1)} %get-tuple-element.146.after.refs_6_, bf16[1536,1536]{1,0:T(8,128)(2,1)S(1)} %bitcast.15), custom_call_target="tpu_custom_call" | custom-call | flops 603979776 | bytes 4718592 | tf_op jit(solution)/shard_map/mask_edges/pallas_call | solution.py:43
  37.1 0.0 collective-permute-done.8.refs_3_
  37.2 0.8 collective-permute-done.5.refs_1_
  38.0 2.8 %collective-permute-done.6.refs_2_ = bf16[192,384]{1,0:T(8,128)(2,1)S(1)} collective-permute-done((bf16[192,384]{1,0:T(8,128)(2,1)S(1)}, bf16[192,384]{1,0:T(8,128)(2,1)S(1)}, u32[]{:S(2)}, u32[]{:S(2)}) %collective-permute-start.6) | collective-permute-done | bytes 147488 | tf_op jit(solution)/shard_map/ppermute | solution.py:599
  40.7 0.6 gather.1
  41.4 1.1 %collective-permute-start.9 = (bf16[128,1152]{1,0:T(8,128)(2,1)S(1)}, bf16[128,1152]{1,0:T(8,128)(2,1)S(1)}, u32[]{:S(2)}, u32[]{:S(2)}) collective-permute-start(bf16[128,1152]{1,0:T(8,128)(2,1)S(1)} %get-tuple-element.153), channel_id=1, source_target_pairs={{0,3},{1,2},{2,1},{3,0},{4,7},{5,6},{6,5},{7,4},{8,11},{9,10},{10,... | collective-permute-start | bytes 884744 | tf_op jit(solution)/shard_map/ppermute | solution.py:599
  42.5 1.4 %collective-permute-start.11 = (bf16[128,1152]{1,0:T(8,128)(2,1)S(1)}, bf16[128,1152]{1,0:T(8,128)(2,1)S(1)}, u32[]{:S(2)}, u32[]{:S(2)}) collective-permute-start(bf16[128,1152]{1,0:T(8,128)(2,1)S(1)} %get-tuple-element.155), channel_id=1, source_target_pairs={{0,1},{1,0},{2,3},{3,2},{4,5},{5,4},{6,7},{7,6},{8,9},{9,8},{10,11... | collective-permute-start | bytes 884744 | tf_op jit(solution)/shard_map/ppermute | solution.py:599
  43.9 1.0 collective-permute-start.12
  45.0 2.7 %project.1 = (f32[192,1536]{1,0:T(8,128)S(1)}, bf16[192,1536]{1,0:T(8,128)(2,1)S(1)}) custom-call(s32[3]{0:T(128)S(1)} %pad_add_fusion.info, bf16[192,384]{1,0:T(8,128)(2,1)S(1)} %get-tuple-element.157.refs_0_, bf16[192,384]{1,0:T(8,128)(2,1)S(1)} %collective-permute-done.5.refs_1_, bf16[192,384]{1,0:T(8,128)(2,1)S(1)} %collective-permute-done.6.refs_2_, ...), custom_call_target="tpu_custom_call" | custom-call | flops 603979776 | bytes 7077888 | tf_op jit(solution)/shard_map/project/pallas_call | solution.py:43
  47.8 4.7 %conv.1 = (bf16[160,1536]{1,0:T(8,128)(2,1)S(1)}, f32[12,160,128]{2,1,0:T(8,128)S(1)}, f32[2,1536]{1,0:T(2,128)S(1)}, bf16[128,768]{1,0:T(8,128)(2,1)S(1)}, bf16[128,768]{1,0:T(8,128)(2,1)S(1)}) custom-call(s32[3]{0:T(128)S(1)} %pad_add_fusion.info, bf16[192,1536]{1,0:T(8,128)(2,1)S(1)} %get-tuple-element.161.conv_in, ...), custom_call_target="tpu_custom_call" | custom-call | flops 786432000 | bytes 2359296 | tf_op jit(solution)/shard_map/conv/pallas_call | solution.py:43
  52.4 3.0 %collective-permute-done.11.refs_5_ = bf16[128,1152]{1,0:T(8,128)(2,1)S(1)} collective-permute-done((bf16[128,1152]{1,0:T(8,128)(2,1)S(1)}, bf16[128,1152]{1,0:T(8,128)(2,1)S(1)}, u32[]{:S(2)}, u32[]{:S(2)}) %collective-permute-start.11) | collective-permute-done | bytes 294944 | tf_op jit(solution)/shard_map/ppermute | solution.py:599
  55.4 3.6 %collective-permute-start.15 = (bf16[128,768]{1,0:T(8,128)(2,1)S(1)}, bf16[128,768]{1,0:T(8,128)(2,1)S(1)}, u32[]{:S(2)}, u32[]{:S(2)}) collective-permute-start(bf16[128,768]{1,0:T(8,128)(2,1)S(1)} %get-tuple-element.175), channel_id=1, source_target_pairs={{0,24},{4,28},{8,16},{12,20},{16,8},{20,12},{24,0},{28,4},{1,25},{... | collective-permute-start | bytes 589832 | tf_op jit(solution)/shard_map/ppermute | solution.py:599
  59.0 0.8 collective-permute-start.13
  59.8 8.1 %conv_back.1 = (bf16[128,1536]{1,0:T(8,128)(2,1)}, bf16[304,384]{1,0:T(8,128)(2,1)S(1)}, bf16[304,384]{1,0:T(8,128)(2,1)S(1)}, bf16[304,384]{1,0:T(8,128)(2,1)S(1)}, bf16[304,384]{1,0:T(8,128)(2,1)S(1)}) custom-call(s32[3]{0:T(128)S(1)} %pad_add_fusion.info, f32[12,160,128]{2,1,0:T(8,128)S(1)} %get-tuple-element.165.grad_conv, ...), custom_call_target="tpu_custom_call" | custom-call | flops 1572864000 | bytes 7864320 | tf_op jit(solution)/shard_map/conv_back/pallas_call | solution.py:43
  67.9 0.2 collective-permute-start.10
  68.1 1.3 %collective-permute-start.16 = (bf16[304,384]{1,0:T(8,128)(2,1)S(1)}, bf16[304,384]{1,0:T(8,128)(2,1)S(1)}, u32[]{:S(2)}, u32[]{:S(2)}) collective-permute-start(bf16[304,384]{1,0:T(8,128)(2,1)S(1)} %get-tuple-element.182), channel_id=1, source_target_pairs={{0,2},{1,3},{2,0},{3,1},{4,6},{5,7},{6,4},{7,5},{8,10},{9,11},{10,... | collective-permute-start | bytes 700424 | tf_op jit(solution)/shard_map/ppermute | solution.py:599
  69.5 1.5 %collective-permute-done.13.refs_5_ = bf16[128,768]{1,0:T(8,128)(2,1)S(1)} collective-permute-done((bf16[128,768]{1,0:T(8,128)(2,1)S(1)}, bf16[128,768]{1,0:T(8,128)(2,1)S(1)}, u32[]{:S(2)}, u32[]{:S(2)}) %collective-permute-start.13) | collective-permute-done | bytes 196640 | tf_op jit(solution)/shard_map/ppermute | solution.py:599
  71.0 1.2 %collective-permute-start.17 = (bf16[304,384]{1,0:T(8,128)(2,1)S(1)}, bf16[304,384]{1,0:T(8,128)(2,1)S(1)}, u32[]{:S(2)}, u32[]{:S(2)}) collective-permute-start(bf16[304,384]{1,0:T(8,128)(2,1)S(1)} %get-tuple-element.183), channel_id=1, source_target_pairs={{0,3},{1,2},{2,1},{3,0},{4,7},{5,6},{6,5},{7,4},{8,11},{9,10},{10,... | collective-permute-start | bytes 700424 | tf_op jit(solution)/shard_map/ppermute | solution.py:599
  72.2 2.8 %collective-permute-done.14.refs_6_ = bf16[128,768]{1,0:T(8,128)(2,1)S(1)} collective-permute-done((bf16[128,768]{1,0:T(8,128)(2,1)S(1)}, bf16[128,768]{1,0:T(8,128)(2,1)S(1)}, u32[]{:S(2)}, u32[]{:S(2)}) %collective-permute-start.14) | collective-permute-done | bytes 196640 | tf_op jit(solution)/shard_map/ppermute | solution.py:599
  75.0 2.1 %block_out.1 = bf16[128,1536]{1,0:T(8,128)(2,1)} custom-call(s32[3]{0:T(128)S(1)} %pad_add_fusion.info, bf16[160,1536]{1,0:T(8,128)(2,1)S(1)} %get-tuple-element.193.conv_act, f32[192,1536]{1,0:T(8,128)S(1)} %get-tuple-element.166.mixed, bf16[1536,1536]{1,0:T(8,128)(2,1)S(1)} %bitcast.15), custom_call_target="tpu_custom_call" | custom-call | flops 603979776 | bytes 6291456 | tf_op jit(solution)/shard_map/block_out/pallas_call | solution.py:43
  77.1 1.7 %point_terms.1 = (bf16[4,96,768]{2,1,0:T(8,128)(2,1)S(1)}, f32[4,96,768]{2,1,0:T(8,128)S(1)}) custom-call(s32[3]{0:T(128)S(1)} %pad_add_fusion.info, bf16[128,768]{1,0:T(8,128)(2,1)S(1)} %get-tuple-element.184.refs_0_, bf16[128,768]{1,0:T(8,128)(2,1)S(1)} %collective-permute-done.3.refs_1_, bf16[128,768]{1,0:T(8,128)(2,1)S(1)} %collective-permute-done.4.refs_2_, ...), custom_call_target="tpu_custom_call" | custom-call | flops 603979776 | bytes 3145728 | tf_op jit(solution)/shard_map/point_terms/pallas_call | solution.py:43
  78.7 1.5 %collective-permute-done.17.refs_7_.refs_3_ = bf16[304,384]{1,0:T(8,128)(2,1)S(1)} collective-permute-done((bf16[304,384]{1,0:T(8,128)(2,1)S(1)}, bf16[304,384]{1,0:T(8,128)(2,1)S(1)}, u32[]{:S(2)}, u32[]{:S(2)}) %collective-permute-start.17) | collective-permute-done | bytes 233504 | tf_op jit(solution)/shard_map/ppermute | solution.py:599
  80.2 1.9 %out_terms.1 = (bf16[4,48,1664]{2,1,0:T(8,128)(2,1)S(1)}, f32[4,48,1664]{2,1,0:T(8,128)S(1)}) custom-call(s32[3]{0:T(128)S(1)} %pad_add_fusion.info, bf16[304,384]{1,0:T(8,128)(2,1)S(1)} %get-tuple-element.202.refs_4_.refs_0_, bf16[304,384]{1,0:T(8,128)(2,1)S(1)} %collective-permute-done.10.refs_5_.refs_1_, ...), custom_call_target="tpu_custom_call" | custom-call | flops 603979776 | bytes 3932160 | tf_op jit(solution)/shard_map/out_terms/pallas_call | solution.py:43
  82.1 0.1 collective-permute-start.25
  82.2 0.5 collective-permute-start.18
  82.7 2.4 %collective-permute-done.18.received = bf16[4,96,768]{2,1,0:T(8,128)(2,1)S(1)} collective-permute-done((bf16[4,96,768]{2,1,0:T(8,128)(2,1)S(1)}, bf16[4,96,768]{2,1,0:T(8,128)(2,1)S(1)}, u32[]{:S(2)}, u32[]{:S(2)}) %collective-permute-start.18) | collective-permute-done | bytes 589856 | tf_op jit(solution)/shard_map/ppermute | solution.py:599
  85.1 0.6 spread.1
  85.8 0.8 collective-permute-start.19
  86.6 1.6 %collective-permute-start.20 = (bf16[96,768]{1,0:T(8,128)(2,1)S(1)}, bf16[96,768]{1,0:T(8,128)(2,1)S(1)}, u32[]{:S(2)}, u32[]{:S(2)}) collective-permute-start(bf16[96,768]{1,0:T(8,128)(2,1)S(1)} %get-tuple-element.200), channel_id=1, source_target_pairs={{0,2},{1,3},{2,0},{3,1},{4,6},{5,7},{6,4},{7,5},{8,10},{9,11},{10,... | collective-permute-start | bytes 442376 | tf_op jit(solution)/shard_map/ppermute | solution.py:599
  88.1 1.2 %collective-permute-start.21 = (bf16[96,768]{1,0:T(8,128)(2,1)S(1)}, bf16[96,768]{1,0:T(8,128)(2,1)S(1)}, u32[]{:S(2)}, u32[]{:S(2)}) collective-permute-start(bf16[96,768]{1,0:T(8,128)(2,1)S(1)} %get-tuple-element.201), channel_id=1, source_target_pairs={{0,3},{1,2},{2,1},{3,0},{4,7},{5,6},{6,5},{7,4},{8,11},{9,10},{10,... | collective-permute-start | bytes 442376 | tf_op jit(solution)/shard_map/ppermute | solution.py:599
  89.3 0.7 halve.2
  90.0 1.5 %collective-permute-start.26 = (bf16[2,48,1664]{2,1,0:T(8,128)(2,1)S(1)}, bf16[2,48,1664]{2,1,0:T(8,128)(2,1)S(1)}, u32[]{:S(2)}, u32[]{:S(2)}) collective-permute-start(bf16[2,48,1664]{2,1,0:T(8,128)(2,1)S(1)} %get-tuple-element.226), channel_id=1, source_target_pairs={{0,8},{4,12},{8,0},{12,4},{16,24},{20,28},{24,16},{28,20},{1,9},{5... | collective-permute-start | bytes 958472 | tf_op jit(solution)/shard_map/ppermute | solution.py:599
  91.5 4.8 %attend_back.1 = (bf16[3,128,384]{2,1,0:T(8,128)(2,1)S(1)}, bf16[3,128,384]{2,1,0:T(8,128)(2,1)S(1)}, bf16[3,128,384]{2,1,0:T(8,128)(2,1)S(1)}, bf16[3,128,384]{2,1,0:T(8,128)(2,1)S(1)}) custom-call(s32[3]{0:T(128)S(1)} %pad_add_fusion.info, bf16[384,384]{1,0:T(8,128)(2,1)S(1)} %get-tuple-element.131.refs_0_, ...), custom_call_target="tpu_custom_call" | custom-call | flops 4026531840 | bytes 3145728 | tf_op jit(solution)/shard_map/attend_back/pallas_call | solution.py:43
  96.4 0.6 collective-permute-start.22
  97.0 1.8 %collective-permute-start.23 = (bf16[3,128,384]{2,1,0:T(8,128)(2,1)S(1)}, bf16[3,128,384]{2,1,0:T(8,128)(2,1)S(1)}, u32[]{:S(2)}, u32[]{:S(2)}) collective-permute-start(bf16[3,128,384]{2,1,0:T(8,128)(2,1)S(1)} %get-tuple-element.214), channel_id=1, source_target_pairs={{0,2},{1,3},{2,0},{3,1},{4,6},{5,7},{6,4},{7,5},{8,10},{9,11},{10,... | collective-permute-start | bytes 884744 | tf_op jit(solution)/shard_map/ppermute | solution.py:599
  98.8 1.1 %collective-permute-start.24 = (bf16[3,128,384]{2,1,0:T(8,128)(2,1)S(1)}, bf16[3,128,384]{2,1,0:T(8,128)(2,1)S(1)}, u32[]{:S(2)}, u32[]{:S(2)}) collective-permute-start(bf16[3,128,384]{2,1,0:T(8,128)(2,1)S(1)} %get-tuple-element.215), channel_id=1, source_target_pairs={{0,3},{1,2},{2,1},{3,0},{4,7},{5,6},{6,5},{7,4},{8,11},{9,10},{10,... | collective-permute-start | bytes 884744 | tf_op jit(solution)/shard_map/ppermute | solution.py:599
  99.9 0.6 halve.3
  100.6 2.7 %collective-permute-start.27 = (bf16[1,48,1664]{2,1,0:T(8,128)(2,1)S(1)}, bf16[1,48,1664]{2,1,0:T(8,128)(2,1)S(1)}, u32[]{:S(2)}, u32[]{:S(2)}) collective-permute-start(bf16[1,48,1664]{2,1,0:T(8,128)(2,1)S(1)} %get-tuple-element.228), channel_id=1, source_target_pairs={{0,16},{4,20},{8,24},{12,28},{16,0},{20,4},{24,8},{28,12},{1,17},{... | collective-permute-start | bytes 479240 | tf_op jit(solution)/shard_map/ppermute | solution.py:599
  103.3 0.6 point_sum.1
  103.9 0.4 collective-permute-start.28
  104.3 2.1 %collective-permute-done.22.refs_1_ = bf16[3,128,384]{2,1,0:T(8,128)(2,1)S(1)} collective-permute-done((bf16[3,128,384]{2,1,0:T(8,128)(2,1)S(1)}, bf16[3,128,384]{2,1,0:T(8,128)(2,1)S(1)}, u32[]{:S(2)}, u32[]{:S(2)}) %collective-permute-start.22) | collective-permute-done | bytes 294944 | tf_op jit(solution)/shard_map/ppermute | solution.py:599
  106.4 3.9 %collective-permute-done.23.refs_2_ = bf16[3,128,384]{2,1,0:T(8,128)(2,1)S(1)} collective-permute-done((bf16[3,128,384]{2,1,0:T(8,128)(2,1)S(1)}, bf16[3,128,384]{2,1,0:T(8,128)(2,1)S(1)}, u32[]{:S(2)}, u32[]{:S(2)}) %collective-permute-start.23) | collective-permute-done | bytes 294944 | tf_op jit(solution)/shard_map/ppermute | solution.py:599
  110.3 0.9 collective-permute-done.24.refs_3_
  111.2 1.6 %unpack.1 = (bf16[128,1536]{1,0:T(8,128)(2,1)}, bf16[128,1536]{1,0:T(8,128)(2,1)}, bf16[128,1536]{1,0:T(8,128)(2,1)}) custom-call(s32[3]{0:T(128)S(1)} %pad_add_fusion.info, bf16[3,128,384]{2,1,0:T(8,128)(2,1)S(1)} %get-tuple-element.212.refs_0_, bf16[3,128,384]{2,1,0:T(8,128)(2,1)S(1)} %collective-permute-done.22.refs_1_, ...), custom_call_target="tpu_custom_call" | custom-call | bytes 2359296 | tf_op jit(solution)/shard_map/unpack/pallas_call | solution.py:43
  112.8 1.6 %finish.1 = (f32[48,1536]{1,0:T(8,128)}, f32[31,48]{1,0:T(8,128)}, f32[3,48]{1,0:T(4,128)}, f32[48,1536]{1,0:T(8,128)}) custom-call(s32[3]{0:T(128)S(1)} %pad_add_fusion.info, f32[1,48,1664]{2,1,0:T(8,128)S(1)} %get-tuple-element.227.kept, bf16[1,48,1664]{2,1,0:T(8,128)(2,1)S(1)} %collective-permute-done.27.received, f32[48,768]{1,0:T(8,128)S(1)} %get-tuple-element.233.own, ...), custom_call_target="tpu_custom_call" | custom-call | bytes 1277952 | tf_op jit(solution)/shard_map/finish/pallas_call | solution.py:43
  (44 shorter events, 0.1 us)
Async XLA Ops:
  0.6 7.9 %copy-start.2 = (bf16[1,128,1536]{2,1,0:T(8,128)(2,1)S(1)}, bf16[1,128,1536]{2,1,0:T(8,128)(2,1)}, u32[]{:S(2)}) copy-start(bf16[1,128,1536]{2,1,0:T(8,128)(2,1)} %param.23) | copy-start | bytes 1179652
  0.7 34.4 %slice-start = ((s8[4718592]{0:T(1024)(128)(4,1)}), s8[524288]{0:T(1024)(128)(4,1)S(1)}, s32[]{:S(2)}) async-start(s8[4718592]{0:T(1024)(128)(4,1)} %bitcast.14), calls=%async_computation | async-start | bytes 1048576
  3.3 16.5 %collective-permute-start = (bf16[576,384]{1,0:T(8,128)(2,1)}, bf16[576,384]{1,0:T(8,128)(2,1)S(1)}, u32[]{:S(2)}, u32[]{:S(2)}) collective-permute-start(bf16[576,384]{1,0:T(8,128)(2,1)} %get-tuple-element.127), channel_id=1, source_target_pairs={{0,1},{1,0},{2,3},{3,2},{4,5},{5,4},{6,7},{7,6},{8,9},{9,8},{10,11... | collective-permute-start | bytes 1327112 | tf_op jit(solution)/shard_map/ppermute | solution.py:599
  6.3 21.1 %collective-permute-start.2 = (bf16[576,384]{1,0:T(8,128)(2,1)}, bf16[576,384]{1,0:T(8,128)(2,1)S(1)}, u32[]{:S(2)}, u32[]{:S(2)}) collective-permute-start(bf16[576,384]{1,0:T(8,128)(2,1)} %get-tuple-element.129), channel_id=1, source_target_pairs={{0,3},{1,2},{2,1},{3,0},{4,7},{5,6},{6,5},{7,4},{8,11},{9,10},{10,... | collective-permute-start | bytes 1327112 | tf_op jit(solution)/shard_map/ppermute | solution.py:599
  7.7 11.7 %collective-permute-start.1 = (bf16[384,384]{1,0:T(8,128)(2,1)}, bf16[384,384]{1,0:T(8,128)(2,1)S(1)}, u32[]{:S(2)}, u32[]{:S(2)}) collective-permute-start(bf16[384,384]{1,0:T(8,128)(2,1)} %get-tuple-element.128), channel_id=1, source_target_pairs={{0,2},{1,3},{2,0},{3,1},{4,6},{5,7},{6,4},{7,5},{8,10},{9,11},{10,... | collective-permute-start | bytes 884744 | tf_op jit(solution)/shard_map/ppermute | solution.py:599
  9.3 22.2 %collective-permute-start.3 = (bf16[128,768]{1,0:T(8,128)(2,1)S(1)}, bf16[128,768]{1,0:T(8,128)(2,1)S(1)}, u32[]{:S(2)}, u32[]{:S(2)}) collective-permute-start(bf16[128,768]{1,0:T(8,128)(2,1)S(1)} %get-tuple-element.139), channel_id=1, source_target_pairs={{0,8},{4,12},{8,0},{12,4},{16,24},{20,28},{24,16},{28,20},{1,9},{5... | collective-permute-start | bytes 589832 | tf_op jit(solution)/shard_map/ppermute | solution.py:599
  11.4 20.1 %collective-permute-start.4 = (bf16[128,768]{1,0:T(8,128)(2,1)S(1)}, bf16[128,768]{1,0:T(8,128)(2,1)S(1)}, u32[]{:S(2)}, u32[]{:S(2)}) collective-permute-start(bf16[128,768]{1,0:T(8,128)(2,1)S(1)} %get-tuple-element.184.refs_0_), channel_id=1, source_target_pairs={{0,16},{4,20},{8,24},{12,28},{16,0},{20,4},{24,8},{28,12},{1,17},{... | collective-permute-start | bytes 589832 | tf_op jit(solution)/shard_map/ppermute | solution.py:599
  13.9 2.3 %copy-start = (bf16[1536,1536]{1,0:T(8,128)(2,1)S(1)}, bf16[1536,1536]{1,0:T(8,128)(2,1)}, u32[]{:S(2)}) copy-start(bf16[1536,1536]{1,0:T(8,128)(2,1)} %point_weight.5) | copy-start | bytes 14155780
  16.3 1.0 copy-start.3
  17.2 17.9 %slice-start.1 = ((s8[4718592]{0:T(1024)(128)(4,1)}), s8[4194304]{0:T(1024)(128)(4,1)S(1)}, s32[]{:S(2)}) async-start(s8[4718592]{0:T(1024)(128)(4,1)} %bitcast.14), calls=%async_computation.1 | async-start | bytes 8388608
  17.2 27.7 %slice-start.2 = ((s8[4718592]{0:T(1024)(128)(4,1)}), s8[4194304]{0:T(1024)(128)(4,1)S(1)}, s32[]{:S(2)}) async-start(s8[4718592]{0:T(1024)(128)(4,1)} %bitcast.16), calls=%async_computation.2 | async-start | bytes 8388608
  19.5 17.7 %collective-permute-start.8 = (bf16[128,768]{1,0:T(8,128)(2,1)S(1)}, bf16[128,768]{1,0:T(8,128)(2,1)S(1)}, u32[]{:S(2)}, u32[]{:S(2)}) collective-permute-start(bf16[128,768]{1,0:T(8,128)(2,1)S(1)} %get-tuple-element.139), channel_id=1, source_target_pairs={{0,24},{4,28},{8,16},{12,20},{16,8},{20,12},{24,0},{28,4},{1,25},{... | collective-permute-start | bytes 589832 | tf_op jit(solution)/shard_map/ppermute | solution.py:599
  27.3 7.7 %copy-start.5 = (f32[1536]{0:T(1024)S(1)}, f32[1536]{0:T(1024)}, u32[]{:S(2)}) copy-start(f32[1536]{0:T(1024)} %param.18) | copy-start | bytes 18436
  27.3 7.7 %copy-start.6 = (f32[1536]{0:T(1024)S(1)}, f32[1536]{0:T(1024)}, u32[]{:S(2)}) copy-start(f32[1536]{0:T(1024)} %param.20) | copy-start | bytes 18436
  27.3 7.7 %copy-start.7 = (f32[1536]{0:T(1024)S(1)}, f32[1536]{0:T(1024)}, u32[]{:S(2)}) copy-start(f32[1536]{0:T(1024)} %param.21) | copy-start | bytes 18436
  27.3 17.7 %slice-start.3 = ((s8[4718592]{0:T(1024)(128)(4,1)}), s8[524288]{0:T(1024)(128)(4,1)S(1)}, s32[]{:S(2)}) async-start(s8[4718592]{0:T(1024)(128)(4,1)} %bitcast.16), calls=%async_computation.3 | async-start | bytes 1048576
  31.5 6.5 %collective-permute-start.5 = (bf16[192,384]{1,0:T(8,128)(2,1)S(1)}, bf16[192,384]{1,0:T(8,128)(2,1)S(1)}, u32[]{:S(2)}, u32[]{:S(2)}) collective-permute-start(bf16[192,384]{1,0:T(8,128)(2,1)S(1)} %get-tuple-element.142), channel_id=1, source_target_pairs={{0,1},{1,0},{2,3},{3,2},{4,5},{5,4},{6,7},{7,6},{8,9},{9,8},{10,11... | collective-permute-start | bytes 442376 | tf_op jit(solution)/shard_map/ppermute | solution.py:599
  33.0 7.7 %collective-permute-start.6 = (bf16[192,384]{1,0:T(8,128)(2,1)S(1)}, bf16[192,384]{1,0:T(8,128)(2,1)S(1)}, u32[]{:S(2)}, u32[]{:S(2)}) collective-permute-start(bf16[192,384]{1,0:T(8,128)(2,1)S(1)} %get-tuple-element.143), channel_id=1, source_target_pairs={{0,2},{1,3},{2,0},{3,1},{4,6},{5,7},{6,4},{7,5},{8,10},{9,11},{10,... | collective-permute-start | bytes 442376 | tf_op jit(solution)/shard_map/ppermute | solution.py:599
  33.5 7.2 %collective-permute-start.7 = (bf16[192,384]{1,0:T(8,128)(2,1)S(1)}, bf16[192,384]{1,0:T(8,128)(2,1)S(1)}, u32[]{:S(2)}, u32[]{:S(2)}) collective-permute-start(bf16[192,384]{1,0:T(8,128)(2,1)S(1)} %get-tuple-element.144), channel_id=1, source_target_pairs={{0,3},{1,2},{2,1},{3,0},{4,7},{5,6},{6,5},{7,4},{8,11},{9,10},{10,... | collective-permute-start | bytes 442376 | tf_op jit(solution)/shard_map/ppermute | solution.py:599
  35.1 9.8 %copy-start.4 = (f32[31,1536]{1,0:T(8,128)S(1)}, f32[31,1536]{1,0:T(8,128)}, u32[]{:S(2)}) copy-start(f32[31,1536]{1,0:T(8,128)} %param.19) | copy-start | bytes 571396
  37.1 7.9 %copy-start.1 = (bf16[1,128,1536]{2,1,0:T(8,128)(2,1)S(1)}, bf16[1,128,1536]{2,1,0:T(8,128)(2,1)}, u32[]{:S(2)}) copy-start(bf16[1,128,1536]{2,1,0:T(8,128)(2,1)} %param.12) | copy-start | bytes 1179652
  41.4 17.6 %collective-permute-start.9 = (bf16[128,1152]{1,0:T(8,128)(2,1)S(1)}, bf16[128,1152]{1,0:T(8,128)(2,1)S(1)}, u32[]{:S(2)}, u32[]{:S(2)}) collective-permute-start(bf16[128,1152]{1,0:T(8,128)(2,1)S(1)} %get-tuple-element.153), channel_id=1, source_target_pairs={{0,3},{1,2},{2,1},{3,0},{4,7},{5,6},{6,5},{7,4},{8,11},{9,10},{10,... | collective-permute-start | bytes 884744 | tf_op jit(solution)/shard_map/ppermute | solution.py:599
  42.5 12.9 %collective-permute-start.11 = (bf16[128,1152]{1,0:T(8,128)(2,1)S(1)}, bf16[128,1152]{1,0:T(8,128)(2,1)S(1)}, u32[]{:S(2)}, u32[]{:S(2)}) collective-permute-start(bf16[128,1152]{1,0:T(8,128)(2,1)S(1)} %get-tuple-element.155), channel_id=1, source_target_pairs={{0,1},{1,0},{2,3},{3,2},{4,5},{5,4},{6,7},{7,6},{8,9},{9,8},{10,11... | collective-permute-start | bytes 884744 | tf_op jit(solution)/shard_map/ppermute | solution.py:599
  43.9 11.5 %collective-permute-start.12 = (bf16[128,1152]{1,0:T(8,128)(2,1)S(1)}, bf16[128,1152]{1,0:T(8,128)(2,1)S(1)}, u32[]{:S(2)}, u32[]{:S(2)}) collective-permute-start(bf16[128,1152]{1,0:T(8,128)(2,1)S(1)} %get-tuple-element.156), channel_id=1, source_target_pairs={{0,2},{1,3},{2,0},{3,1},{4,6},{5,7},{6,4},{7,5},{8,10},{9,11},{10,... | collective-permute-start | bytes 884744 | tf_op jit(solution)/shard_map/ppermute | solution.py:599
  55.4 16.8 %collective-permute-start.15 = (bf16[128,768]{1,0:T(8,128)(2,1)S(1)}, bf16[128,768]{1,0:T(8,128)(2,1)S(1)}, u32[]{:S(2)}, u32[]{:S(2)}) collective-permute-start(bf16[128,768]{1,0:T(8,128)(2,1)S(1)} %get-tuple-element.175), channel_id=1, source_target_pairs={{0,24},{4,28},{8,16},{12,20},{16,8},{20,12},{24,0},{28,4},{1,25},{... | collective-permute-start | bytes 589832 | tf_op jit(solution)/shard_map/ppermute | solution.py:599
  59.0 15.9 %collective-permute-start.14 = (bf16[128,768]{1,0:T(8,128)(2,1)S(1)}, bf16[128,768]{1,0:T(8,128)(2,1)S(1)}, u32[]{:S(2)}, u32[]{:S(2)}) collective-permute-start(bf16[128,768]{1,0:T(8,128)(2,1)S(1)} %get-tuple-element.175), channel_id=1, source_target_pairs={{0,16},{4,20},{8,24},{12,28},{16,0},{20,4},{24,8},{28,12},{1,17},{... | collective-permute-start | bytes 589832 | tf_op jit(solution)/shard_map/ppermute | solution.py:599
  59.0 11.9 %collective-permute-start.13 = (bf16[128,768]{1,0:T(8,128)(2,1)S(1)}, bf16[128,768]{1,0:T(8,128)(2,1)S(1)}, u32[]{:S(2)}, u32[]{:S(2)}) collective-permute-start(bf16[128,768]{1,0:T(8,128)(2,1)S(1)} %get-tuple-element.188.refs_4_), channel_id=1, source_target_pairs={{0,8},{4,12},{8,0},{12,4},{16,24},{20,28},{24,16},{28,20},{1,9},{5... | collective-permute-start | bytes 589832 | tf_op jit(solution)/shard_map/ppermute | solution.py:599
  67.9 9.2 %collective-permute-start.10 = (bf16[304,384]{1,0:T(8,128)(2,1)S(1)}, bf16[304,384]{1,0:T(8,128)(2,1)S(1)}, u32[]{:S(2)}, u32[]{:S(2)}) collective-permute-start(bf16[304,384]{1,0:T(8,128)(2,1)S(1)} %get-tuple-element.169), channel_id=1, source_target_pairs={{0,1},{1,0},{2,3},{3,2},{4,5},{5,4},{6,7},{7,6},{8,9},{9,8},{10,11... | collective-permute-start | bytes 700424 | tf_op jit(solution)/shard_map/ppermute | solution.py:599
  68.1 10.6 %collective-permute-start.16 = (bf16[304,384]{1,0:T(8,128)(2,1)S(1)}, bf16[304,384]{1,0:T(8,128)(2,1)S(1)}, u32[]{:S(2)}, u32[]{:S(2)}) collective-permute-start(bf16[304,384]{1,0:T(8,128)(2,1)S(1)} %get-tuple-element.182), channel_id=1, source_target_pairs={{0,2},{1,3},{2,0},{3,1},{4,6},{5,7},{6,4},{7,5},{8,10},{9,11},{10,... | collective-permute-start | bytes 700424 | tf_op jit(solution)/shard_map/ppermute | solution.py:599
  71.0 9.3 %collective-permute-start.17 = (bf16[304,384]{1,0:T(8,128)(2,1)S(1)}, bf16[304,384]{1,0:T(8,128)(2,1)S(1)}, u32[]{:S(2)}, u32[]{:S(2)}) collective-permute-start(bf16[304,384]{1,0:T(8,128)(2,1)S(1)} %get-tuple-element.183), channel_id=1, source_target_pairs={{0,3},{1,2},{2,1},{3,0},{4,7},{5,6},{6,5},{7,4},{8,11},{9,10},{10,... | collective-permute-start | bytes 700424 | tf_op jit(solution)/shard_map/ppermute | solution.py:599
  82.1 7.2 %collective-permute-start.25 = (bf16[4,48,1664]{2,1,0:T(8,128)(2,1)S(1)}, bf16[4,48,1664]{2,1,0:T(8,128)(2,1)S(1)}, u32[]{:S(2)}, u32[]{:S(2)}) collective-permute-start(bf16[4,48,1664]{2,1,0:T(8,128)(2,1)S(1)} %get-tuple-element.224), channel_id=1, source_target_pairs={{0,4},{4,0},{8,12},{12,8},{16,20},{20,16},{24,28},{28,24},{1,5},{5... | collective-permute-start | bytes 1916936 | tf_op jit(solution)/shard_map/ppermute | solution.py:599
  82.2 2.9 %collective-permute-start.18 = (bf16[4,96,768]{2,1,0:T(8,128)(2,1)S(1)}, bf16[4,96,768]{2,1,0:T(8,128)(2,1)S(1)}, u32[]{:S(2)}, u32[]{:S(2)}) collective-permute-start(bf16[4,96,768]{2,1,0:T(8,128)(2,1)S(1)} %get-tuple-element.197), channel_id=1, source_target_pairs={{0,4},{4,0},{8,12},{12,8},{16,20},{20,16},{24,28},{28,24},{1,5},{5... | collective-permute-start | bytes 1769480 | tf_op jit(solution)/shard_map/ppermute | solution.py:599
  85.8 10.6 %collective-permute-start.19 = (bf16[96,768]{1,0:T(8,128)(2,1)S(1)}, bf16[96,768]{1,0:T(8,128)(2,1)S(1)}, u32[]{:S(2)}, u32[]{:S(2)}) collective-permute-start(bf16[96,768]{1,0:T(8,128)(2,1)S(1)} %get-tuple-element.199), channel_id=1, source_target_pairs={{0,1},{1,0},{2,3},{3,2},{4,5},{5,4},{6,7},{7,6},{8,9},{9,8},{10,11... | collective-permute-start | bytes 442376 | tf_op jit(solution)/shard_map/ppermute | solution.py:599
  86.6 9.8 %collective-permute-start.20 = (bf16[96,768]{1,0:T(8,128)(2,1)S(1)}, bf16[96,768]{1,0:T(8,128)(2,1)S(1)}, u32[]{:S(2)}, u32[]{:S(2)}) collective-permute-start(bf16[96,768]{1,0:T(8,128)(2,1)S(1)} %get-tuple-element.200), channel_id=1, source_target_pairs={{0,2},{1,3},{2,0},{3,1},{4,6},{5,7},{6,4},{7,5},{8,10},{9,11},{10,... | collective-permute-start | bytes 442376 | tf_op jit(solution)/shard_map/ppermute | solution.py:599
  88.1 8.2 %collective-permute-start.21 = (bf16[96,768]{1,0:T(8,128)(2,1)S(1)}, bf16[96,768]{1,0:T(8,128)(2,1)S(1)}, u32[]{:S(2)}, u32[]{:S(2)}) collective-permute-start(bf16[96,768]{1,0:T(8,128)(2,1)S(1)} %get-tuple-element.201), channel_id=1, source_target_pairs={{0,3},{1,2},{2,1},{3,0},{4,7},{5,6},{6,5},{7,4},{8,11},{9,10},{10,... | collective-permute-start | bytes 442376 | tf_op jit(solution)/shard_map/ppermute | solution.py:599
  90.0 10.0 %collective-permute-start.26 = (bf16[2,48,1664]{2,1,0:T(8,128)(2,1)S(1)}, bf16[2,48,1664]{2,1,0:T(8,128)(2,1)S(1)}, u32[]{:S(2)}, u32[]{:S(2)}) collective-permute-start(bf16[2,48,1664]{2,1,0:T(8,128)(2,1)S(1)} %get-tuple-element.226), channel_id=1, source_target_pairs={{0,8},{4,12},{8,0},{12,4},{16,24},{20,28},{24,16},{28,20},{1,9},{5... | collective-permute-start | bytes 958472 | tf_op jit(solution)/shard_map/ppermute | solution.py:599
  96.4 10.0 %collective-permute-start.22 = (bf16[3,128,384]{2,1,0:T(8,128)(2,1)S(1)}, bf16[3,128,384]{2,1,0:T(8,128)(2,1)S(1)}, u32[]{:S(2)}, u32[]{:S(2)}) collective-permute-start(bf16[3,128,384]{2,1,0:T(8,128)(2,1)S(1)} %get-tuple-element.213), channel_id=1, source_target_pairs={{0,1},{1,0},{2,3},{3,2},{4,5},{5,4},{6,7},{7,6},{8,9},{9,8},{10,11... | collective-permute-start | bytes 884744 | tf_op jit(solution)/shard_map/ppermute | solution.py:599
  97.0 13.3 %collective-permute-start.23 = (bf16[3,128,384]{2,1,0:T(8,128)(2,1)S(1)}, bf16[3,128,384]{2,1,0:T(8,128)(2,1)S(1)}, u32[]{:S(2)}, u32[]{:S(2)}) collective-permute-start(bf16[3,128,384]{2,1,0:T(8,128)(2,1)S(1)} %get-tuple-element.214), channel_id=1, source_target_pairs={{0,2},{1,3},{2,0},{3,1},{4,6},{5,7},{6,4},{7,5},{8,10},{9,11},{10,... | collective-permute-start | bytes 884744 | tf_op jit(solution)/shard_map/ppermute | solution.py:599
  98.8 12.4 %collective-permute-start.24 = (bf16[3,128,384]{2,1,0:T(8,128)(2,1)S(1)}, bf16[3,128,384]{2,1,0:T(8,128)(2,1)S(1)}, u32[]{:S(2)}, u32[]{:S(2)}) collective-permute-start(bf16[3,128,384]{2,1,0:T(8,128)(2,1)S(1)} %get-tuple-element.215), channel_id=1, source_target_pairs={{0,3},{1,2},{2,1},{3,0},{4,7},{5,6},{6,5},{7,4},{8,11},{9,10},{10,... | collective-permute-start | bytes 884744 | tf_op jit(solution)/shard_map/ppermute | solution.py:599
  100.6 12.3 %collective-permute-start.27 = (bf16[1,48,1664]{2,1,0:T(8,128)(2,1)S(1)}, bf16[1,48,1664]{2,1,0:T(8,128)(2,1)S(1)}, u32[]{:S(2)}, u32[]{:S(2)}) collective-permute-start(bf16[1,48,1664]{2,1,0:T(8,128)(2,1)S(1)} %get-tuple-element.228), channel_id=1, source_target_pairs={{0,16},{4,20},{8,24},{12,28},{16,0},{20,4},{24,8},{28,12},{1,17},{... | collective-permute-start | bytes 479240 | tf_op jit(solution)/shard_map/ppermute | solution.py:599
  103.9 8.9 %collective-permute-start.28 = (bf16[48,768]{1,0:T(8,128)(2,1)S(1)}, bf16[48,768]{1,0:T(8,128)(2,1)S(1)}, u32[]{:S(2)}, u32[]{:S(2)}) collective-permute-start(bf16[48,768]{1,0:T(8,128)(2,1)S(1)} %get-tuple-element.234), channel_id=1, source_target_pairs={{0,16},{4,20},{8,24},{12,28},{16,0},{20,4},{24,8},{28,12},{1,17},{... | collective-permute-start | bytes 221192 | tf_op jit(solution)/shard_map/ppermute | solution.py:599
